TPU v7x, 512 devices: a whole 4x4x16 slice. The times are simulated.
512 devices in a mesh: state: 32 (over z, y_hi), member: 16 (over y_lo, x, core).
Axes of the slice: x: 4, y: 4 (y_hi: 2, y_lo: 2; y = y_hi * 2 + y_lo), z: 16, core: 2. Of those that a mesh axis runs over, the one named last changes fastest.
Arguments:
- base_state: float32 [131072], P('state'), may hold values from -6 to 6
- anomalies: bfloat16 [1024, 131072], P('member', 'state'), may hold values from -6 to 6
- transform: bfloat16 [1024, 1024], P('member')
- weights: float32 [1024], P('member'), may hold values from -6 to 6
- observed: float32 [131072], P('state'), may hold values from -6 to 6
- obs_scale: float32 [131072], P('state'), may hold values from 0.1 to 1
- obs_rows: int32 [131072], P('state'), may hold values from 0 to 131071, as said below
- offsets: int32 [8], replicated, may hold values from -512 to 512, as said below
Outputs:
- hessian: float32 [1024, 1024], P('member', 'state')
- gradient: float32 [1024], P('member')
Inputs may be any that keep to these rules, and one draw needn't show every extreme that they name: `obs_rows`: observation o with p * 4096 <= o < (p + 1) * 4096 lies in state rows p * 4096 to (p + 1) * 4096 - 1; observation 0 is at row 0 and observation 131072 - 1 at row 131071. offsets -512 and 512 both occur.
All inputs are finite; a program needn't handle non-finite values.
Results may differ from a plain program's by a relative error of at most 0.0042.
Values may be sent and summed in bfloat16 or wider, within the bound.
No kernel may reach another device: no remote copies, remote signals or barrier semaphores. Data moves between devices by JAX's collectives and lax.ppermute only.
A program may use at most 64 MiB of HBM per device.

v0:
```python
import math

import jax
import jax.numpy as jnp
from jax import lax
from jax.sharding import PartitionSpec as P

K = 8
REACH = 512


def extended_2(block, sides, width):
    for axis, dim in sides:
        count = lax.axis_size(axis)
        forward = [(i, i + 1) for i in range(count - 1)]
        backward = [(target, source) for source, target in forward]
        low = lax.ppermute(
            lax.slice_in_dim(block, block.shape[dim] - width, None, axis=dim), axis, forward
        )
        high = lax.ppermute(lax.slice_in_dim(block, 0, width, axis=dim), axis, backward)
        block = jnp.concatenate([low, block, high], axis=dim)
    return block


def on_device(base_state, anomalies, transform, weights, observed, obs_scale, obs_rows, offsets):
    members = transform.shape[1]
    member_share = transform.shape[0]
    state_rows = anomalies.shape[1]
    transformed = jnp.dot(
        transform,
        lax.all_gather(anomalies, "member", axis=0, tiled=True),
        preferred_element_type=jnp.float32,
    )
    ensemble = (transformed + base_state[None, :]).astype(jnp.bfloat16)
    extended = extended_2(ensemble, (("state", 1),), REACH)
    local_rows = obs_rows - lax.axis_index("state") * state_rows + REACH
    stencil_mean = jnp.zeros((member_share, obs_rows.shape[0]), jnp.float32)
    for tap_index in range(K):
        stencil_mean = stencil_mean + jnp.take(
            extended, local_rows + offsets[tap_index], axis=1
        ).astype(jnp.float32)
    stencil_mean = stencil_mean / K
    predicted = stencil_mean + 0.25 * stencil_mean * stencil_mean
    obs_average = lax.psum(jnp.sum(predicted, axis=0), "member") / members
    scaled = (obs_scale * (predicted - obs_average) / math.sqrt(members - 1)).astype(jnp.bfloat16)
    innovation = obs_scale * (observed - obs_average)
    gram_block = lax.dot_general(
        scaled,
        lax.all_gather(scaled, "member", axis=0, tiled=True),
        (((1,), (1,)), ((), ())),
        preferred_element_type=jnp.float32,
    )
    gram_rows = lax.psum_scatter(gram_block, "state", scatter_dimension=1, tiled=True)
    column_count = gram_rows.shape[1]
    row_global = lax.axis_index("member") * member_share + jnp.arange(member_share, dtype=jnp.int32)
    col_global = lax.axis_index("state") * column_count + jnp.arange(column_count, dtype=jnp.int32)
    identity_part = (row_global[:, None] == col_global[None, :]).astype(jnp.float32)
    hessian = gram_rows + identity_part
    gradient_part = jnp.dot(scaled.astype(jnp.float32), innovation, precision=lax.Precision.HIGHEST)
    gradient = weights - lax.psum(gradient_part, "state")
    return (hessian, gradient)


def solution(mesh):
    placed = (
        P("state"),
        P("member", "state"),
        P("member", None),
        P("member"),
        P("state"),
        P("state"),
        P("state"),
        P(),
    )
    return jax.shard_map(
        on_device,
        mesh=mesh,
        in_specs=placed,
        out_specs=(P("member", "state"), P("member")),
        check_vma=False,
    )
```

profile of v0, /device:TPU:2, one launch (start us, length us, event | category | flops | bytes accessed | tf_op | source)
XLA Modules:
  0.0 992.9 jit_solution(18113990096773668429)
XLA Ops:
  7.2 0.0 copy-start
  7.2 0.0 all-gather.3.cloned.1.call-start
  7.2 0.7 all-gather.3.cloned.1.call-update
  7.9 0.0 all-gather.5.cloned.1.call-start
  8.0 1.6 fusion.11
  9.6 5.7 fusion.1
  15.3 0.0 copy-start.2
  15.3 59.0 %all-gather.3.cloned.1.call-done = bf16[1024,4096]{1,0:T(8,128)(2,1)} async-done(((bf16[64,4096]{1,0:T(8,128)(2,1)}), bf16[1024,4096]{1,0:T(8,128)(2,1)}) %all-gather.3.cloned.1.call-update) | async-done | bytes 8388624 | tf_op jit(solution)/shard_map/all_gather | solution.py:31
  74.3 0.0 copy-done
  74.3 5.0 fusion
  79.3 4.9 collective-permute-start
  84.2 1.3 collective-permute-start.1
  85.5 0.0 copy-done.2
  85.5 5.0 compare_and_fusion.7
  90.6 0.0 collective-permute-done
  90.6 1.3 collective-permute-done.1
  91.9 0.7 copy.18
  92.7 15.0 %gather_fusion.7 = bf16[4096,64]{1,0:T(8,128)(2,1)} fusion(bf16[64,5120]{0,1:T(8,128)(2,1)S(1)} %copy.18, s32[4096]{0:T(1024)S(1)} %get-tuple-element.24), kind=kCustom, calls=%fused_computation.7.clone | custom fusion | bytes 1064960 | tf_op jit(solution)/shard_map/jit(_take)/gather | solution.py:39
  107.7 15.0 %gather_fusion.6 = bf16[4096,64]{1,0:T(8,128)(2,1)} fusion(bf16[64,5120]{0,1:T(8,128)(2,1)S(1)} %copy.18, s32[4096]{0:T(1024)S(1)} %get-tuple-element.23), kind=kCustom, calls=%fused_computation.6.clone | custom fusion | bytes 1064960 | tf_op jit(solution)/shard_map/jit(_take)/gather | solution.py:39
  122.7 15.0 %gather_fusion.5 = bf16[4096,64]{1,0:T(8,128)(2,1)} fusion(bf16[64,5120]{0,1:T(8,128)(2,1)S(1)} %copy.18, s32[4096]{0:T(1024)S(1)} %get-tuple-element.22), kind=kCustom, calls=%fused_computation.5.clone | custom fusion | bytes 1064960 | tf_op jit(solution)/shard_map/jit(_take)/gather | solution.py:39
  137.7 15.0 %gather_fusion.4 = bf16[4096,64]{1,0:T(8,128)(2,1)} fusion(bf16[64,5120]{0,1:T(8,128)(2,1)S(1)} %copy.18, s32[4096]{0:T(1024)S(1)} %get-tuple-element.21), kind=kCustom, calls=%fused_computation.4.clone | custom fusion | bytes 1064960 | tf_op jit(solution)/shard_map/jit(_take)/gather | solution.py:39
  152.7 15.0 %gather_fusion.3 = bf16[4096,64]{1,0:T(8,128)(2,1)} fusion(bf16[64,5120]{0,1:T(8,128)(2,1)S(1)} %copy.18, s32[4096]{0:T(1024)S(1)} %get-tuple-element.20), kind=kCustom, calls=%fused_computation.3.clone | custom fusion | bytes 1064960 | tf_op jit(solution)/shard_map/jit(_take)/gather | solution.py:39
  167.7 15.1 %gather_fusion.2 = bf16[4096,64]{1,0:T(8,128)(2,1)} fusion(bf16[64,5120]{0,1:T(8,128)(2,1)S(1)} %copy.18, s32[4096]{0:T(1024)S(1)} %get-tuple-element.19), kind=kCustom, calls=%fused_computation.2.clone | custom fusion | bytes 1064960 | tf_op jit(solution)/shard_map/jit(_take)/gather | solution.py:39
  182.8 15.0 %gather_fusion.1 = bf16[4096,64]{1,0:T(8,128)(2,1)} fusion(bf16[64,5120]{0,1:T(8,128)(2,1)S(1)} %copy.18, s32[4096]{0:T(1024)S(1)} %get-tuple-element.18), kind=kCustom, calls=%fused_computation.1.clone | custom fusion | bytes 1064960 | tf_op jit(solution)/shard_map/jit(_take)/gather | solution.py:39
  197.8 15.0 %gather_fusion = bf16[4096,64]{1,0:T(8,128)(2,1)} fusion(bf16[64,5120]{0,1:T(8,128)(2,1)S(1)} %copy.18, s32[4096]{0:T(1024)S(1)} %get-tuple-element.17), kind=kCustom, calls=%fused_computation.clone | custom fusion | bytes 1064960 | tf_op jit(solution)/shard_map/jit(_take)/gather | solution.py:39
  212.8 0.0 copy-start.1
  212.8 0.0 copy-start.3
  212.8 8.7 fusion.9
  221.5 49.5 %psum.14 = f32[4096]{0:T(1024)S(1)} all-reduce(f32[4096]{0:T(1024)S(1)} %get-tuple-element.3), channel_id=1, replica_groups=mesh['state'=32,'member'=16] {'member'}, use_global_device_ids=true, to_apply=%region_1.3 | all-reduce | flops 4096 | bytes 32768 | tf_op jit(solution)/shard_map/psum | solution.py:44
  271.0 0.0 copy-done.1
  271.0 0.0 copy-done.3
  271.0 2.4 multiply_convert_fusion
  273.4 1.2 copy.26
  274.6 0.0 all-gather.5.cloned.1.call-update
  274.6 0.0 copy-start.4
  274.6 0.0 reduce-scatter.2.cloned.1.call-start
  274.7 64.4 %all-gather.5.cloned.1.call-done = bf16[1024,4096]{1,0:T(8,128)(2,1)} async-done(((bf16[64,4096]{1,0:T(8,128)(2,1)}), bf16[1024,4096]{1,0:T(8,128)(2,1)}) %all-gather.5.cloned.1.call-update) | async-done | bytes 8388624 | tf_op jit(solution)/shard_map/all_gather | solution.py:49
  339.0 6.5 fusion.12
  345.6 0.0 reduce-scatter.2.cloned.1.call-update
  345.6 0.5 convolution_bitcast_fusion
  346.1 78.5 %psum.15 = f32[64]{0:T(128)S(1)} all-reduce(f32[64]{0:T(128)S(1)} %convolution_bitcast_fusion), channel_id=1, replica_groups=mesh['state'=32,'member'=16] {'state'}, use_global_device_ids=true, to_apply=%region_3.5 | all-reduce | flops 64 | bytes 512 | tf_op jit(solution)/shard_map/psum | solution.py:60
  424.6 0.0 copy-done.4
  424.6 0.5 sub.25
  425.1 559.8 %reduce-scatter.2.cloned.1.call-done = f32[64,32]{0,1:T(8,128)} async-done(((f32[64,1024]{0,1:T(8,128)}), f32[64,32]{0,1:T(8,128)}) %reduce-scatter.2.cloned.1.call-update) | async-done | bytes 8208 | tf_op jit(solution)/shard_map/reduce_scatter | solution.py:53
  985.0 1.4 convert_add_fusion
  (5 shorter events, 0.1 us)
Async XLA Ops:
  7.2 67.2 %copy-start = (bf16[64,1024]{1,0:T(8,128)(2,1)S(1)}, bf16[64,1024]{1,0:T(8,128)(2,1)}, u32[]{:S(2)}) copy-start(bf16[64,1024]{1,0:T(8,128)(2,1)} %param.12) | copy-start | bytes 393220
  7.2 67.1 %all-gather.3.cloned.1.call-start = ((), (), s32[]{:S(2)}) async-start(), calls=%async_computation.1 | async-start | bytes 8912896 | tf_op jit(solution)/shard_map/all_gather | solution.py:31
  7.9 331.1 %all-gather.5.cloned.1.call-start = ((), (), s32[]{:S(2)}) async-start(), calls=%async_computation.2 | async-start | bytes 8912896 | tf_op jit(solution)/shard_map/all_gather | solution.py:49
  15.3 70.2 %copy-start.2 = (s32[4096]{0:T(1024)S(1)}, s32[4096]{0:T(1024)}, u32[]{:S(2)}) copy-start(s32[4096]{0:T(1024)} %param.16) | copy-start | bytes 49156
  79.3 11.3 %collective-permute-start = (bf16[64,512]{1,0:T(8,128)(2,1)S(1)}, bf16[64,512]{1,0:T(8,128)(2,1)S(1)}, u32[]{:S(2)}, u32[]{:S(2)}) collective-permute-start(bf16[64,512]{1,0:T(8,128)(2,1)S(1)} %get-tuple-element.5), channel_id=1, source_target_pairs={{0,16},{16,32},{32,48},{48,64},{64,80},{80,96},{96,112},{112,128},... | collective-permute-start | bytes 196616 | tf_op jit(solution)/shard_map/ppermute | solution.py:17
  84.2 7.7 collective-permute-start.1
  212.8 58.2 %copy-start.1 = (f32[4096]{0:T(1024)S(1)}, f32[4096]{0:T(1024)}, u32[]{:S(2)}) copy-start(f32[4096]{0:T(1024)} %param.15) | copy-start | bytes 49156
  212.8 58.2 %copy-start.3 = (f32[4096]{0:T(1024)S(1)}, f32[4096]{0:T(1024)}, u32[]{:S(2)}) copy-start(f32[4096]{0:T(1024)} %param.14) | copy-start | bytes 49156
  274.6 150.0 %copy-start.4 = (f32[64]{0:T(128)S(1)}, f32[64]{0:T(128)}, u32[]{:S(2)}) copy-start(f32[64]{0:T(128)} %param.13) | copy-start | bytes 772
  274.6 710.4 %reduce-scatter.2.cloned.1.call-start = ((), (), s32[]{:S(2)}) async-start(), calls=%async_computation.3 | async-start | bytes 540672 | tf_op jit(solution)/shard_map/reduce_scatter | solution.py:53
Sparse Core Ops, SparseCore 0:
  10.2 64.1 all-gather.2
  274.7 64.2 all-gather.4
  345.7 639.2 reduce-scatter.1
where the time goes:
time: 993 us
  waiting for transfers between devices  685 us (69%)
  blocking collectives  128 us (13%)
  local copies, waits for them, and re-layouts  124 us (12%)
  other arithmetic  23.7 us (2%)
  between operations  13.9 us (1%)
  matrix products  12 us (1%)
    reduce_scatter x1, waiting for transfers between devices, on_device(): lax.psum_scatter(gram_block, 'state', scatter_dimension=1, tiled=True)  560 us
    gather x8, local copies, waits for them, and re-layouts, on_device(): jnp.take(extended, local_rows + offsets[tap_index], axis=1)  120 us
    psum x1, blocking collectives, on_device(): gradient = weights - lax.psum(gradient_part, 'state')  78.5 us
    all_gather x1, waiting for transfers between devices, on_device(): lax.all_gather(scaled, 'member', axis=0, tiled=True)  64.4 us
    all_gather x1, waiting for transfers between devices, on_device(): lax.all_gather(anomalies, 'member', axis=0, tiled=True)  59 us
    psum x1, blocking collectives, on_device(): obs_average = lax.psum(jnp.sum(predicted, axis=0), 'member') / members  49.5 us
  transfers between devices with their start and end apart: 5, of which 4 were waited for; matrix products, arithmetic and copies ran while one was open for 1% of the time, Pallas kernels for 0%

commit v1 on v0

v1 whole, which is shorter than its diff:
```python
import math

import jax
import jax.numpy as jnp
from jax import lax
from jax.experimental import pallas as pl
from jax.experimental.pallas import tpu as pltpu
from jax.sharding import Mesh, PartitionSpec as P

M = 1024
S = 4096
REACH = 512
TAPS = 8
ROWS = 64
BF = jnp.bfloat16
F32 = jnp.float32
NT = (((1,), (1,)), ((), ()))
VMEM_LIMIT = 50 * 1024 * 1024


def call(kernel, out_shape, in_specs, scratch=(), flops=0, nbytes=0):
    return pl.pallas_call(
        kernel,
        out_shape=out_shape,
        in_specs=in_specs,
        out_specs=jax.tree.map(lambda _: pl.BlockSpec(memory_space=pltpu.VMEM), out_shape),
        scratch_shapes=list(scratch),
        compiler_params=pltpu.CompilerParams(vmem_limit_bytes=VMEM_LIMIT),
        cost_estimate=pl.CostEstimate(flops=flops, bytes_accessed=nbytes, transcendentals=0),
    )


def vmem():
    return pl.BlockSpec(memory_space=pltpu.VMEM)


def smem():
    return pl.BlockSpec(memory_space=pltpu.SMEM)


def three_parts(value):
    high = value.astype(BF)
    rest = value - high.astype(F32)
    middle = rest.astype(BF)
    low = (rest - middle.astype(F32)).astype(BF)
    return high, middle, low


def base_rows(base):
    high, middle, low = three_parts(base)
    zeros = jnp.zeros((13, base.shape[1]), BF)
    return jnp.concatenate([high, middle, low, zeros], axis=0)


def pack_kernel(place, anomalies, base, to_core, edge_own, edge_other):
    core = place[0]
    wide = S // 2 + REACH

    @pl.when(core == 0)
    def _():
        to_core[...] = anomalies[:, S - wide :]
        edge_own[0:ROWS] = anomalies[:, S - REACH :]
        edge_own[ROWS:] = base_rows(base[:, S - REACH :])
        edge_other[...] = anomalies[:, :REACH]

    @pl.when(core == 1)
    def _():
        to_core[...] = anomalies[:, :wide]
        edge_own[0:ROWS] = anomalies[:, :REACH]
        edge_own[ROWS:] = base_rows(base[:, :REACH])
        edge_other[...] = anomalies[:, S - REACH :]


CH = 256
PITCH = 144
NCH = 12


def stencil_kernel(
    place, offsets, anomalies, base, from_core, edge_own, edge_other, keep, send, base_mean, rows
):
    core = place[0]
    y_lo = place[1]
    wide = S // 2 + REACH

    def fill(chunk, first, second, extra):
        at = chunk * PITCH
        rows[at : at + ROWS] = first
        rows[at + ROWS : at + 2 * ROWS] = second
        rows[at + 2 * ROWS : at + PITCH] = extra

    @pl.when(core == 0)
    def _():
        for k in range(2):
            c = slice(k * CH, k * CH + CH)
            fill(k, edge_own[0:ROWS, c], edge_other[:, c], edge_own[ROWS:, c])
        for k in range(wide // CH):
            c = slice(k * CH, k * CH + CH)
            fill(k + 2, anomalies[:, c], from_core[:, c], base_rows(base[:, c]))

    @pl.when(core == 1)
    def _():
        for k in range(wide // CH):
            c = slice(k * CH, k * CH + CH)
            d = slice(S - wide + k * CH, S - wide + k * CH + CH)
            fill(k, from_core[:, c], anomalies[:, d], base_rows(base[:, d]))
        for k in range(2):
            c = slice(k * CH, k * CH + CH)
            fill(k + wide // CH, edge_other[:, c], edge_own[0:ROWS, c], edge_own[ROWS:, c])

    total = jnp.zeros((8 * PITCH, CH), F32)
    for k in range(5):
        shift = (
            lax.broadcasted_iota(jnp.int32, (CH, CH), 0)
            - lax.broadcasted_iota(jnp.int32, (CH, CH), 1)
            + (k * CH - REACH)
        )
        count = jnp.zeros((CH, CH), F32)
        for tap in range(TAPS):
            count = count + jnp.where(shift == offsets[tap], 1.0 / TAPS, 0.0)
        total = total + jnp.dot(
            rows[k * PITCH : (k + 8) * PITCH], count.astype(BF), preferred_element_type=F32
        )

    def put(target, half):
        for j in range(4):
            at = (half * 4 + j) * PITCH
            target[:, j * CH : j * CH + CH] = total[at : at + 2 * ROWS].astype(BF)

    def put_base(half):
        for j in range(4):
            at = (half * 4 + j) * PITCH + 2 * ROWS
            base_mean[:, j * CH : j * CH + CH] = (
                total[at : at + 1] + total[at + 1 : at + 2] + total[at + 2 : at + 3]
            )

    @pl.when(y_lo == 0)
    def _():
        put(keep, 0)
        put(send, 1)
        put_base(0)

    @pl.when(y_lo == 1)
    def _():
        put(keep, 1)
        put(send, 0)
        put_base(1)


def weight_kernel(place, observed, obs_scale, obs_rows, weight_row, value_row):
    first = place[2]
    scale = obs_scale[...]
    square = scale * scale
    value = square * observed[...]
    at = obs_rows[...] - first
    high = at >> 7
    low = at & 127
    inside = (at >= 0) & (at < S // 4)
    lanes = lax.broadcasted_iota(jnp.int32, (128, S), 0) == low
    lanes = jnp.where(lanes, 1.0, 0.0).astype(BF)
    blocks = (lax.broadcasted_iota(jnp.int32, (8, S), 0) == high) & inside
    parts = []
    for term in (square, value):
        for part in three_parts(term):
            parts.append(jnp.where(blocks, part.astype(F32), 0.0))
    left = jnp.concatenate(parts, axis=0).astype(BF)
    sums = lax.dot_general(left, lanes, NT, preferred_element_type=F32)
    weight = sums[0:8] + sums[8:16] + sums[16:24]
    worth = sums[24:32] + sums[32:40] + sums[40:48]
    for k in range(8):
        weight_row[:, k * 128 : k * 128 + 128] = weight[k : k + 1]
        value_row[:, k * 128 : k * 128 + 128] = worth[k : k + 1]


def two_part_rows(value, spare):
    high = value.astype(BF).astype(F32)
    low = value - high
    row = jnp.concatenate([high, low], axis=1)
    return jnp.concatenate([row, jnp.zeros((spare - 1, 128), F32)], axis=0).astype(BF)


def gram_kernel(
    place, transform, b00, b01, b10, b11, b20, b21, b30, b31, base_mean, weight_row, value_row,
    out, gathered, centred, scaled, part,
):
    y_lo = place[1]
    x = place[3]
    for step, pair in enumerate(((b00, b01), (b10, b11), (b20, b21), (b30, b31))):
        other = lax.rem(x + (0, 3, 1, 2)[step], 4)
        for side in range(2):
            y = y_lo if side == 0 else 1 - y_lo
            at = pl.multiple_of(y * 512 + other * 128, 128)
            gathered[pl.ds(at, 128)] = pair[side][...]

    mine = (pl.multiple_of(x * 128, 128), pl.multiple_of(512 + x * 128, 128))
    part[...] = jnp.zeros_like(part)
    for k in range(4):
        c = slice(k * CH, k * CH + CH)
        mean = jnp.dot(transform[...], gathered[:, c], preferred_element_type=F32)
        mean = mean + base_mean[:, c]
        predicted = mean + 0.25 * mean * mean
        average = jnp.sum(predicted, axis=0, keepdims=True) * (1.0 / M)
        difference = predicted - average
        centred[...] = difference
        weight = weight_row[:, c]
        scaled[:, c] = (difference * jnp.sqrt(weight * (1.0 / (M - 1)))).astype(BF)
        slope = (value_row[:, c] - weight * average) * (1.0 / math.sqrt(M - 1))
        for side in range(2):
            part[side * 128 : side * 128 + 128] += (
                centred[pl.ds(mine[side], 128)] * slope
            )
    rows = jnp.concatenate([scaled[pl.ds(mine[0], 128)], scaled[pl.ds(mine[1], 128)]], axis=0)
    gram = lax.dot_general(scaled[...], rows, NT, preferred_element_type=F32)
    left_half = lax.broadcasted_iota(jnp.int32, (16, 128), 1) < 64
    slopes = jnp.sum(part[...].T, axis=0, keepdims=True)
    for y in range(2):
        lanes = slice(y * 128, y * 128 + 128)
        sums = slopes[:, lanes]
        for core in range(2):
            tail = two_part_rows(sums[:, core * 64 : core * 64 + 64], 16)
            for y_hi in range(2):
                target = out.at[y_hi * 4 + y * 2 + core]
                for z in range(16):
                    at = z * 64 + y_hi * 32
                    top = gram[at : at + 16, lanes]
                    bottom = gram[at + 16 : at + 32, lanes]
                    if core == 0:
                        packed = jnp.where(left_half, top, pltpu.roll(bottom, 64, 1))
                    else:
                        packed = jnp.where(left_half, pltpu.roll(top, 64, 1), bottom)
                    target[z * 16 : z * 16 + 16] = packed.astype(BF)
                target[256:272] = tail


def middle_kernel(parts, out):
    total = jnp.sum(parts[...].astype(F32), axis=0)
    slopes = total[256:257]
    tail = jnp.concatenate([slopes, jnp.zeros((7, 128), F32)], axis=0)
    for z in range(16):
        out[z, 0:16] = total[z * 16 : z * 16 + 16]
        out[z, 16:24] = tail


def last_kernel(place, parts, weights, hessian, gradient):
    total = jnp.sum(parts[...], axis=0)
    packed = total[0:16]
    tall = jnp.concatenate([packed, jnp.zeros((112, 128), F32)], axis=0).T
    block = jnp.concatenate([tall[0:64, 0:16], tall[64:128, 0:16]], axis=1)
    row = lax.broadcasted_iota(jnp.int32, (ROWS, 32), 0) + place[4]
    column = lax.broadcasted_iota(jnp.int32, (ROWS, 32), 1) + place[5]
    hessian[...] = block + jnp.where(row == column, 1.0, 0.0)
    slopes = total[16:17, 0:64] + total[16:17, 64:128]
    gradient[...] = weights[...] - slopes


def on_device(base_state, anomalies, transform, weights, observed, obs_scale, obs_rows, offsets):
    z = lax.axis_index("z")
    y_hi = lax.axis_index("y_hi")
    y_lo = lax.axis_index("y_lo")
    x = lax.axis_index("x")
    core = lax.axis_index("core")
    state = z * 2 + y_hi
    column0 = state * S + core * (S // 2) + y_lo * (S // 4)
    place = jnp.stack(
        [core, y_lo, column0, x, (y_lo * 8 + x * 2 + core) * ROWS, state * 32]
    ).astype(jnp.int32)
    base = base_state.reshape(1, S)

    whole_transform = lax.all_gather(transform, ("y_lo", "x", "core"), axis=0, tiled=True)

    shape = lambda *s: jax.ShapeDtypeStruct(s, BF)
    wide = S // 2 + REACH
    to_core, edge_own, edge_other = call(
        pack_kernel,
        (shape(ROWS, wide), shape(ROWS + 16, REACH), shape(ROWS, REACH)),
        [smem(), vmem(), vmem()],
        nbytes=2**20,
    )(place, anomalies, base)

    swap = [(0, 1), (1, 0)]
    own_pairs = [(s * 2, s * 2 + 2) for s in range(31)] + [
        (s * 2 + 1, s * 2 - 1) for s in range(1, 32)
    ]
    other_pairs = [(s * 2 + 1, s * 2 + 2) for s in range(31)] + [
        (s * 2, s * 2 - 1) for s in range(1, 32)
    ]
    from_core = lax.ppermute(to_core, "core", swap)
    edge_own = lax.ppermute(edge_own, ("z", "y_hi", "core"), own_pairs)
    edge_other = lax.ppermute(edge_other, ("z", "y_hi", "core"), other_pairs)

    row = lambda v: v.reshape(1, S)
    f32 = lambda *s: jax.ShapeDtypeStruct(s, F32)
    weight_row, value_row = call(
        weight_kernel,
        (f32(1, S // 4), f32(1, S // 4)),
        [smem(), vmem(), vmem(), vmem()],
        flops=2 * 48 * S * 128,
        nbytes=2**20,
    )(place, row(observed), row(obs_scale), row(obs_rows))

    keep, send, base_mean = call(
        stencil_kernel,
        (shape(128, S // 4), shape(128, S // 4), f32(1, S // 4)),
        [smem(), smem()] + [vmem()] * 5,
        scratch=[pltpu.VMEM((NCH * PITCH, CH), BF)],
        flops=2 * 1152 * 1280 * 256,
        nbytes=2**21,
    )(place, offsets, anomalies, base, from_core, edge_own, edge_other)

    ring = lambda d: [(i, (i + d) % 4) for i in range(4)]
    got = lax.ppermute(send, "y_lo", swap)
    left = lax.ppermute(keep, "x", ring(1))
    right = lax.ppermute(keep, "x", ring(3))
    left_got = lax.ppermute(got, "x", ring(1))
    right_got = lax.ppermute(got, "x", ring(3))
    far = lax.ppermute(left, "x", ring(1))
    far_got = lax.ppermute(right_got, "x", ring(3))

    parts = call(
        gram_kernel,
        shape(8, 272, 128),
        [smem()] + [vmem()] * 12,
        scratch=[
            pltpu.VMEM((M, S // 4), BF),
            pltpu.VMEM((M, CH), F32),
            pltpu.VMEM((M, S // 4), BF),
            pltpu.VMEM((256, CH), F32),
        ],
        flops=2 * M * M * 1280,
        nbytes=2**22,
    )(
        place, whole_transform, keep, got, left, left_got, right, right_got, far, far_got,
        base_mean, weight_row, value_row,
    )
    parts = lax.all_to_all(parts, ("y_hi", "y_lo", "core"), 0, 0)
    sums = call(middle_kernel, f32(16, 24, 128), [vmem()], nbytes=2**19)(parts)
    sums = lax.all_to_all(sums, "z", 0, 0)
    hessian, gradient = call(
        last_kernel, (f32(ROWS, 32), f32(1, ROWS)), [smem(), vmem(), vmem()], nbytes=2**18
    )(place, sums, weights.reshape(1, ROWS))
    return hessian, gradient.reshape(ROWS)


def solution(mesh):
    fine = Mesh(mesh.devices.reshape(16, 2, 2, 4, 2), ("z", "y_hi", "y_lo", "x", "core"))
    state = ("z", "y_hi")
    member = ("y_lo", "x", "core")
    placed = (
        P(state),
        P(member, state),
        P(member, None),
        P(member),
        P(state),
        P(state),
        P(state),
        P(),
    )
    return jax.shard_map(
        on_device,
        mesh=fine,
        in_specs=placed,
        out_specs=(P(member, state), P(member)),
        check_vma=False,
    )
```

time: 993 us -> 128 us (0.13)
  the two profiles are of different devices: /device:TPU:2 before, /device:TPU:64 now
where the time goes in v1:
time: 128 us; the launch traced here: 127 us
  blocking collectives  45.4 us (35%)
  starting transfers between devices  30.7 us (24%)
  waiting for transfers between devices  21 us (16%)
  between operations  14.2 us (11%)
  Pallas kernels  12.4 us (10%)
  local copies, waits for them, and re-layouts  3.2 us (2%)
    all_to_all x1, blocking collectives, on_device(): sums = lax.all_to_all(sums, 'z', 0, 0)  31.3 us
    all_to_all x1, blocking collectives, on_device(): parts = lax.all_to_all(parts, ('y_hi', 'y_lo', 'core'), 0, 0)  14.1 us
    ppermute x1, waiting for transfers between devices, on_device(): got = lax.ppermute(send, 'y_lo', swap)  7.49 us
    pallas_call x1, Pallas kernels, on_device(): call(gram_kernel, shape(8, 272, 128), [smem()] + [vmem()] * 12, scratch=[...  7.17 us
    ppermute x1, waiting for transfers between devices, on_device(): edge_other = lax.ppermute(edge_other, ('z', 'y_hi', 'core'), other_pairs)  6.06 us
    ppermute x1, starting transfers between devices, on_device(): edge_own = lax.ppermute(edge_own, ('z', 'y_hi', 'core'), own_pairs)  5.1 us
    ppermute x1, starting transfers between devices, on_device(): right_got = lax.ppermute(got, 'x', ring(3))  4.68 us
    ppermute x1, starting transfers between devices, on_device(): left_got = lax.ppermute(got, 'x', ring(1))  3.92 us
  transfers between devices with their start and end apart: 11, of which 6 were waited for; matrix products, arithmetic and copies ran while one was open for 0% of the time, Pallas kernels for 3%

profile of v1, /device:TPU:64, one launch (start us, length us, event | category | flops | bytes accessed | tf_op | source)
XLA Modules:
  0.0 127.0 jit_solution(14661122340095040829)
XLA Ops:
  7.2 0.0 copy-start.5
  7.2 0.0 copy-start.4
  7.2 0.0 copy-start.3
  7.2 0.0 all-gather.2.cloned.1.call-start
  7.2 0.7 all-gather.2.cloned.1.call-update
  7.9 0.1 stack.27.place
  8.0 0.0 copy-start
  8.0 1.0 copy-done
  9.1 0.0 copy-start.1
  9.1 0.7 copy-done.1
  9.8 0.6 shard_map.95
  10.4 1.9 %collective-permute-start = (bf16[64,2560]{1,0:T(8,128)(2,1)S(1)}, bf16[64,2560]{1,0:T(8,128)(2,1)S(1)}, u32[]{:S(2)}, u32[]{:S(2)}) collective-permute-start(bf16[64,2560]{1,0:T(8,128)(2,1)S(1)} %get-tuple-element.12), channel_id=1, source_target_pairs={{0,1},{1,0},{2,3},{3,2},{4,5},{5,4},{6,7},{7,6},{8,9},{9,8},{10,11... | collective-permute-start | bytes 983048 | tf_op jit(solution)/shard_map/ppermute | solution.py:287
  12.3 5.1 %collective-permute-start.1 = (bf16[80,512]{1,0:T(8,128)(2,1)S(1)}, bf16[80,512]{1,0:T(8,128)(2,1)S(1)}, u32[]{:S(2)}, u32[]{:S(2)}) collective-permute-start(bf16[80,512]{1,0:T(8,128)(2,1)S(1)} %get-tuple-element.13), channel_id=1, source_target_pairs={{0,16},{16,32},{32,48},{48,64},{64,80},{80,96},{96,112},{112,128},... | collective-permute-start | bytes 245768 | tf_op jit(solution)/shard_map/ppermute | solution.py:288
  17.4 1.9 %collective-permute-start.2 = (bf16[64,512]{1,0:T(8,128)(2,1)S(1)}, bf16[64,512]{1,0:T(8,128)(2,1)S(1)}, u32[]{:S(2)}, u32[]{:S(2)}) collective-permute-start(bf16[64,512]{1,0:T(8,128)(2,1)S(1)} %get-tuple-element.14), channel_id=1, source_target_pairs={{1,16},{17,32},{33,48},{49,64},{65,80},{81,96},{97,112},{113,128},... | collective-permute-start | bytes 196616 | tf_op jit(solution)/shard_map/ppermute | solution.py:289
  19.4 6.1 %collective-permute-done.2.edge_other = bf16[64,512]{1,0:T(8,128)(2,1)S(1)} collective-permute-done((bf16[64,512]{1,0:T(8,128)(2,1)S(1)}, bf16[64,512]{1,0:T(8,128)(2,1)S(1)}, u32[]{:S(2)}, u32[]{:S(2)}) %collective-permute-start.2) | collective-permute-done | bytes 65568 | tf_op jit(solution)/shard_map/ppermute | solution.py:289
  25.4 0.0 collective-permute-done.1.edge_own
  25.4 0.0 collective-permute-done.from_core
  25.4 0.0 copy-start.6
  25.4 0.7 copy-done.6
  26.1 2.4 %shard_map.96 = (bf16[128,1024]{1,0:T(8,128)(2,1)S(1)}, bf16[128,1024]{1,0:T(8,128)(2,1)S(1)}, f32[1,1024]{1,0:T(1,128)S(1)}) custom-call(s32[6]{0:T(128)S(1)} %stack.27.place, s32[8]{0:T(128)S(1)} %copy-done.6, bf16[64,4096]{1,0:T(8,128)(2,1)S(1)} %copy-done, f32[1,4096]{1,0:T(1,128)S(1)} %bitcast.13, bf16[64,2560]{1,0:T(8,128)(2,1)S(1)} %collective-permute-done.from_core, ...), custom_call_target="tpu_custom_call" | custom-call | flops 754974720 | bytes 2097152 | tf_op jit(solution)/shard_map/pallas_call | solution.py:301
  28.4 2.6 %collective-permute-start.3 = (bf16[128,1024]{1,0:T(8,128)(2,1)S(1)}, bf16[128,1024]{1,0:T(8,128)(2,1)S(1)}, u32[]{:S(2)}, u32[]{:S(2)}) collective-permute-start(bf16[128,1024]{1,0:T(8,128)(2,1)S(1)} %get-tuple-element.16), channel_id=1, source_target_pairs={{0,8},{8,0},{1,9},{9,1},{2,10},{10,2},{3,11},{11,3},{4,12},{12,4},... | collective-permute-start | bytes 786440 | tf_op jit(solution)/shard_map/ppermute | solution.py:311
  31.0 3.4 %collective-permute-start.4 = (bf16[128,1024]{1,0:T(8,128)(2,1)S(1)}, bf16[128,1024]{1,0:T(8,128)(2,1)S(1)}, u32[]{:S(2)}, u32[]{:S(2)}) collective-permute-start(bf16[128,1024]{1,0:T(8,128)(2,1)S(1)} %get-tuple-element.15.b00), channel_id=1, source_target_pairs={{0,2},{2,4},{4,6},{6,0},{1,3},{3,5},{5,7},{7,1},{8,10},{10,12},{12... | collective-permute-start | bytes 786440 | tf_op jit(solution)/shard_map/ppermute | solution.py:312
  34.4 7.5 %collective-permute-done.3.b01 = bf16[128,1024]{1,0:T(8,128)(2,1)S(1)} collective-permute-done((bf16[128,1024]{1,0:T(8,128)(2,1)S(1)}, bf16[128,1024]{1,0:T(8,128)(2,1)S(1)}, u32[]{:S(2)}, u32[]{:S(2)}) %collective-permute-start.3) | collective-permute-done | bytes 262176 | tf_op jit(solution)/shard_map/ppermute | solution.py:311
  41.9 4.7 %collective-permute-start.7 = (bf16[128,1024]{1,0:T(8,128)(2,1)S(1)}, bf16[128,1024]{1,0:T(8,128)(2,1)S(1)}, u32[]{:S(2)}, u32[]{:S(2)}) collective-permute-start(bf16[128,1024]{1,0:T(8,128)(2,1)S(1)} %collective-permute-done.3.b01), channel_id=1, source_target_pairs={{0,6},{2,0},{4,2},{6,4},{1,7},{3,1},{5,3},{7,5},{8,14},{10,8},{12,... | collective-permute-start | bytes 786440 | tf_op jit(solution)/shard_map/ppermute | solution.py:315
  46.6 1.9 %collective-permute-start.6 = (bf16[128,1024]{1,0:T(8,128)(2,1)S(1)}, bf16[128,1024]{1,0:T(8,128)(2,1)S(1)}, u32[]{:S(2)}, u32[]{:S(2)}) collective-permute-start(bf16[128,1024]{1,0:T(8,128)(2,1)S(1)} %get-tuple-element.15.b00), channel_id=1, source_target_pairs={{0,6},{2,0},{4,2},{6,4},{1,7},{3,1},{5,3},{7,5},{8,14},{10,8},{12,... | collective-permute-start | bytes 786440 | tf_op jit(solution)/shard_map/ppermute | solution.py:313
  48.6 3.9 %collective-permute-start.5 = (bf16[128,1024]{1,0:T(8,128)(2,1)S(1)}, bf16[128,1024]{1,0:T(8,128)(2,1)S(1)}, u32[]{:S(2)}, u32[]{:S(2)}) collective-permute-start(bf16[128,1024]{1,0:T(8,128)(2,1)S(1)} %collective-permute-done.3.b01), channel_id=1, source_target_pairs={{0,2},{2,4},{4,6},{6,0},{1,3},{3,5},{5,7},{7,1},{8,10},{10,12},{12... | collective-permute-start | bytes 786440 | tf_op jit(solution)/shard_map/ppermute | solution.py:314
  52.5 0.0 collective-permute-done.4.b10
  52.5 1.9 %collective-permute-start.8 = (bf16[128,1024]{1,0:T(8,128)(2,1)S(1)}, bf16[128,1024]{1,0:T(8,128)(2,1)S(1)}, u32[]{:S(2)}, u32[]{:S(2)}) collective-permute-start(bf16[128,1024]{1,0:T(8,128)(2,1)S(1)} %collective-permute-done.4.b10), channel_id=1, source_target_pairs={{0,2},{2,4},{4,6},{6,0},{1,3},{3,5},{5,7},{7,1},{8,10},{10,12},{12... | collective-permute-start | bytes 786440 | tf_op jit(solution)/shard_map/ppermute | solution.py:316
  54.4 1.8 %collective-permute-done.7.b21 = bf16[128,1024]{1,0:T(8,128)(2,1)S(1)} collective-permute-done((bf16[128,1024]{1,0:T(8,128)(2,1)S(1)}, bf16[128,1024]{1,0:T(8,128)(2,1)S(1)}, u32[]{:S(2)}, u32[]{:S(2)}) %collective-permute-start.7) | collective-permute-done | bytes 262176 | tf_op jit(solution)/shard_map/ppermute | solution.py:315
  56.2 3.3 %collective-permute-start.9 = (bf16[128,1024]{1,0:T(8,128)(2,1)S(1)}, bf16[128,1024]{1,0:T(8,128)(2,1)S(1)}, u32[]{:S(2)}, u32[]{:S(2)}) collective-permute-start(bf16[128,1024]{1,0:T(8,128)(2,1)S(1)} %collective-permute-done.7.b21), channel_id=1, source_target_pairs={{0,6},{2,0},{4,2},{6,4},{1,7},{3,1},{5,3},{7,5},{8,14},{10,8},{12,... | collective-permute-start | bytes 786440 | tf_op jit(solution)/shard_map/ppermute | solution.py:317
  59.6 0.0 copy-done.5
  59.6 0.0 copy-done.4
  59.6 0.0 copy-done.3
  59.6 1.1 shard_map.97
  60.7 1.3 %collective-permute-done.6.b20 = bf16[128,1024]{1,0:T(8,128)(2,1)S(1)} collective-permute-done((bf16[128,1024]{1,0:T(8,128)(2,1)S(1)}, bf16[128,1024]{1,0:T(8,128)(2,1)S(1)}, u32[]{:S(2)}, u32[]{:S(2)}) %collective-permute-start.6) | collective-permute-done | bytes 262176 | tf_op jit(solution)/shard_map/ppermute | solution.py:313
  62.0 0.0 collective-permute-done.5.b11
  62.0 1.5 %collective-permute-done.8.b30 = bf16[128,1024]{1,0:T(8,128)(2,1)S(1)} collective-permute-done((bf16[128,1024]{1,0:T(8,128)(2,1)S(1)}, bf16[128,1024]{1,0:T(8,128)(2,1)S(1)}, u32[]{:S(2)}, u32[]{:S(2)}) %collective-permute-start.8) | collective-permute-done | bytes 262176 | tf_op jit(solution)/shard_map/ppermute | solution.py:316
  63.5 2.1 %collective-permute-done.9.b31 = bf16[128,1024]{1,0:T(8,128)(2,1)S(1)} collective-permute-done((bf16[128,1024]{1,0:T(8,128)(2,1)S(1)}, bf16[128,1024]{1,0:T(8,128)(2,1)S(1)}, u32[]{:S(2)}, u32[]{:S(2)}) %collective-permute-start.9) | collective-permute-done | bytes 262176 | tf_op jit(solution)/shard_map/ppermute | solution.py:317
  65.7 0.0 all-gather.2.cloned.1.call-done.transform
  65.7 7.2 %shard_map.98 = bf16[8,272,128]{2,1,0:T(8,128)(2,1)S(1)} custom-call(s32[6]{0:T(128)S(1)} %stack.27.place, bf16[1024,1024]{1,0:T(8,128)(2,1)} %all-gather.2.cloned.1.call-done.transform, bf16[128,1024]{1,0:T(8,128)(2,1)S(1)} %get-tuple-element.15.b00, bf16[128,1024]{1,0:T(8,128)(2,1)S(1)} %collective-permute-done.3.b01, ...), custom_call_target="tpu_custom_call" | custom-call | flops 2684354560 | bytes 4194304 | tf_op jit(solution)/shard_map/pallas_call | solution.py:319
  72.8 0.0 copy-start.2
  72.8 14.1 %all_to_all.10.parts = bf16[8,272,128]{2,1,0:T(8,128)(2,1)S(1)} all-to-all(bf16[8,272,128]{2,1,0:T(8,128)(2,1)S(1)} %shard_map.98), channel_id=1, replica_groups=mesh['z'=16,'y_hi'=2,'y_lo'=2,'x'=4,'core'=2] {'y_hi','y_lo','core'}, dimensions={0} | all-to-all | bytes 1114112 | tf_op jit(solution)/shard_map/all_to_all | solution.py:335
  87.0 0.1 shard_map.99
  87.1 31.3 %all_to_all.11.parts = f32[16,24,128]{2,1,0:T(8,128)S(1)} all-to-all(f32[16,24,128]{2,1,0:T(8,128)S(1)} %shard_map.99), channel_id=1, replica_groups=mesh['z'=16,'y_hi'=2,'y_lo'=2,'x'=4,'core'=2] {'z'}, dimensions={0} | all-to-all | bytes 393216 | tf_op jit(solution)/shard_map/all_to_all | solution.py:337
  118.4 0.0 copy-done.2
  118.4 1.1 shard_map.100
  119.5 0.7 copy.10
Async XLA Ops:
  7.2 52.4 %copy-start.5 = (s32[4096]{0:T(1024)S(1)}, s32[4096]{0:T(1024)}, u32[]{:S(2)}) copy-start(s32[4096]{0:T(1024)} %param.14) | copy-start | bytes 49156
  7.2 52.4 %copy-start.4 = (f32[4096]{0:T(1024)S(1)}, f32[4096]{0:T(1024)}, u32[]{:S(2)}) copy-start(f32[4096]{0:T(1024)} %param.13) | copy-start | bytes 49156
  7.2 52.4 %copy-start.3 = (f32[4096]{0:T(1024)S(1)}, f32[4096]{0:T(1024)}, u32[]{:S(2)}) copy-start(f32[4096]{0:T(1024)} %param.12) | copy-start | bytes 49156
  7.2 58.5 %all-gather.2.cloned.1.call-start = ((), (), s32[]{:S(2)}) async-start(), calls=%async_computation.2 | async-start | bytes 2228224 | tf_op jit(solution)/shard_map/all_gather | solution.py:269
  8.0 1.0 copy-start
  9.1 0.7 copy-start.1
  10.4 15.0 %collective-permute-start = (bf16[64,2560]{1,0:T(8,128)(2,1)S(1)}, bf16[64,2560]{1,0:T(8,128)(2,1)S(1)}, u32[]{:S(2)}, u32[]{:S(2)}) collective-permute-start(bf16[64,2560]{1,0:T(8,128)(2,1)S(1)} %get-tuple-element.12), channel_id=1, source_target_pairs={{0,1},{1,0},{2,3},{3,2},{4,5},{5,4},{6,7},{7,6},{8,9},{9,8},{10,11... | collective-permute-start | bytes 983048 | tf_op jit(solution)/shard_map/ppermute | solution.py:287
  12.3 13.1 %collective-permute-start.1 = (bf16[80,512]{1,0:T(8,128)(2,1)S(1)}, bf16[80,512]{1,0:T(8,128)(2,1)S(1)}, u32[]{:S(2)}, u32[]{:S(2)}) collective-permute-start(bf16[80,512]{1,0:T(8,128)(2,1)S(1)} %get-tuple-element.13), channel_id=1, source_target_pairs={{0,16},{16,32},{32,48},{48,64},{64,80},{80,96},{96,112},{112,128},... | collective-permute-start | bytes 245768 | tf_op jit(solution)/shard_map/ppermute | solution.py:288
  17.4 8.0 %collective-permute-start.2 = (bf16[64,512]{1,0:T(8,128)(2,1)S(1)}, bf16[64,512]{1,0:T(8,128)(2,1)S(1)}, u32[]{:S(2)}, u32[]{:S(2)}) collective-permute-start(bf16[64,512]{1,0:T(8,128)(2,1)S(1)} %get-tuple-element.14), channel_id=1, source_target_pairs={{1,16},{17,32},{33,48},{49,64},{65,80},{81,96},{97,112},{113,128},... | collective-permute-start | bytes 196616 | tf_op jit(solution)/shard_map/ppermute | solution.py:289
  25.4 0.7 copy-start.6
  28.4 13.5 %collective-permute-start.3 = (bf16[128,1024]{1,0:T(8,128)(2,1)S(1)}, bf16[128,1024]{1,0:T(8,128)(2,1)S(1)}, u32[]{:S(2)}, u32[]{:S(2)}) collective-permute-start(bf16[128,1024]{1,0:T(8,128)(2,1)S(1)} %get-tuple-element.16), channel_id=1, source_target_pairs={{0,8},{8,0},{1,9},{9,1},{2,10},{10,2},{3,11},{11,3},{4,12},{12,4},... | collective-permute-start | bytes 786440 | tf_op jit(solution)/shard_map/ppermute | solution.py:311
  31.0 21.4 %collective-permute-start.4 = (bf16[128,1024]{1,0:T(8,128)(2,1)S(1)}, bf16[128,1024]{1,0:T(8,128)(2,1)S(1)}, u32[]{:S(2)}, u32[]{:S(2)}) collective-permute-start(bf16[128,1024]{1,0:T(8,128)(2,1)S(1)} %get-tuple-element.15.b00), channel_id=1, source_target_pairs={{0,2},{2,4},{4,6},{6,0},{1,3},{3,5},{5,7},{7,1},{8,10},{10,12},{12... | collective-permute-start | bytes 786440 | tf_op jit(solution)/shard_map/ppermute | solution.py:312
  41.9 14.3 %collective-permute-start.7 = (bf16[128,1024]{1,0:T(8,128)(2,1)S(1)}, bf16[128,1024]{1,0:T(8,128)(2,1)S(1)}, u32[]{:S(2)}, u32[]{:S(2)}) collective-permute-start(bf16[128,1024]{1,0:T(8,128)(2,1)S(1)} %collective-permute-done.3.b01), channel_id=1, source_target_pairs={{0,6},{2,0},{4,2},{6,4},{1,7},{3,1},{5,3},{7,5},{8,14},{10,8},{12,... | collective-permute-start | bytes 786440 | tf_op jit(solution)/shard_map/ppermute | solution.py:315
  46.6 15.4 %collective-permute-start.6 = (bf16[128,1024]{1,0:T(8,128)(2,1)S(1)}, bf16[128,1024]{1,0:T(8,128)(2,1)S(1)}, u32[]{:S(2)}, u32[]{:S(2)}) collective-permute-start(bf16[128,1024]{1,0:T(8,128)(2,1)S(1)} %get-tuple-element.15.b00), channel_id=1, source_target_pairs={{0,6},{2,0},{4,2},{6,4},{1,7},{3,1},{5,3},{7,5},{8,14},{10,8},{12,... | collective-permute-start | bytes 786440 | tf_op jit(solution)/shard_map/ppermute | solution.py:313
  48.6 13.4 %collective-permute-start.5 = (bf16[128,1024]{1,0:T(8,128)(2,1)S(1)}, bf16[128,1024]{1,0:T(8,128)(2,1)S(1)}, u32[]{:S(2)}, u32[]{:S(2)}) collective-permute-start(bf16[128,1024]{1,0:T(8,128)(2,1)S(1)} %collective-permute-done.3.b01), channel_id=1, source_target_pairs={{0,2},{2,4},{4,6},{6,0},{1,3},{3,5},{5,7},{7,1},{8,10},{10,12},{12... | collective-permute-start | bytes 786440 | tf_op jit(solution)/shard_map/ppermute | solution.py:314
  52.5 11.0 %collective-permute-start.8 = (bf16[128,1024]{1,0:T(8,128)(2,1)S(1)}, bf16[128,1024]{1,0:T(8,128)(2,1)S(1)}, u32[]{:S(2)}, u32[]{:S(2)}) collective-permute-start(bf16[128,1024]{1,0:T(8,128)(2,1)S(1)} %collective-permute-done.4.b10), channel_id=1, source_target_pairs={{0,2},{2,4},{4,6},{6,0},{1,3},{3,5},{5,7},{7,1},{8,10},{10,12},{12... | collective-permute-start | bytes 786440 | tf_op jit(solution)/shard_map/ppermute | solution.py:316
  56.2 9.4 %collective-permute-start.9 = (bf16[128,1024]{1,0:T(8,128)(2,1)S(1)}, bf16[128,1024]{1,0:T(8,128)(2,1)S(1)}, u32[]{:S(2)}, u32[]{:S(2)}) collective-permute-start(bf16[128,1024]{1,0:T(8,128)(2,1)S(1)} %collective-permute-done.7.b21), channel_id=1, source_target_pairs={{0,6},{2,0},{4,2},{6,4},{1,7},{3,1},{5,3},{7,5},{8,14},{10,8},{12,... | collective-permute-start | bytes 786440 | tf_op jit(solution)/shard_map/ppermute | solution.py:317
  72.8 45.5 %copy-start.2 = (f32[64]{0:T(128)S(1)}, f32[64]{0:T(128)}, u32[]{:S(2)}) copy-start(f32[64]{0:T(128)} %param.11) | copy-start | bytes 772
Sparse Core Ops, SparseCore 0:
  10.2 48.0 all-gather.1

commit v2 on v0

v2 whole, which is shorter than its diff:
```python
import math

import jax
import jax.numpy as jnp
from jax import lax
from jax.experimental import pallas as pl
from jax.experimental.pallas import tpu as pltpu
from jax.sharding import Mesh, PartitionSpec as P

M = 1024
S = 4096
REACH = 512
TAPS = 8
ROWS = 64
GROUP = 8
COLS = S // GROUP
CH = 256
PITCH = 80
BF = jnp.bfloat16
F32 = jnp.float32
NT = (((1,), (1,)), ((), ()))
VMEM_LIMIT = 50 * 1024 * 1024


def call(kernel, out_shape, in_specs, scratch=(), flops=0, nbytes=0):
    return pl.pallas_call(
        kernel,
        out_shape=out_shape,
        in_specs=in_specs,
        out_specs=jax.tree.map(lambda _: pl.BlockSpec(memory_space=pltpu.VMEM), out_shape),
        scratch_shapes=list(scratch),
        compiler_params=pltpu.CompilerParams(vmem_limit_bytes=VMEM_LIMIT),
        cost_estimate=pl.CostEstimate(flops=flops, bytes_accessed=nbytes, transcendentals=0),
    )


def vmem():
    return pl.BlockSpec(memory_space=pltpu.VMEM)


def smem():
    return pl.BlockSpec(memory_space=pltpu.SMEM)


def shape(*dims):
    return jax.ShapeDtypeStruct(dims, BF)


def shape32(*dims):
    return jax.ShapeDtypeStruct(dims, F32)


def three_parts(value):
    high = value.astype(BF)
    rest = value - high.astype(F32)
    middle = rest.astype(BF)
    low = (rest - middle.astype(F32)).astype(BF)
    return high, middle, low


def base_rows(base):
    high, middle, low = three_parts(base)
    zeros = jnp.zeros((13, base.shape[1]), BF)
    return jnp.concatenate([high, middle, low, zeros], axis=0)


def edge_kernel(anomalies, base, low, high, base_low, base_high, sems):
    first = pl.ds(0, REACH)
    last = pl.ds(S - REACH, REACH)
    copies = [
        pltpu.make_async_copy(anomalies.at[:, first], low.at[pl.ds(0, ROWS)], sems.at[0]),
        pltpu.make_async_copy(anomalies.at[:, last], high.at[pl.ds(0, ROWS)], sems.at[1]),
        pltpu.make_async_copy(base.at[:, first], base_low, sems.at[2]),
        pltpu.make_async_copy(base.at[:, last], base_high, sems.at[3]),
    ]
    for copy in copies:
        copy.start()
    for copy in copies:
        copy.wait()
    low[ROWS:] = base_rows(base_low[...])
    high[ROWS:] = base_rows(base_high[...])


def stencil_kernel(
    place, offsets, anomalies, base, below, above, transform, out, base_mean, rows, means
):
    def fill(chunk, block, extra):
        at = chunk * PITCH
        rows[at : at + ROWS] = block
        rows[at + ROWS : at + PITCH] = extra

    inner = S // CH
    outer = REACH // CH
    for k in range(outer):
        c = slice(k * CH, k * CH + CH)
        fill(k, below[0:ROWS, c], below[ROWS:, c])
        fill(outer + inner + k, above[0:ROWS, c], above[ROWS:, c])
    for k in range(inner):
        c = slice(k * CH, k * CH + CH)
        fill(outer + k, anomalies[:, c], base_rows(base[:, c]))

    total = jnp.zeros((inner * PITCH, CH), F32)
    for k in range(2 * outer + 1):
        shift = (
            lax.broadcasted_iota(jnp.int32, (CH, CH), 0)
            - lax.broadcasted_iota(jnp.int32, (CH, CH), 1)
            + (k * CH - REACH)
        )
        count = jnp.zeros((CH, CH), F32)
        for tap in range(TAPS):
            count = count + jnp.where(shift == offsets[tap], 1.0 / TAPS, 0.0)
        total = total + jnp.dot(
            rows[k * PITCH : (k + inner) * PITCH], count.astype(BF), preferred_element_type=F32
        )
    for k in range(inner):
        at = k * PITCH
        c = slice(k % 2 * CH, k % 2 * CH + CH)
        out[k // 2, :, c] = total[at : at + ROWS].astype(BF)
        at = at + ROWS
        means[:, k * CH : k * CH + CH] = (
            total[at : at + 1] + total[at + 1 : at + 2] + total[at + 2 : at + 3]
        )
    for k in range(GROUP):
        out[k, :, COLS:] = transform[...]
    base_mean[...] = means[:, pl.ds(pl.multiple_of(place[1] * COLS, COLS), COLS)]


def weight_kernel(place, observed, obs_scale, obs_rows, weight_row, value_row):
    scale = obs_scale[...]
    square = scale * scale
    value = square * observed[...]
    at = obs_rows[...] - place[2]
    high = at >> 7
    low = at & 127
    lanes = lax.broadcasted_iota(jnp.int32, (128, S), 0) == low
    lanes = jnp.where(lanes, 1.0, 0.0).astype(BF)
    blocks = lax.broadcasted_iota(jnp.int32, (8, S), 0) == high
    parts = []
    for term in (square, value):
        for part in three_parts(term):
            parts.append(jnp.where(blocks, part.astype(F32), 0.0))
    left = jnp.concatenate(parts, axis=0).astype(BF)
    sums = lax.dot_general(left, lanes, NT, preferred_element_type=F32)
    weight = sums[0:8] + sums[8:16] + sums[16:24]
    worth = sums[24:32] + sums[32:40] + sums[40:48]
    for k in range(COLS // 128):
        weight_row[:, k * 128 : k * 128 + 128] = weight[k : k + 1]
        value_row[:, k * 128 : k * 128 + 128] = worth[k : k + 1]


def two_part_rows(value, count):
    high = value.astype(BF).astype(F32)
    low = value - high
    row = jnp.concatenate([high, low], axis=1)
    return jnp.concatenate([row, jnp.zeros((count - 1, 128), F32)], axis=0).astype(BF)


def gram_kernel(
    place, mine, other, base_mean, weight_row, value_row,
    out, transform, gathered, centred, scaled, part,
):
    core = place[0]
    for k in range(GROUP):
        for block, side in ((mine, core), (other, 1 - core)):
            at = pl.ds(pl.multiple_of(k * 128 + side * ROWS, ROWS), ROWS)
            gathered[at] = block[k, :, 0:COLS]
            transform[at] = block[k, :, COLS:]

    own = [pl.ds(pl.multiple_of(k * 128 + core * ROWS, ROWS), ROWS) for k in range(GROUP)]
    for k in range(COLS // CH):
        c = slice(k * CH, k * CH + CH)
        mean = jnp.dot(transform[...], gathered[:, c], preferred_element_type=F32)
        mean = mean + base_mean[:, c]
        predicted = mean + 0.25 * mean * mean
        average = jnp.sum(predicted, axis=0, keepdims=True) * (1.0 / M)
        difference = predicted - average
        centred[k] = difference
        weight = weight_row[:, c]
        scaled[:, c] = (difference * jnp.sqrt(weight * (1.0 / (M - 1)))).astype(BF)
        slope = (value_row[:, c] - weight * average) * (1.0 / math.sqrt(M - 1))
        for j in range(GROUP):
            product = centred[k, own[j]] * slope
            product = product[:, :128] + product[:, 128:]
            if k == 0:
                part[j * ROWS : j * ROWS + ROWS] = product
            else:
                part[j * ROWS : j * ROWS + ROWS] += product
    rows = jnp.concatenate([scaled[own[j]] for j in range(GROUP)], axis=0)
    slopes = jnp.sum(part[...].T, axis=0, keepdims=True)
    left_half = lax.broadcasted_iota(jnp.int32, (16, 128), 1) < ROWS
    gram = lax.dot_general(scaled[...], rows, NT, preferred_element_type=F32)
    for j in range(GROUP):
        lanes = slice(j // 2 * 128, j // 2 * 128 + 128)
        tail = two_part_rows(slopes[:, j * ROWS : j * ROWS + ROWS], 16)
        for y_hi in range(2):
            target = out.at[y_hi * GROUP + j]
            for z in range(16):
                at = z * 64 + y_hi * 32
                top = gram[at : at + 16, lanes]
                bottom = gram[at + 16 : at + 32, lanes]
                if j % 2 == 0:
                    packed = jnp.where(left_half, top, pltpu.roll(bottom, ROWS, 1))
                else:
                    packed = jnp.where(left_half, pltpu.roll(top, ROWS, 1), bottom)
                target[z * 16 : z * 16 + 16] = packed.astype(BF)
            target[256:272] = tail


def middle_kernel(parts, out):
    total = jnp.sum(parts[...].astype(F32), axis=0)
    tail = two_part_rows(total[256:257, 0:ROWS] + total[256:257, ROWS:], 8)
    for z in range(16):
        out[z, 0:16] = total[z * 16 : z * 16 + 16].astype(BF)
        out[z, 16:24] = tail


def last_kernel(place, parts, weights, hessian, gradient):
    total = jnp.sum(parts[...].astype(F32), axis=0)
    packed = total[0:16]
    tall = jnp.concatenate([packed, jnp.zeros((112, 128), F32)], axis=0).T
    block = jnp.concatenate([tall[0:ROWS, 0:16], tall[ROWS:, 0:16]], axis=1)
    row = lax.broadcasted_iota(jnp.int32, (ROWS, 32), 0) + place[3]
    column = lax.broadcasted_iota(jnp.int32, (ROWS, 32), 1) + place[4]
    hessian[...] = block + jnp.where(row == column, 1.0, 0.0)
    gradient[...] = weights[...] - (total[16:17, 0:ROWS] + total[16:17, ROWS:])


def on_device(base_state, anomalies, transform, weights, observed, obs_scale, obs_rows, offsets):
    state = lax.axis_index("z") * 2 + lax.axis_index("y_hi")
    core = lax.axis_index("core")
    column = lax.axis_index("y_lo") * 4 + lax.axis_index("x")
    place = jnp.stack(
        [core, column, state * S + column * COLS, (column * 2 + core) * ROWS, state * 32]
    ).astype(jnp.int32)
    row = lambda v: v.reshape(1, S)

    low, high = call(
        edge_kernel,
        (shape(PITCH, REACH), shape(PITCH, REACH)),
        [pl.BlockSpec(memory_space=pl.ANY)] * 2,
        scratch=[
            pltpu.VMEM((1, REACH), F32),
            pltpu.VMEM((1, REACH), F32),
            pltpu.SemaphoreType.DMA((4,)),
        ],
        nbytes=2**18,
    )(anomalies, row(base_state))
    up = [(s, s + 1) for s in range(31)]
    down = [(s + 1, s) for s in range(31)]
    below = lax.ppermute(high, ("z", "y_hi"), up)
    above = lax.ppermute(low, ("z", "y_hi"), down)

    weight_row, value_row = call(
        weight_kernel,
        (shape32(1, COLS), shape32(1, COLS)),
        [smem(), vmem(), vmem(), vmem()],
        flops=2 * 48 * S * 128,
        nbytes=2**20,
    )(place, row(observed), row(obs_scale), row(obs_rows))

    outgoing, base_mean = call(
        stencil_kernel,
        (shape(GROUP, ROWS, COLS + M), shape32(1, COLS)),
        [smem(), smem()] + [vmem()] * 5,
        scratch=[
            pltpu.VMEM(((S + 2 * REACH) // CH * PITCH, CH), BF),
            pltpu.VMEM((1, S), F32),
        ],
        flops=2 * 1280 * 1280 * 256,
        nbytes=2**21,
    )(place, offsets, anomalies, row(base_state), below, above, transform)

    mine = lax.all_to_all(outgoing, ("y_lo", "x"), 0, 0)
    other = lax.ppermute(mine, "core", [(0, 1), (1, 0)])

    parts = call(
        gram_kernel,
        shape(2 * GROUP, 272, 128),
        [smem()] + [vmem()] * 5,
        scratch=[
            pltpu.VMEM((M, M), BF),
            pltpu.VMEM((M, COLS), BF),
            pltpu.VMEM((COLS // CH, M, CH), F32),
            pltpu.VMEM((M, COLS), BF),
            pltpu.VMEM((GROUP * ROWS, 128), F32),
        ],
        flops=2 * M * M * 768,
        nbytes=2**22,
    )(place, mine, other, base_mean, weight_row, value_row)
    parts = lax.all_to_all(parts, ("y_hi", "y_lo", "x"), 0, 0)
    sums = call(middle_kernel, shape(16, 24, 128), [vmem()], nbytes=2**20)(parts)
    sums = lax.all_to_all(sums, "z", 0, 0)
    hessian, gradient = call(
        last_kernel, (shape32(ROWS, 32), shape32(1, ROWS)), [smem(), vmem(), vmem()], nbytes=2**18
    )(place, sums, weights.reshape(1, ROWS))
    return hessian, gradient.reshape(ROWS)


def solution(mesh):
    fine = Mesh(mesh.devices.reshape(16, 2, 2, 4, 2), ("z", "y_hi", "y_lo", "x", "core"))
    state = ("z", "y_hi")
    member = ("y_lo", "x", "core")
    placed = (
        P(state),
        P(member, state),
        P(member, None),
        P(member),
        P(state),
        P(state),
        P(state),
        P(),
    )
    return jax.shard_map(
        on_device,
        mesh=fine,
        in_specs=placed,
        out_specs=(P(member, state), P(member)),
        check_vma=False,
    )
```

time: 993 us -> 110 us (0.11)
  waiting for transfers between devices: 685 us -> 8.73 us
  local copies, waits for them, and re-layouts: 124 us -> 7.03 us
  blocking collectives: 128 us -> 75.4 us
  other arithmetic: 23.7 us -> 0 us
  between operations: 13.9 us -> 0.77 us
  matrix products: 12 us -> 0 us
    reduce_scatter x1 -> x0, waiting for transfers between devices: 560 us -> none  [on_device(): lax.psum_scatter(gram_block, 'state', scatter_dimension=1, tiled=True)]
    psum x2 -> x0, blocking collectives: 128 us -> none  [the longest x1 78.5 us: on_device(): gradient = weights - lax.psum(gradient_part, 'state')]
    all_gather x2 -> x0, waiting for transfers between devices: 123 us -> none  [the longest x1 64.4 us: on_device(): lax.all_gather(scaled, 'member', axis=0, tiled=True)]
    gather x8 -> x0, local copies, waits for them, and re-layouts: 120 us -> none  [on_device(): jnp.take(extended, local_rows + offsets[tap_index], axis=1)]
    all_to_all x0 -> x3, blocking collectives: none -> 75.4 us  [the longest x1 27.9 us: on_device(): sums = lax.all_to_all(sums, 'z', 0, 0)]
    dot_general x3 -> x0, matrix products: 12 us -> none  [the longest x1 6.55 us: on_device(): lax.dot_general(scaled, lax.all_gather(scaled, 'member', axis=0, tiled=Tr...]
  transfers between devices with their start and end apart: 5 -> 3, of which waited for: 4 -> 3; matrix products, arithmetic and copies ran while one was open for 1% -> 0% of each run, Pallas kernels for 0% -> 1%
where the time goes in v2:
time: 110 us
  blocking collectives  75.4 us (69%)
  Pallas kernels  9.35 us (8%)
  waiting for transfers between devices  8.73 us (8%)
  starting transfers between devices  8.3 us (8%)
  local copies, waits for them, and re-layouts  7.03 us (6%)
    all_to_all x1, blocking collectives, on_device(): sums = lax.all_to_all(sums, 'z', 0, 0)  27.9 us
    all_to_all x1, blocking collectives, on_device(): mine = lax.all_to_all(outgoing, ('y_lo', 'x'), 0, 0)  23.8 us
    all_to_all x1, blocking collectives, on_device(): parts = lax.all_to_all(parts, ('y_hi', 'y_lo', 'x'), 0, 0)  23.7 us
    unnamed x23, local copies, waits for them, and re-layouts  6.95 us
    ppermute x1, waiting for transfers between devices, on_device(): above = lax.ppermute(low, ('z', 'y_hi'), down)  5.8 us
    ppermute x1, starting transfers between devices, on_device(): below = lax.ppermute(high, ('z', 'y_hi'), up)  5.1 us
    pallas_call x1, Pallas kernels, on_device(): call(gram_kernel, shape(2 * GROUP, 272, 128), [smem()] + [vmem()] * 5, sc...  4.41 us
    pallas_call x1, Pallas kernels, on_device(): call(stencil_kernel, (shape(GROUP, ROWS, COLS + M), shape32(1, COLS)), [s...  2.42 us
  transfers between devices with their start and end apart: 3, of which 3 were waited for; matrix products, arithmetic and copies ran while one was open for 0% of the time, Pallas kernels for 1%

profile of v2, /device:TPU:2, one launch (start us, length us, event | category | flops | bytes accessed | tf_op | source)
XLA Modules:
  0.0 109.6 jit_solution(10855248605205557592)
XLA Ops:
  0.6 0.0 copy-start
  0.6 1.0 copy-done
  1.7 0.0 copy-start.2
  1.7 0.7 copy-done.2
  2.4 0.1 shard_map.95
  2.5 5.1 %collective-permute-start = (bf16[80,512]{1,0:T(8,128)(2,1)S(1)}, bf16[80,512]{1,0:T(8,128)(2,1)S(1)}, u32[]{:S(2)}, u32[]{:S(2)}) collective-permute-start(bf16[80,512]{1,0:T(8,128)(2,1)S(1)} %get-tuple-element.10), channel_id=1, source_target_pairs={{0,16},{16,32},{32,48},{48,64},{64,80},{80,96},{96,112},{112,128},... | collective-permute-start | bytes 245768 | tf_op jit(solution)/shard_map/ppermute | solution.py:250
  7.6 1.3 %collective-permute-start.1 = (bf16[80,512]{1,0:T(8,128)(2,1)S(1)}, bf16[80,512]{1,0:T(8,128)(2,1)S(1)}, u32[]{:S(2)}, u32[]{:S(2)}) collective-permute-start(bf16[80,512]{1,0:T(8,128)(2,1)S(1)} %get-tuple-element.11), channel_id=1, source_target_pairs={{16,0},{32,16},{48,32},{64,48},{80,64},{96,80},{112,96},{128,112},... | collective-permute-start | bytes 245768 | tf_op jit(solution)/shard_map/ppermute | solution.py:251
  8.9 0.1 stack.23.place
  9.0 0.6 collective-permute-done.below
  9.6 5.8 %collective-permute-done.1.above = bf16[80,512]{1,0:T(8,128)(2,1)S(1)} collective-permute-done((bf16[80,512]{1,0:T(8,128)(2,1)S(1)}, bf16[80,512]{1,0:T(8,128)(2,1)S(1)}, u32[]{:S(2)}, u32[]{:S(2)}) %collective-permute-start.1) | collective-permute-done | bytes 81952 | tf_op jit(solution)/shard_map/ppermute | solution.py:251
  15.4 0.0 copy-start.1
  15.4 1.0 copy-done.1
  16.5 0.0 copy-start.3
  16.5 0.7 copy-done.3
  17.2 0.0 copy-start.5
  17.2 0.9 copy-done.5
  18.1 0.0 copy-start.9
  18.1 0.7 copy-done.9
  18.8 2.4 %shard_map.96 = (bf16[8,64,1536]{2,1,0:T(8,128)(2,1)S(1)}, f32[1,512]{1,0:T(1,128)S(1)}) custom-call(s32[5]{0:T(128)S(1)} %stack.23.place, s32[8]{0:T(128)S(1)} %copy-done.9, bf16[64,4096]{1,0:T(8,128)(2,1)S(1)} %copy-done.1, f32[1,4096]{1,0:T(1,128)S(1)} %bitcast.12, bf16[80,512]{1,0:T(8,128)(2,1)S(1)} %collective-permute-done.below, ...), custom_call_target="tpu_custom_call" | custom-call | flops 838860800 | bytes 2097152 | tf_op jit(solution)/shard_map/pallas_call | solution.py:261
  21.2 0.0 copy-start.6
  21.2 0.0 copy-start.7
  21.2 0.0 copy-start.8
  21.2 23.8 %all_to_all.15.mine = bf16[8,64,1536]{2,1,0:T(8,128)(2,1)S(1)} all-to-all(bf16[8,64,1536]{2,1,0:T(8,128)(2,1)S(1)} %get-tuple-element.12), channel_id=1, replica_groups=mesh['z'=16,'y_hi'=2,'y_lo'=2,'x'=4,'core'=2] {'y_lo','x'}, dimensions={0} | all-to-all | bytes 3145728 | tf_op jit(solution)/shard_map/all_to_all | solution.py:273
  45.0 1.9 %collective-permute-start.2 = (bf16[8,64,1536]{2,1,0:T(8,128)(2,1)S(1)}, bf16[8,64,1536]{2,1,0:T(8,128)(2,1)S(1)}, u32[]{:S(2)}, u32[]{:S(2)}) collective-permute-start(bf16[8,64,1536]{2,1,0:T(8,128)(2,1)S(1)} %all_to_all.15.mine), channel_id=1, source_target_pairs={{0,1},{1,0},{2,3},{3,2},{4,5},{5,4},{6,7},{7,6},{8,9},{9,8},{10,11... | collective-permute-start | bytes 4718600 | tf_op jit(solution)/shard_map/ppermute | solution.py:274
  46.9 0.0 copy-done.6
  46.9 0.0 copy-done.7
  46.9 0.0 copy-done.8
  46.9 1.1 shard_map.97
  48.0 2.3 %collective-permute-done.2.other = bf16[8,64,1536]{2,1,0:T(8,128)(2,1)S(1)} collective-permute-done((bf16[8,64,1536]{2,1,0:T(8,128)(2,1)S(1)}, bf16[8,64,1536]{2,1,0:T(8,128)(2,1)S(1)}, u32[]{:S(2)}, u32[]{:S(2)}) %collective-permute-start.2) | collective-permute-done | bytes 1572896 | tf_op jit(solution)/shard_map/ppermute | solution.py:274
  50.3 0.0 copy-start.10
  50.3 1.2 %copy-done.10 = bf16[8,64,1536]{2,1,0:T(8,128)(2,1)} copy-done((bf16[8,64,1536]{2,1,0:T(8,128)(2,1)}, bf16[8,64,1536]{2,1,0:T(8,128)(2,1)S(1)}, u32[]{:S(2)}) %copy-start.10) | copy-done | bytes 1572888
  51.5 4.4 %shard_map.98 = bf16[16,272,128]{2,1,0:T(8,128)(2,1)S(1)} custom-call(s32[5]{0:T(128)S(1)} %stack.23.place, bf16[8,64,1536]{2,1,0:T(8,128)(2,1)S(1)} %all_to_all.15.mine, bf16[8,64,1536]{2,1,0:T(8,128)(2,1)} %copy-done.10, f32[1,512]{1,0:T(1,128)S(1)} %get-tuple-element.13.base_mean, f32[1,512]{1,0:T(1,128)S(1)} %get-tuple-element.14.weight_row, ...), custom_call_target="tpu_custom_call" | custom-call | flops 1610612736 | bytes 4194304 | tf_op jit(solution)/shard_map/pallas_call | solution.py:276
  55.9 0.0 copy-start.4
  55.9 23.7 %all_to_all.16.parts = bf16[16,272,128]{2,1,0:T(8,128)(2,1)S(1)} all-to-all(bf16[16,272,128]{2,1,0:T(8,128)(2,1)S(1)} %shard_map.98), channel_id=1, replica_groups=mesh['z'=16,'y_hi'=2,'y_lo'=2,'x'=4,'core'=2] {'y_hi','y_lo','x'}, dimensions={0} | all-to-all | bytes 2228224 | tf_op jit(solution)/shard_map/all_to_all | solution.py:290
  79.6 0.2 shard_map.99
  79.8 27.9 %all_to_all.17.parts = bf16[16,24,128]{2,1,0:T(8,128)(2,1)S(1)} all-to-all(bf16[16,24,128]{2,1,0:T(8,128)(2,1)S(1)} %shard_map.99), channel_id=1, replica_groups=mesh['z'=16,'y_hi'=2,'y_lo'=2,'x'=4,'core'=2] {'z'}, dimensions={0} | all-to-all | bytes 196608 | tf_op jit(solution)/shard_map/all_to_all | solution.py:292
  107.7 0.0 copy-done.4
  107.7 1.1 %shard_map.100 = (f32[64,32]{1,0:T(8,128)S(1)}, f32[1,64]{1,0:T(1,128)}) custom-call(s32[5]{0:T(128)S(1)} %stack.23.place, bf16[16,24,128]{2,1,0:T(8,128)(2,1)S(1)} %all_to_all.17.parts, f32[1,64]{1,0:T(1,128)S(1)} %bitcast.13), custom_call_target="tpu_custom_call" | custom-call | bytes 262144 | tf_op jit(solution)/shard_map/pallas_call | solution.py:293
  108.9 0.7 copy.10
Async XLA Ops:
  0.6 1.0 copy-start
  1.7 0.7 copy-start.2
  2.5 7.1 %collective-permute-start = (bf16[80,512]{1,0:T(8,128)(2,1)S(1)}, bf16[80,512]{1,0:T(8,128)(2,1)S(1)}, u32[]{:S(2)}, u32[]{:S(2)}) collective-permute-start(bf16[80,512]{1,0:T(8,128)(2,1)S(1)} %get-tuple-element.10), channel_id=1, source_target_pairs={{0,16},{16,32},{32,48},{48,64},{64,80},{80,96},{96,112},{112,128},... | collective-permute-start | bytes 245768 | tf_op jit(solution)/shard_map/ppermute | solution.py:250
  7.6 7.8 %collective-permute-start.1 = (bf16[80,512]{1,0:T(8,128)(2,1)S(1)}, bf16[80,512]{1,0:T(8,128)(2,1)S(1)}, u32[]{:S(2)}, u32[]{:S(2)}) collective-permute-start(bf16[80,512]{1,0:T(8,128)(2,1)S(1)} %get-tuple-element.11), channel_id=1, source_target_pairs={{16,0},{32,16},{48,32},{64,48},{80,64},{96,80},{112,96},{128,112},... | collective-permute-start | bytes 245768 | tf_op jit(solution)/shard_map/ppermute | solution.py:251
  15.4 1.0 copy-start.1
  16.5 0.7 copy-start.3
  17.2 0.9 copy-start.5
  18.1 0.7 copy-start.9
  21.2 25.7 %copy-start.6 = (f32[4096]{0:T(1024)S(1)}, f32[4096]{0:T(1024)}, u32[]{:S(2)}) copy-start(f32[4096]{0:T(1024)} %param.12) | copy-start | bytes 49156
  21.2 25.7 %copy-start.7 = (f32[4096]{0:T(1024)S(1)}, f32[4096]{0:T(1024)}, u32[]{:S(2)}) copy-start(f32[4096]{0:T(1024)} %param.13) | copy-start | bytes 49156
  21.2 25.7 %copy-start.8 = (s32[4096]{0:T(1024)S(1)}, s32[4096]{0:T(1024)}, u32[]{:S(2)}) copy-start(s32[4096]{0:T(1024)} %param.14) | copy-start | bytes 49156
  45.0 5.3 %collective-permute-start.2 = (bf16[8,64,1536]{2,1,0:T(8,128)(2,1)S(1)}, bf16[8,64,1536]{2,1,0:T(8,128)(2,1)S(1)}, u32[]{:S(2)}, u32[]{:S(2)}) collective-permute-start(bf16[8,64,1536]{2,1,0:T(8,128)(2,1)S(1)} %all_to_all.15.mine), channel_id=1, source_target_pairs={{0,1},{1,0},{2,3},{3,2},{4,5},{5,4},{6,7},{7,6},{8,9},{9,8},{10,11... | collective-permute-start | bytes 4718600 | tf_op jit(solution)/shard_map/ppermute | solution.py:274
  50.3 1.2 %copy-start.10 = (bf16[8,64,1536]{2,1,0:T(8,128)(2,1)}, bf16[8,64,1536]{2,1,0:T(8,128)(2,1)S(1)}, u32[]{:S(2)}) copy-start(bf16[8,64,1536]{2,1,0:T(8,128)(2,1)S(1)} %collective-permute-done.2.other) | copy-start | bytes 4718596
  55.9 51.9 %copy-start.4 = (f32[64]{0:T(128)S(1)}, f32[64]{0:T(128)}, u32[]{:S(2)}) copy-start(f32[64]{0:T(128)} %param.11) | copy-start | bytes 772

commit v3 on v2

v3 whole, which is shorter than its diff:
```python
import math

import jax
import jax.numpy as jnp
from jax import lax
from jax.experimental import pallas as pl
from jax.experimental.pallas import tpu as pltpu
from jax.sharding import Mesh, PartitionSpec as P

M = 1024
S = 4096
REACH = 512
TAPS = 8
ROWS = 64
GROUP = 8
COLS = S // GROUP
CH = 256
PITCH = 80
EDGE = 2 * REACH
TILES = 2 * REACH // CH + 1
OUTER = EDGE // CH
INNER = S // CH - OUTER
BF = jnp.bfloat16
F32 = jnp.float32
NT = (((1,), (1,)), ((), ()))
MIB = 2**20
FULL = 63


def call(kernel, out_shape, in_specs, scratch=(), flops=0, nbytes=0, limit=16, alias=None):
    return pl.pallas_call(
        kernel,
        out_shape=out_shape,
        in_specs=in_specs,
        out_specs=jax.tree.map(lambda _: pl.BlockSpec(memory_space=pltpu.VMEM), out_shape),
        scratch_shapes=list(scratch),
        compiler_params=pltpu.CompilerParams(vmem_limit_bytes=limit * MIB),
        input_output_aliases=alias or {},
        cost_estimate=pl.CostEstimate(flops=flops, bytes_accessed=nbytes, transcendentals=0),
    )


def spot():
    state = lax.axis_index("z") * 2 + lax.axis_index("y_hi")
    column = lax.axis_index("y_lo") * 4 + lax.axis_index("x")
    return state, column, (column * 2 + lax.axis_index("core")) * ROWS, state * 32


def vmem():
    return pl.BlockSpec(memory_space=pltpu.VMEM)


def smem():
    return pl.BlockSpec(memory_space=pltpu.SMEM)


def hbm():
    return pl.BlockSpec(memory_space=pltpu.HBM)


def shape(*dims):
    return jax.ShapeDtypeStruct(dims, BF)


def shape32(*dims):
    return jax.ShapeDtypeStruct(dims, F32)


def three_parts(value):
    high = value.astype(BF)
    rest = value - high.astype(F32)
    middle = rest.astype(BF)
    low = (rest - middle.astype(F32)).astype(BF)
    return high, middle, low


def base_rows(base):
    high, middle, low = three_parts(base)
    zeros = jnp.zeros((13, base.shape[1]), BF)
    return jnp.concatenate([high, middle, low, zeros], axis=0)


def sums_at_rows(first_line, lines, observed, obs_scale, at):
    square = obs_scale * obs_scale
    value = square * observed
    high = at >> 7
    low = at & 127
    lanes = lax.broadcasted_iota(jnp.int32, (128, S), 0) == low
    lanes = jnp.where(lanes, 1.0, 0.0).astype(BF)
    line = lax.broadcasted_iota(jnp.int32, (8, S), 0)
    blocks = (line + first_line == high) & (line < lines)
    parts = []
    for term in (square, value):
        for part in three_parts(term):
            parts.append(jnp.where(blocks, part.astype(F32), 0.0))
    left = jnp.concatenate(parts, axis=0).astype(BF)
    sums = lax.dot_general(left, lanes, NT, preferred_element_type=F32)
    weight = sums[0:8] + sums[8:16] + sums[16:24]
    value = sums[24:32] + sums[32:40] + sums[40:48]
    return [weight[k : k + 1] for k in range(lines)], [value[k : k + 1] for k in range(lines)]


def edge_kernel(
    anomalies, base, observed, obs_scale, obs_rows, edge,
    base_edge, observed_all, scale_all, rows_all, sems,
):
    border = pl.ds(S - EDGE, EDGE)
    copies = [
        pltpu.make_async_copy(obs_rows, rows_all, sems.at[0]),
        pltpu.make_async_copy(obs_scale, scale_all, sems.at[1]),
        pltpu.make_async_copy(observed, observed_all, sems.at[2]),
        pltpu.make_async_copy(base.at[:, border], base_edge, sems.at[3]),
        pltpu.make_async_copy(anomalies.at[:, border], edge.at[pl.ds(0, ROWS)], sems.at[4]),
    ]
    for copy in copies:
        copy.start()
    for copy in copies[:4]:
        copy.wait()
    weight, value = sums_at_rows(
        S // 128 - 4, 4, observed_all[...], scale_all[...], rows_all[...] - spot()[0] * S
    )
    empty = [jnp.zeros((1, EDGE - REACH), F32)]
    extra = list(three_parts(base_edge[...]))
    for row in (weight, value):
        extra += three_parts(jnp.concatenate(empty + row, axis=1))
    extra.append(jnp.zeros((7, EDGE), BF))
    edge[ROWS:] = jnp.concatenate(extra, axis=0)
    copies[4].wait()


def banded(rows, band, first, count):
    total = jnp.zeros((count * PITCH, CH), F32)
    for k in range(TILES):
        at = (first + k) * PITCH
        total = total + jnp.dot(
            rows[at : at + count * PITCH],
            band[k * CH : k * CH + CH],
            preferred_element_type=F32,
        )
    return total


def put_chunk(total, k, chunk, out, means):
    at = k * PITCH
    out[chunk // 2, :, chunk % 2 * CH : chunk % 2 * CH + CH] = total[at : at + ROWS].astype(BF)
    at = at + ROWS
    means[:, chunk * CH : chunk * CH + CH] = (
        total[at : at + 1] + total[at + 1 : at + 2] + total[at + 2 : at + 3]
    )


def inner_kernel(offsets, anomalies, base, transform, out, band, border, means, rows, sems):
    copies = [
        pltpu.make_async_copy(transform, out.at[k, :, pl.ds(COLS, M)], sems.at[k])
        for k in range(GROUP)
    ]
    for copy in copies:
        copy.start()
    for k in range(S // CH):
        c = slice(k * CH, k * CH + CH)
        at = k * PITCH
        rows[at : at + ROWS] = anomalies[:, c]
        rows[at + ROWS : at + PITCH] = base_rows(base[:, c])
    for k in range(TILES):
        shift = (
            lax.broadcasted_iota(jnp.int32, (CH, CH), 0)
            - lax.broadcasted_iota(jnp.int32, (CH, CH), 1)
            + (k * CH - REACH)
        )
        count = jnp.zeros((CH, CH), F32)
        for tap in range(TAPS):
            count = count + jnp.where(shift == offsets[tap], 1.0 / TAPS, 0.0)
        band[k * CH : k * CH + CH] = count.astype(BF)
    total = banded(rows, band, 0, INNER)
    means[...] = jnp.zeros_like(means)
    for k in range(INNER):
        put_chunk(total, k, k + OUTER, out, means)
    border[...] = rows[0 : OUTER * PITCH]
    for copy in copies:
        copy.wait()


def outer_kernel(edge, band, border, means_in, out_in, out, base_mean, rows, means):
    state, column, _, _ = spot()
    whole = state > 0
    means[...] = means_in[...]
    for k in range(OUTER):
        at = k * PITCH
        rows[at : at + PITCH] = edge[:, k * CH : k * CH + CH]
        rows[at + OUTER * PITCH : at + (OUTER + 1) * PITCH] = border[at : at + PITCH]
    seen = jnp.where(whole, 1.0, 0.0).astype(BF)
    before = rows[2 * PITCH : 4 * PITCH]
    after = rows[4 * PITCH : 6 * PITCH]
    rows[4 * PITCH : 6 * PITCH] = after * seen
    total = banded(rows, band, 0, 2)
    for k in range(2):
        put_chunk(total, k, k, out, means)
    rows[4 * PITCH : 6 * PITCH] = after
    rows[2 * PITCH : 4 * PITCH] = before * seen
    total = banded(rows, band, 2, 2)
    for k in range(2):
        put_chunk(total, k, k + 2, out, means)
    base_mean[...] = means[:, pl.ds(pl.multiple_of(column * COLS, COLS), COLS)]


def weight_kernel(observed, obs_scale, obs_rows, edge, weight_row, value_row):
    state, column, _, _ = spot()
    weight, value = sums_at_rows(
        (column - 1) * 4, 4, observed[...], obs_scale[...], obs_rows[...] - state * S
    )
    half = pl.ds(EDGE - REACH, REACH)
    row = lambda k: edge[ROWS : ROWS + 16, half][k : k + 1].astype(F32)
    mine = column > 0
    for rows, target, at in ((weight, weight_row, 3), (value, value_row, 6)):
        sent = row(at) + row(at + 1) + row(at + 2)
        target[...] = jnp.where(mine, jnp.concatenate(rows, axis=1), sent)


def two_part_rows(value, count):
    high = value.astype(BF).astype(F32)
    low = value - high
    row = jnp.concatenate([high, low], axis=1)
    return jnp.concatenate([row, jnp.zeros((count - 1, 128), F32)], axis=0).astype(BF)


def gram_kernel(
    mine, other, base_mean, weight_row, value_row,
    out, transform, gathered, centred, scaled, part,
):
    core = lax.axis_index("core")
    for k in range(GROUP):
        for block, side in ((mine, core), (other, 1 - core)):
            at = pl.ds(pl.multiple_of(k * 128 + side * ROWS, ROWS), ROWS)
            gathered[at] = block[k, :, 0:COLS]
            transform[at] = block[k, :, COLS:]

    own = [pl.ds(pl.multiple_of(k * 128 + core * ROWS, ROWS), ROWS) for k in range(GROUP)]
    for k in range(COLS // CH):
        c = slice(k * CH, k * CH + CH)
        mean = jnp.dot(transform[...], gathered[:, c], preferred_element_type=F32)
        mean = mean + base_mean[:, c]
        predicted = mean + 0.25 * mean * mean
        average = jnp.sum(predicted, axis=0, keepdims=True) * (1.0 / M)
        difference = predicted - average
        centred[k] = difference
        weight = weight_row[:, c]
        scaled[:, c] = (difference * jnp.sqrt(weight * (1.0 / (M - 1)))).astype(BF)
        slope = (value_row[:, c] - weight * average) * (1.0 / math.sqrt(M - 1))
        for j in range(GROUP):
            product = centred[k, own[j]] * slope
            product = product[:, :128] + product[:, 128:]
            if k == 0:
                part[j * ROWS : j * ROWS + ROWS] = product
            else:
                part[j * ROWS : j * ROWS + ROWS] += product
    rows = jnp.concatenate([scaled[own[j]] for j in range(GROUP)], axis=0)
    slopes = jnp.sum(part[...].T, axis=0, keepdims=True)
    left_half = lax.broadcasted_iota(jnp.int32, (16, 128), 1) < ROWS
    gram = lax.dot_general(scaled[...], rows, NT, preferred_element_type=F32)
    for j in range(GROUP):
        lanes = slice(j // 2 * 128, j // 2 * 128 + 128)
        tail = two_part_rows(slopes[:, j * ROWS : j * ROWS + ROWS], 16)
        for y_hi in range(2):
            target = out.at[y_hi * GROUP + j]
            for z in range(16):
                at = z * 64 + y_hi * 32
                top = gram[at : at + 16, lanes]
                bottom = gram[at + 16 : at + 32, lanes]
                if j % 2 == 0:
                    packed = jnp.where(left_half, top, pltpu.roll(bottom, ROWS, 1))
                else:
                    packed = jnp.where(left_half, pltpu.roll(top, ROWS, 1), bottom)
                target[z * 16 : z * 16 + 16] = packed.astype(BF)
            target[256:272] = tail


def middle_kernel(parts, out):
    total = jnp.sum(parts[...].astype(F32), axis=0)
    tail = two_part_rows(total[256:257, 0:ROWS] + total[256:257, ROWS:], 8)
    for z in range(16):
        out[z, 0:16] = total[z * 16 : z * 16 + 16].astype(BF)
        out[z, 16:24] = tail


def last_kernel(parts, weights, hessian, gradient):
    _, _, row0, column0 = spot()
    total = jnp.sum(parts[...].astype(F32), axis=0)
    row = lax.broadcasted_iota(jnp.int32, (16, ROWS), 1) + row0
    column = lax.broadcasted_iota(jnp.int32, (16, ROWS), 0) + column0
    for half in range(2):
        block = total[0:16, half * ROWS : half * ROWS + ROWS]
        same = row == column + half * 16
        hessian[half * 16 : half * 16 + 16] = block + jnp.where(same, 1.0, 0.0)
    gradient[...] = weights[...] - (total[16:17, 0:ROWS] + total[16:17, ROWS:])


def on_device(base_state, anomalies, transform, weights, observed, obs_scale, obs_rows, offsets):
    row = lambda v: v.reshape(1, S)
    base = row(base_state)
    obs = (row(observed), row(obs_scale), row(obs_rows))

    edge = call(
        edge_kernel,
        shape(PITCH, EDGE),
        [hbm()] * 5,
        scratch=[
            pltpu.VMEM((1, EDGE), F32),
            pltpu.VMEM((1, S), F32),
            pltpu.VMEM((1, S), F32),
            pltpu.VMEM((1, S), jnp.int32),
            pltpu.SemaphoreType.DMA((5,)),
        ],
        nbytes=MIB,
        limit=FULL,
    )(anomalies, base, *obs)
    edge = lax.ppermute(edge, ("z", "y_hi"), [(s, (s + 1) % 32) for s in range(32)])

    outgoing, band, border, means = call(
        inner_kernel,
        (
            shape(GROUP, ROWS, COLS + M),
            shape(TILES * CH, CH),
            shape(OUTER * PITCH, CH),
            shape32(1, S),
        ),
        [smem()] + [vmem()] * 2 + [hbm()],
        scratch=[
            pltpu.VMEM((S // CH * PITCH, CH), BF),
            pltpu.SemaphoreType.DMA((GROUP,)),
        ],
        flops=2 * INNER * PITCH * TILES * CH * CH,
        nbytes=4 * MIB,
    )(offsets, anomalies, base, transform)
    outgoing, base_mean = call(
        outer_kernel,
        (shape(GROUP, ROWS, COLS + M), shape32(1, COLS)),
        [vmem()] * 5,
        scratch=[pltpu.VMEM((2 * OUTER * PITCH, CH), BF), pltpu.VMEM((1, S), F32)],
        flops=2 * OUTER * PITCH * TILES * CH * CH,
        nbytes=MIB,
        alias={4: 0},
    )(edge, band, border, means, outgoing)

    mine = lax.all_to_all(outgoing, ("y_lo", "x"), 0, 0)
    other = lax.ppermute(mine, "core", [(0, 1), (1, 0)])

    weight_row, value_row = call(
        weight_kernel,
        (shape32(1, COLS), shape32(1, COLS)),
        [vmem()] * 4,
        flops=2 * 48 * S * 128,
        nbytes=MIB,
    )(*obs, edge)

    parts = call(
        gram_kernel,
        shape(2 * GROUP, 272, 128),
        [vmem()] * 5,
        scratch=[
            pltpu.VMEM((M, M), BF),
            pltpu.VMEM((M, COLS), BF),
            pltpu.VMEM((COLS // CH, M, CH), F32),
            pltpu.VMEM((M, COLS), BF),
            pltpu.VMEM((GROUP * ROWS, 128), F32),
        ],
        flops=2 * M * M * 768,
        nbytes=4 * MIB,
        limit=32,
    )(mine, other, base_mean, weight_row, value_row)
    parts = lax.all_to_all(parts, ("y_hi", "y_lo", "x"), 0, 0)
    sums = call(middle_kernel, shape(16, 24, 128), [vmem()], nbytes=2**20)(parts)
    sums = lax.all_to_all(sums, "z", 0, 0)
    hessian, gradient = call(
        last_kernel, (shape32(32, ROWS), shape32(1, ROWS)), [vmem()] * 2, nbytes=MIB // 4
    )(sums, weights.reshape(1, ROWS))
    return hessian.T, gradient.reshape(ROWS)


def solution(mesh):
    fine = Mesh(mesh.devices.reshape(16, 2, 2, 4, 2), ("z", "y_hi", "y_lo", "x", "core"))
    state = ("z", "y_hi")
    member = ("y_lo", "x", "core")
    placed = (
        P(state),
        P(member, state),
        P(member, None),
        P(member),
        P(state),
        P(state),
        P(state),
        P(),
    )
    return jax.shard_map(
        on_device,
        mesh=fine,
        in_specs=placed,
        out_specs=(P(member, state), P(member)),
        check_vma=False,
    )
```

time: 110 us -> 98.4 us (0.89)
  blocking collectives: 75.4 us -> 67.3 us
  local copies, waits for them, and re-layouts: 7.03 us -> 3.34 us
  waiting for transfers between devices: 8.73 us -> 10.2 us
  starting transfers between devices: 8.3 us -> 7.01 us
    all_to_all x1, blocking collectives: 27.9 us -> 22 us  [on_device(): sums = lax.all_to_all(sums, 'z', 0, 0)]
    unnamed x23 -> x16, local copies, waits for them, and re-layouts: 6.95 us -> 3.34 us
    all_to_all x1, blocking collectives: 23.7 us -> 20.8 us  [on_device(): parts = lax.all_to_all(parts, ('y_hi', 'y_lo', 'x'), 0, 0)]
    ppermute x2 -> x1, starting transfers between devices: 6.39 us -> 5.1 us  [on_device(): lax.ppermute(edge, ('z', 'y_hi'), [(s, (s + 1) % 32) for s in range(32)])]
    ppermute x2 -> x1, waiting for transfers between devices: 6.44 us -> 7.45 us  [on_device(): lax.ppermute(edge, ('z', 'y_hi'), [(s, (s + 1) % 32) for s in range(32)])]
    pallas_call x5 -> x6, Pallas kernels: 9.12 us -> 9.07 us  [the longest x1 2.81 us: on_device(): call(gram_kernel, shape(2 * GROUP, 272, 128), [vmem()] * 5, scratch=[pltp...]
  transfers between devices with their start and end apart: 3 -> 2, of which waited for: 3 -> 2; matrix products, arithmetic and copies ran while one was open for 0% -> 0% of each run, Pallas kernels for 1% -> 3%
where the time goes in v3:
time: 98.4 us; the launch traced here: 97.9 us
  blocking collectives  67.3 us (68%)
  waiting for transfers between devices  10.2 us (10%)
  Pallas kernels  9.3 us (9%)
  starting transfers between devices  7.01 us (7%)
  local copies, waits for them, and re-layouts  3.34 us (3%)
    all_to_all x1, blocking collectives, on_device(): mine = lax.all_to_all(outgoing, ('y_lo', 'x'), 0, 0)  24.5 us
    all_to_all x1, blocking collectives, on_device(): sums = lax.all_to_all(sums, 'z', 0, 0)  22 us
    all_to_all x1, blocking collectives, on_device(): parts = lax.all_to_all(parts, ('y_hi', 'y_lo', 'x'), 0, 0)  20.8 us
    ppermute x1, waiting for transfers between devices, on_device(): lax.ppermute(edge, ('z', 'y_hi'), [(s, (s + 1) % 32) for s in range(32)])  7.45 us
    ppermute x1, starting transfers between devices, on_device(): lax.ppermute(edge, ('z', 'y_hi'), [(s, (s + 1) % 32) for s in range(32)])  5.1 us
    unnamed x16, local copies, waits for them, and re-layouts  3.34 us
    pallas_call x1, Pallas kernels, on_device(): call(gram_kernel, shape(2 * GROUP, 272, 128), [vmem()] * 5, scratch=[pltp...  2.81 us
    ppermute x1, waiting for transfers between devices, on_device(): other = lax.ppermute(mine, 'core', [(0, 1), (1, 0)])  2.79 us
  transfers between devices with their start and end apart: 2, of which 2 were waited for; matrix products, arithmetic and copies ran while one was open for 0% of the time, Pallas kernels for 3%

profile of v3, /device:TPU:2, one launch (start us, length us, event | category | flops | bytes accessed | tf_op | source)
XLA Modules:
  0.0 97.9 jit_solution(8337100896671654737)
XLA Ops:
  0.6 2.0 %shard_map.95 = bf16[80,1024]{1,0:T(8,128)(2,1)} custom-call(bf16[64,4096]{1,0:T(8,128)(2,1)} %anomalies.3, f32[1,4096]{1,0:T(1,128)} %bitcast.13, f32[1,4096]{1,0:T(1,128)} %bitcast.7, f32[1,4096]{1,0:T(1,128)} %bitcast.9, s32[1,4096]{1,0:T(1,128)} %bitcast.11), custom_call_target="tpu_custom_call" | custom-call | bytes 1048576 | tf_op jit(solution)/shard_map/pallas_call | solution.py:302
  2.7 5.1 %collective-permute-start = (bf16[80,1024]{1,0:T(8,128)(2,1)}, bf16[80,1024]{1,0:T(8,128)(2,1)S(1)}, u32[]{:S(2)}, u32[]{:S(2)}) collective-permute-start(bf16[80,1024]{1,0:T(8,128)(2,1)} %shard_map.95), channel_id=1, source_target_pairs={{0,16},{16,32},{32,48},{48,64},{64,80},{80,96},{96,112},{112,128},... | collective-permute-start | bytes 491528 | tf_op jit(solution)/shard_map/ppermute | solution.py:316
  7.8 0.0 copy-start
  7.8 1.0 %copy-done = bf16[64,4096]{1,0:T(8,128)(2,1)S(1)} copy-done((bf16[64,4096]{1,0:T(8,128)(2,1)S(1)}, bf16[64,4096]{1,0:T(8,128)(2,1)}, u32[]{:S(2)}) %copy-start) | copy-done | bytes 524312
  8.8 0.0 copy-start.4
  8.8 0.7 copy-done.4
  9.5 0.0 copy-start.6
  9.5 0.9 copy-done.6
  10.4 0.0 copy-start.7
  10.4 0.7 copy-done.7
  11.1 2.5 %shard_map.96 = (bf16[8,64,1536]{2,1,0:T(8,128)(2,1)S(1)}, bf16[1280,256]{1,0:T(8,128)(2,1)S(1)}, bf16[320,256]{1,0:T(8,128)(2,1)S(1)}, f32[1,4096]{1,0:T(1,128)S(1)}) custom-call(s32[8]{0:T(128)S(1)} %copy-done.7, bf16[64,4096]{1,0:T(8,128)(2,1)S(1)} %copy-done, f32[1,4096]{1,0:T(1,128)S(1)} %bitcast.14, bf16[64,1024]{1,0:T(8,128)(2,1)S(1)} %copy-done.6), custom_call_target="tpu_custom_call" | custom-call | flops 629145600 | bytes 4194304 | tf_op jit(solution)/shard_map/pallas_call | solution.py:318
  13.6 7.5 %collective-permute-done.edge = bf16[80,1024]{1,0:T(8,128)(2,1)S(1)} collective-permute-done((bf16[80,1024]{1,0:T(8,128)(2,1)}, bf16[80,1024]{1,0:T(8,128)(2,1)S(1)}, u32[]{:S(2)}, u32[]{:S(2)}) %collective-permute-start) | collective-permute-done | bytes 163872 | tf_op jit(solution)/shard_map/ppermute | solution.py:316
  21.1 0.4 shard_map.97
  21.5 0.0 copy-start.1
  21.5 0.0 copy-start.2
  21.5 0.0 copy-start.3
  21.5 24.5 %all_to_all.15.mine = bf16[8,64,1536]{2,1,0:T(8,128)(2,1)S(1)} all-to-all(bf16[8,64,1536]{2,1,0:T(8,128)(2,1)S(1)} %get-tuple-element.16), channel_id=1, replica_groups=mesh['z'=16,'y_hi'=2,'y_lo'=2,'x'=4,'core'=2] {'y_lo','x'}, dimensions={0} | all-to-all | bytes 3145728 | tf_op jit(solution)/shard_map/all_to_all | solution.py:344
  46.0 1.9 %collective-permute-start.1 = (bf16[8,64,1536]{2,1,0:T(8,128)(2,1)S(1)}, bf16[8,64,1536]{2,1,0:T(8,128)(2,1)S(1)}, u32[]{:S(2)}, u32[]{:S(2)}) collective-permute-start(bf16[8,64,1536]{2,1,0:T(8,128)(2,1)S(1)} %all_to_all.15.mine), channel_id=1, source_target_pairs={{0,1},{1,0},{2,3},{3,2},{4,5},{5,4},{6,7},{7,6},{8,9},{9,8},{10,11... | collective-permute-start | bytes 4718600 | tf_op jit(solution)/shard_map/ppermute | solution.py:345
  47.9 0.0 copy-done.1
  47.9 0.0 copy-done.2
  47.9 0.0 copy-done.3
  47.9 0.6 shard_map.98
  48.5 2.8 %collective-permute-done.1.other = bf16[8,64,1536]{2,1,0:T(8,128)(2,1)S(1)} collective-permute-done((bf16[8,64,1536]{2,1,0:T(8,128)(2,1)S(1)}, bf16[8,64,1536]{2,1,0:T(8,128)(2,1)S(1)}, u32[]{:S(2)}, u32[]{:S(2)}) %collective-permute-start.1) | collective-permute-done | bytes 1572896 | tf_op jit(solution)/shard_map/ppermute | solution.py:345
  51.3 2.8 %shard_map.99 = bf16[16,272,128]{2,1,0:T(8,128)(2,1)S(1)} custom-call(bf16[8,64,1536]{2,1,0:T(8,128)(2,1)S(1)} %all_to_all.15.mine, bf16[8,64,1536]{2,1,0:T(8,128)(2,1)S(1)} %collective-permute-done.1.other, f32[1,512]{1,0:T(1,128)S(1)} %get-tuple-element.17.base_mean, f32[1,512]{1,0:T(1,128)S(1)} %get-tuple-element.18.weight_row, ...), custom_call_target="tpu_custom_call" | custom-call | flops 1610612736 | bytes 4194304 | tf_op jit(solution)/shard_map/pallas_call | solution.py:355
  54.1 0.0 copy-start.5
  54.1 20.8 %all_to_all.16.parts = bf16[16,272,128]{2,1,0:T(8,128)(2,1)S(1)} all-to-all(bf16[16,272,128]{2,1,0:T(8,128)(2,1)S(1)} %shard_map.99), channel_id=1, replica_groups=mesh['z'=16,'y_hi'=2,'y_lo'=2,'x'=4,'core'=2] {'y_hi','y_lo','x'}, dimensions={0} | all-to-all | bytes 2228224 | tf_op jit(solution)/shard_map/all_to_all | solution.py:370
  74.9 0.2 shard_map.100
  75.1 22.0 %all_to_all.17.parts = bf16[16,24,128]{2,1,0:T(8,128)(2,1)S(1)} all-to-all(bf16[16,24,128]{2,1,0:T(8,128)(2,1)S(1)} %shard_map.100), channel_id=1, replica_groups=mesh['z'=16,'y_hi'=2,'y_lo'=2,'x'=4,'core'=2] {'z'}, dimensions={0} | all-to-all | bytes 196608 | tf_op jit(solution)/shard_map/all_to_all | solution.py:372
  97.1 0.0 copy-done.5
  97.1 0.8 shard_map.101
Async XLA Ops:
  2.7 18.4 %collective-permute-start = (bf16[80,1024]{1,0:T(8,128)(2,1)}, bf16[80,1024]{1,0:T(8,128)(2,1)S(1)}, u32[]{:S(2)}, u32[]{:S(2)}) collective-permute-start(bf16[80,1024]{1,0:T(8,128)(2,1)} %shard_map.95), channel_id=1, source_target_pairs={{0,16},{16,32},{32,48},{48,64},{64,80},{80,96},{96,112},{112,128},... | collective-permute-start | bytes 491528 | tf_op jit(solution)/shard_map/ppermute | solution.py:316
  7.8 1.0 %copy-start = (bf16[64,4096]{1,0:T(8,128)(2,1)S(1)}, bf16[64,4096]{1,0:T(8,128)(2,1)}, u32[]{:S(2)}) copy-start(bf16[64,4096]{1,0:T(8,128)(2,1)} %anomalies.3) | copy-start | bytes 1572868
  8.8 0.7 copy-start.4
  9.5 0.9 copy-start.6
  10.4 0.7 copy-start.7
  21.5 26.4 %copy-start.1 = (f32[4096]{0:T(1024)S(1)}, f32[4096]{0:T(1024)}, u32[]{:S(2)}) copy-start(f32[4096]{0:T(1024)} %param.12) | copy-start | bytes 49156
  21.5 26.4 %copy-start.2 = (f32[4096]{0:T(1024)S(1)}, f32[4096]{0:T(1024)}, u32[]{:S(2)}) copy-start(f32[4096]{0:T(1024)} %param.13) | copy-start | bytes 49156
  21.5 26.4 %copy-start.3 = (s32[4096]{0:T(1024)S(1)}, s32[4096]{0:T(1024)}, u32[]{:S(2)}) copy-start(s32[4096]{0:T(1024)} %param.14) | copy-start | bytes 49156
  46.0 5.3 %collective-permute-start.1 = (bf16[8,64,1536]{2,1,0:T(8,128)(2,1)S(1)}, bf16[8,64,1536]{2,1,0:T(8,128)(2,1)S(1)}, u32[]{:S(2)}, u32[]{:S(2)}) collective-permute-start(bf16[8,64,1536]{2,1,0:T(8,128)(2,1)S(1)} %all_to_all.15.mine), channel_id=1, source_target_pairs={{0,1},{1,0},{2,3},{3,2},{4,5},{5,4},{6,7},{7,6},{8,9},{9,8},{10,11... | collective-permute-start | bytes 4718600 | tf_op jit(solution)/shard_map/ppermute | solution.py:345
  54.1 43.0 %copy-start.5 = (f32[64]{0:T(128)S(1)}, f32[64]{0:T(128)}, u32[]{:S(2)}) copy-start(f32[64]{0:T(128)} %param.11) | copy-start | bytes 772

commit v4 on v3

--- a/solution.py
+++ b/solution.py
@@ -80,28 +80,24 @@
     return jnp.concatenate([high, middle, low, zeros], axis=0)
 
 
-def sums_at_rows(first_line, lines, observed, obs_scale, at):
+def sums_at_rows(first_line, observed, obs_scale, at):
     square = obs_scale * obs_scale
-    value = square * observed
     high = at >> 7
     low = at & 127
     lanes = lax.broadcasted_iota(jnp.int32, (128, S), 0) == low
     lanes = jnp.where(lanes, 1.0, 0.0).astype(BF)
     line = lax.broadcasted_iota(jnp.int32, (8, S), 0)
-    blocks = (line + first_line == high) & (line < lines)
-    parts = []
-    for term in (square, value):
-        for part in three_parts(term):
-            parts.append(jnp.where(blocks, part.astype(F32), 0.0))
-    left = jnp.concatenate(parts, axis=0).astype(BF)
+    term = jnp.where(line < 4, square, square * observed)
+    term = jnp.where((line & 3) + first_line == high, term, 0.0)
+    left = jnp.concatenate([part.astype(F32) for part in three_parts(term)], axis=0).astype(BF)
     sums = lax.dot_general(left, lanes, NT, preferred_element_type=F32)
-    weight = sums[0:8] + sums[8:16] + sums[16:24]
-    value = sums[24:32] + sums[32:40] + sums[40:48]
-    return [weight[k : k + 1] for k in range(lines)], [value[k : k + 1] for k in range(lines)]
+    sums = sums[0:8] + sums[8:16] + sums[16:24]
+    rows = [jnp.concatenate([sums[k : k + 1] for k in range(at, at + 4)], axis=1) for at in (0, 4)]
+    return rows
 
 
 def edge_kernel(
-    anomalies, base, observed, obs_scale, obs_rows, edge,
+    anomalies, base, observed, obs_scale, obs_rows, edge, first,
     base_edge, observed_all, scale_all, rows_all, sems,
 ):
     border = pl.ds(S - EDGE, EDGE)
@@ -111,21 +107,23 @@
         pltpu.make_async_copy(observed, observed_all, sems.at[2]),
         pltpu.make_async_copy(base.at[:, border], base_edge, sems.at[3]),
         pltpu.make_async_copy(anomalies.at[:, border], edge.at[pl.ds(0, ROWS)], sems.at[4]),
+        pltpu.make_async_copy(anomalies.at[:, pl.ds(0, EDGE)], first, sems.at[5]),
     ]
     for copy in copies:
         copy.start()
     for copy in copies[:4]:
         copy.wait()
     weight, value = sums_at_rows(
-        S // 128 - 4, 4, observed_all[...], scale_all[...], rows_all[...] - spot()[0] * S
-    )
-    empty = [jnp.zeros((1, EDGE - REACH), F32)]
+        S // 128 - 4, observed_all[...], scale_all[...], rows_all[...] - spot()[0] * S
+    )
+    empty = jnp.zeros((1, EDGE - REACH), F32)
     extra = list(three_parts(base_edge[...]))
     for row in (weight, value):
-        extra += three_parts(jnp.concatenate(empty + row, axis=1))
+        extra += three_parts(jnp.concatenate([empty, row], axis=1))
     extra.append(jnp.zeros((7, EDGE), BF))
     edge[ROWS:] = jnp.concatenate(extra, axis=0)
     copies[4].wait()
+    copies[5].wait()
 
 
 def banded(rows, band, first, count):
@@ -175,19 +173,22 @@
     means[...] = jnp.zeros_like(means)
     for k in range(INNER):
         put_chunk(total, k, k + OUTER, out, means)
-    border[...] = rows[0 : OUTER * PITCH]
+    for k in range(OUTER):
+        border[k * 16 : k * 16 + 16] = rows[k * PITCH + ROWS : (k + 1) * PITCH]
     for copy in copies:
         copy.wait()
 
 
-def outer_kernel(edge, band, border, means_in, out_in, out, base_mean, rows, means):
+def outer_kernel(edge, first, band, border, means_in, out_in, out, base_mean, rows, means):
     state, column, _, _ = spot()
     whole = state > 0
     means[...] = means_in[...]
     for k in range(OUTER):
         at = k * PITCH
         rows[at : at + PITCH] = edge[:, k * CH : k * CH + CH]
-        rows[at + OUTER * PITCH : at + (OUTER + 1) * PITCH] = border[at : at + PITCH]
+        at = at + OUTER * PITCH
+        rows[at : at + ROWS] = first[:, k * CH : k * CH + CH]
+        rows[at + ROWS : at + PITCH] = border[k * 16 : k * 16 + 16]
     seen = jnp.where(whole, 1.0, 0.0).astype(BF)
     before = rows[2 * PITCH : 4 * PITCH]
     after = rows[4 * PITCH : 6 * PITCH]
@@ -206,14 +207,14 @@
 def weight_kernel(observed, obs_scale, obs_rows, edge, weight_row, value_row):
     state, column, _, _ = spot()
     weight, value = sums_at_rows(
-        (column - 1) * 4, 4, observed[...], obs_scale[...], obs_rows[...] - state * S
+        (column - 1) * 4, observed[...], obs_scale[...], obs_rows[...] - state * S
     )
     half = pl.ds(EDGE - REACH, REACH)
     row = lambda k: edge[ROWS : ROWS + 16, half][k : k + 1].astype(F32)
     mine = column > 0
-    for rows, target, at in ((weight, weight_row, 3), (value, value_row, 6)):
+    for own, target, at in ((weight, weight_row, 3), (value, value_row, 6)):
         sent = row(at) + row(at + 1) + row(at + 2)
-        target[...] = jnp.where(mine, jnp.concatenate(rows, axis=1), sent)
+        target[...] = jnp.where(mine, own, sent)
 
 
 def two_part_rows(value, count):
@@ -228,11 +229,13 @@
     out, transform, gathered, centred, scaled, part,
 ):
     core = lax.axis_index("core")
+    crossed = jnp.where(spot()[1] * COLS < EDGE, GROUP // 2, 0)
     for k in range(GROUP):
         for block, side in ((mine, core), (other, 1 - core)):
             at = pl.ds(pl.multiple_of(k * 128 + side * ROWS, ROWS), ROWS)
-            gathered[at] = block[k, :, 0:COLS]
             transform[at] = block[k, :, COLS:]
+            home = lax.rem(k + crossed, GROUP) * 128 + side * ROWS
+            gathered[pl.ds(pl.multiple_of(home, ROWS), ROWS)] = block[k, :, 0:COLS]
 
     own = [pl.ds(pl.multiple_of(k * 128 + core * ROWS, ROWS), ROWS) for k in range(GROUP)]
     for k in range(COLS // CH):
@@ -276,10 +279,10 @@
 
 def middle_kernel(parts, out):
     total = jnp.sum(parts[...].astype(F32), axis=0)
-    tail = two_part_rows(total[256:257, 0:ROWS] + total[256:257, ROWS:], 8)
+    tail = two_part_rows(total[256:257, 0:ROWS] + total[256:257, ROWS:], 16)
     for z in range(16):
         out[z, 0:16] = total[z * 16 : z * 16 + 16].astype(BF)
-        out[z, 16:24] = tail
+        out[z, 16:32] = tail
 
 
 def last_kernel(parts, weights, hessian, gradient):
@@ -299,28 +302,31 @@
     base = row(base_state)
     obs = (row(observed), row(obs_scale), row(obs_rows))
 
-    edge = call(
+    edge, first = call(
         edge_kernel,
-        shape(PITCH, EDGE),
+        (shape(PITCH, EDGE), shape(ROWS, EDGE)),
         [hbm()] * 5,
         scratch=[
             pltpu.VMEM((1, EDGE), F32),
             pltpu.VMEM((1, S), F32),
             pltpu.VMEM((1, S), F32),
             pltpu.VMEM((1, S), jnp.int32),
-            pltpu.SemaphoreType.DMA((5,)),
+            pltpu.SemaphoreType.DMA((6,)),
         ],
+        flops=4 * 10**9,
         nbytes=MIB,
         limit=FULL,
     )(anomalies, base, *obs)
-    edge = lax.ppermute(edge, ("z", "y_hi"), [(s, (s + 1) % 32) for s in range(32)])
+    onward = [(d, (d + 2) % 64 ^ 1) for d in range(64)]
+    edge = lax.ppermute(edge, ("z", "y_hi", "y_lo"), onward)
+    first = lax.ppermute(first, "y_lo", [(0, 1), (1, 0)])
 
     outgoing, band, border, means = call(
         inner_kernel,
         (
             shape(GROUP, ROWS, COLS + M),
             shape(TILES * CH, CH),
-            shape(OUTER * PITCH, CH),
+            shape(OUTER * 16, CH),
             shape32(1, S),
         ),
         [smem()] + [vmem()] * 2 + [hbm()],
@@ -334,12 +340,12 @@
     outgoing, base_mean = call(
         outer_kernel,
         (shape(GROUP, ROWS, COLS + M), shape32(1, COLS)),
-        [vmem()] * 5,
+        [vmem()] * 6,
         scratch=[pltpu.VMEM((2 * OUTER * PITCH, CH), BF), pltpu.VMEM((1, S), F32)],
         flops=2 * OUTER * PITCH * TILES * CH * CH,
         nbytes=MIB,
-        alias={4: 0},
-    )(edge, band, border, means, outgoing)
+        alias={5: 0},
+    )(edge, first, band, border, means, outgoing)
 
     mine = lax.all_to_all(outgoing, ("y_lo", "x"), 0, 0)
     other = lax.ppermute(mine, "core", [(0, 1), (1, 0)])
@@ -368,7 +374,7 @@
         limit=32,
     )(mine, other, base_mean, weight_row, value_row)
     parts = lax.all_to_all(parts, ("y_hi", "y_lo", "x"), 0, 0)
-    sums = call(middle_kernel, shape(16, 24, 128), [vmem()], nbytes=2**20)(parts)
+    sums = call(middle_kernel, shape(16, 32, 128), [vmem()], nbytes=2**20)(parts)
     sums = lax.all_to_all(sums, "z", 0, 0)
     hessian, gradient = call(
         last_kernel, (shape32(32, ROWS), shape32(1, ROWS)), [vmem()] * 2, nbytes=MIB // 4

time: 98.4 us -> 98.6 us (level)
  local copies, waits for them, and re-layouts: 3.34 us -> 0.04 us
  starting transfers between devices: 7.01 us -> 8.88 us
  waiting for transfers between devices: 10.2 us -> 11.5 us
    unnamed x16, local copies, waits for them, and re-layouts: 3.34 us -> 0.04 us
    ppermute x1 -> x2, starting transfers between devices: 5.1 us -> 6.97 us  [the longest x1 4.92 us: on_device(): edge = lax.ppermute(edge, ('z', 'y_hi', 'y_lo'), onward)]
    ppermute x1 -> x2, waiting for transfers between devices: 7.45 us -> 8.66 us  [the longest x1 6.25 us: on_device(): edge = lax.ppermute(edge, ('z', 'y_hi', 'y_lo'), onward)]
  transfers between devices with their start and end apart: 2 -> 3, of which waited for: 2 -> 3; matrix products, arithmetic and copies ran while one was open for 0% -> 0% of each run, Pallas kernels for 3% -> 3%
where the time goes in v4:
time: 98.6 us; the launch traced here: 98.3 us
  blocking collectives  67.7 us (69%)
  waiting for transfers between devices  11.5 us (12%)
  Pallas kernels  9.36 us (9%)
  starting transfers between devices  8.88 us (9%)
    all_to_all x1, blocking collectives, on_device(): mine = lax.all_to_all(outgoing, ('y_lo', 'x'), 0, 0)  24.4 us
    all_to_all x1, blocking collectives, on_device(): sums = lax.all_to_all(sums, 'z', 0, 0)  22.5 us
    all_to_all x1, blocking collectives, on_device(): parts = lax.all_to_all(parts, ('y_hi', 'y_lo', 'x'), 0, 0)  20.8 us
    ppermute x1, waiting for transfers between devices, on_device(): edge = lax.ppermute(edge, ('z', 'y_hi', 'y_lo'), onward)  6.25 us
    ppermute x1, starting transfers between devices, on_device(): edge = lax.ppermute(edge, ('z', 'y_hi', 'y_lo'), onward)  4.92 us
    pallas_call x1, Pallas kernels, on_device(): call(gram_kernel, shape(2 * GROUP, 272, 128), [vmem()] * 5, scratch=[pltp...  2.86 us
    ppermute x1, waiting for transfers between devices, on_device(): other = lax.ppermute(mine, 'core', [(0, 1), (1, 0)])  2.85 us
    pallas_call x1, Pallas kernels, on_device(): call(inner_kernel, (shape(GROUP, ROWS, COLS + M), shape(TILES * CH, CH),...  2.56 us
  transfers between devices with their start and end apart: 3, of which 3 were waited for; matrix products, arithmetic and copies ran while one was open for 0% of the time, Pallas kernels for 3%

profile of v4, /device:TPU:2, one launch (start us, length us, event | category | flops | bytes accessed | tf_op | source)
XLA Modules:
  0.0 98.3 jit_solution(6133451005461124985)
XLA Ops:
  0.6 0.0 copy-start.4
  0.6 0.0 copy-start.5
  0.7 0.0 copy-start.6
  0.7 0.0 copy-start.7
  0.7 2.1 %shard_map.95 = (bf16[80,1024]{1,0:T(8,128)(2,1)}, bf16[64,1024]{1,0:T(8,128)(2,1)}) custom-call(bf16[64,4096]{1,0:T(8,128)(2,1)} %anomalies.3, f32[1,4096]{1,0:T(1,128)} %bitcast.14, f32[1,4096]{1,0:T(1,128)} %bitcast.7, f32[1,4096]{1,0:T(1,128)} %bitcast.9, s32[1,4096]{1,0:T(1,128)} %bitcast.11), custom_call_target="tpu_custom_call" | custom-call | flops 4000000000 | bytes 1048576 | tf_op jit(solution)/shard_map/pallas_call | solution.py:305
  2.7 4.9 %collective-permute-start = (bf16[80,1024]{1,0:T(8,128)(2,1)}, bf16[80,1024]{1,0:T(8,128)(2,1)S(1)}, u32[]{:S(2)}, u32[]{:S(2)}) collective-permute-start(bf16[80,1024]{1,0:T(8,128)(2,1)} %get-tuple-element.14), channel_id=1, source_target_pairs={{0,24},{8,16},{16,40},{24,32},{32,56},{40,48},{48,72},{56,64},{64,... | collective-permute-start | bytes 491528 | tf_op jit(solution)/shard_map/ppermute | solution.py:321
  7.7 2.0 %collective-permute-start.1 = (bf16[64,1024]{1,0:T(8,128)(2,1)}, bf16[64,1024]{1,0:T(8,128)(2,1)S(1)}, u32[]{:S(2)}, u32[]{:S(2)}) collective-permute-start(bf16[64,1024]{1,0:T(8,128)(2,1)} %get-tuple-element.15), channel_id=1, source_target_pairs={{0,8},{8,0},{1,9},{9,1},{2,10},{10,2},{3,11},{11,3},{4,12},{12,4},... | collective-permute-start | bytes 393224 | tf_op jit(solution)/shard_map/ppermute | solution.py:322
  9.7 0.0 copy-done.4
  9.7 0.0 copy-done.5
  9.7 0.0 copy-done.6
  9.8 0.0 copy-done.7
  9.8 2.6 %shard_map.96 = (bf16[8,64,1536]{2,1,0:T(8,128)(2,1)S(1)}, bf16[1280,256]{1,0:T(8,128)(2,1)S(1)}, bf16[64,256]{1,0:T(8,128)(2,1)S(1)}, f32[1,4096]{1,0:T(1,128)S(1)}) custom-call(s32[8]{0:T(128)S(1)} %copy-done.7, bf16[64,4096]{1,0:T(8,128)(2,1)S(1)} %copy-done.4, f32[1,4096]{1,0:T(1,128)S(1)} %bitcast.15, bf16[64,1024]{1,0:T(8,128)(2,1)S(1)} %copy-done.5), custom_call_target="tpu_custom_call" | custom-call | flops 629145600 | bytes 4194304 | tf_op jit(solution)/shard_map/pallas_call | solution.py:324
  12.3 2.4 %collective-permute-done.1.first = bf16[64,1024]{1,0:T(8,128)(2,1)S(1)} collective-permute-done((bf16[64,1024]{1,0:T(8,128)(2,1)}, bf16[64,1024]{1,0:T(8,128)(2,1)S(1)}, u32[]{:S(2)}, u32[]{:S(2)}) %collective-permute-start.1) | collective-permute-done | bytes 131104 | tf_op jit(solution)/shard_map/ppermute | solution.py:322
  14.7 6.3 %collective-permute-done.edge = bf16[80,1024]{1,0:T(8,128)(2,1)S(1)} collective-permute-done((bf16[80,1024]{1,0:T(8,128)(2,1)}, bf16[80,1024]{1,0:T(8,128)(2,1)S(1)}, u32[]{:S(2)}, u32[]{:S(2)}) %collective-permute-start) | collective-permute-done | bytes 163872 | tf_op jit(solution)/shard_map/ppermute | solution.py:321
  21.0 0.4 shard_map.97
  21.4 0.0 copy-start
  21.4 0.0 copy-start.1
  21.4 0.0 copy-start.2
  21.4 24.4 %all_to_all.15.mine = bf16[8,64,1536]{2,1,0:T(8,128)(2,1)S(1)} all-to-all(bf16[8,64,1536]{2,1,0:T(8,128)(2,1)S(1)} %get-tuple-element.20), channel_id=1, replica_groups=mesh['z'=16,'y_hi'=2,'y_lo'=2,'x'=4,'core'=2] {'y_lo','x'}, dimensions={0} | all-to-all | bytes 3145728 | tf_op jit(solution)/shard_map/all_to_all | solution.py:350
  45.8 1.9 %collective-permute-start.2 = (bf16[8,64,1536]{2,1,0:T(8,128)(2,1)S(1)}, bf16[8,64,1536]{2,1,0:T(8,128)(2,1)S(1)}, u32[]{:S(2)}, u32[]{:S(2)}) collective-permute-start(bf16[8,64,1536]{2,1,0:T(8,128)(2,1)S(1)} %all_to_all.15.mine), channel_id=1, source_target_pairs={{0,1},{1,0},{2,3},{3,2},{4,5},{5,4},{6,7},{7,6},{8,9},{9,8},{10,11... | collective-permute-start | bytes 4718600 | tf_op jit(solution)/shard_map/ppermute | solution.py:351
  47.7 0.0 copy-done
  47.7 0.0 copy-done.1
  47.7 0.0 copy-done.2
  47.7 0.5 shard_map.98
  48.2 2.9 %collective-permute-done.2.other = bf16[8,64,1536]{2,1,0:T(8,128)(2,1)S(1)} collective-permute-done((bf16[8,64,1536]{2,1,0:T(8,128)(2,1)S(1)}, bf16[8,64,1536]{2,1,0:T(8,128)(2,1)S(1)}, u32[]{:S(2)}, u32[]{:S(2)}) %collective-permute-start.2) | collective-permute-done | bytes 1572896 | tf_op jit(solution)/shard_map/ppermute | solution.py:351
  51.1 2.9 %shard_map.99 = bf16[16,272,128]{2,1,0:T(8,128)(2,1)S(1)} custom-call(bf16[8,64,1536]{2,1,0:T(8,128)(2,1)S(1)} %all_to_all.15.mine, bf16[8,64,1536]{2,1,0:T(8,128)(2,1)S(1)} %collective-permute-done.2.other, f32[1,512]{1,0:T(1,128)S(1)} %get-tuple-element.21.base_mean, f32[1,512]{1,0:T(1,128)S(1)} %get-tuple-element.22.weight_row, ...), custom_call_target="tpu_custom_call" | custom-call | flops 1610612736 | bytes 4194304 | tf_op jit(solution)/shard_map/pallas_call | solution.py:361
  53.9 0.0 copy-start.3
  54.0 20.8 %all_to_all.16.parts = bf16[16,272,128]{2,1,0:T(8,128)(2,1)S(1)} all-to-all(bf16[16,272,128]{2,1,0:T(8,128)(2,1)S(1)} %shard_map.99), channel_id=1, replica_groups=mesh['z'=16,'y_hi'=2,'y_lo'=2,'x'=4,'core'=2] {'y_hi','y_lo','x'}, dimensions={0} | all-to-all | bytes 2228224 | tf_op jit(solution)/shard_map/all_to_all | solution.py:376
  74.8 0.2 shard_map.100
  75.0 22.5 %all_to_all.17.parts = bf16[16,32,128]{2,1,0:T(8,128)(2,1)S(1)} all-to-all(bf16[16,32,128]{2,1,0:T(8,128)(2,1)S(1)} %shard_map.100), channel_id=1, replica_groups=mesh['z'=16,'y_hi'=2,'y_lo'=2,'x'=4,'core'=2] {'z'}, dimensions={0} | all-to-all | bytes 262144 | tf_op jit(solution)/shard_map/all_to_all | solution.py:378
  97.5 0.0 copy-done.3
  97.5 0.8 shard_map.101
Async XLA Ops:
  0.6 9.1 %copy-start.4 = (bf16[64,4096]{1,0:T(8,128)(2,1)S(1)}, bf16[64,4096]{1,0:T(8,128)(2,1)}, u32[]{:S(2)}) copy-start(bf16[64,4096]{1,0:T(8,128)(2,1)} %anomalies.3) | copy-start | bytes 1572868
  0.6 9.1 %copy-start.5 = (bf16[64,1024]{1,0:T(8,128)(2,1)S(1)}, bf16[64,1024]{1,0:T(8,128)(2,1)}, u32[]{:S(2)}) copy-start(bf16[64,1024]{1,0:T(8,128)(2,1)} %transform.1) | copy-start | bytes 393220
  0.7 9.1 %copy-start.6 = (f32[4096]{0:T(1024)S(1)}, f32[4096]{0:T(1024)}, u32[]{:S(2)}) copy-start(f32[4096]{0:T(1024)} %param.8) | copy-start | bytes 49156
  0.7 9.1 %copy-start.7 = (s32[8]{0:T(128)S(1)}, s32[8]{0:T(128)}, u32[]{:S(2)}) copy-start(s32[8]{0:T(128)} %offsets.1) | copy-start | bytes 100
  2.7 18.3 %collective-permute-start = (bf16[80,1024]{1,0:T(8,128)(2,1)}, bf16[80,1024]{1,0:T(8,128)(2,1)S(1)}, u32[]{:S(2)}, u32[]{:S(2)}) collective-permute-start(bf16[80,1024]{1,0:T(8,128)(2,1)} %get-tuple-element.14), channel_id=1, source_target_pairs={{0,24},{8,16},{16,40},{24,32},{32,56},{40,48},{48,72},{56,64},{64,... | collective-permute-start | bytes 491528 | tf_op jit(solution)/shard_map/ppermute | solution.py:321
  7.7 7.1 %collective-permute-start.1 = (bf16[64,1024]{1,0:T(8,128)(2,1)}, bf16[64,1024]{1,0:T(8,128)(2,1)S(1)}, u32[]{:S(2)}, u32[]{:S(2)}) collective-permute-start(bf16[64,1024]{1,0:T(8,128)(2,1)} %get-tuple-element.15), channel_id=1, source_target_pairs={{0,8},{8,0},{1,9},{9,1},{2,10},{10,2},{3,11},{11,3},{4,12},{12,4},... | collective-permute-start | bytes 393224 | tf_op jit(solution)/shard_map/ppermute | solution.py:322
  21.4 26.3 %copy-start = (f32[4096]{0:T(1024)S(1)}, f32[4096]{0:T(1024)}, u32[]{:S(2)}) copy-start(f32[4096]{0:T(1024)} %param.12) | copy-start | bytes 49156
  21.4 26.3 %copy-start.1 = (f32[4096]{0:T(1024)S(1)}, f32[4096]{0:T(1024)}, u32[]{:S(2)}) copy-start(f32[4096]{0:T(1024)} %param.13) | copy-start | bytes 49156
  21.4 26.3 %copy-start.2 = (s32[4096]{0:T(1024)S(1)}, s32[4096]{0:T(1024)}, u32[]{:S(2)}) copy-start(s32[4096]{0:T(1024)} %param.14) | copy-start | bytes 49156
  45.8 5.3 %collective-permute-start.2 = (bf16[8,64,1536]{2,1,0:T(8,128)(2,1)S(1)}, bf16[8,64,1536]{2,1,0:T(8,128)(2,1)S(1)}, u32[]{:S(2)}, u32[]{:S(2)}) collective-permute-start(bf16[8,64,1536]{2,1,0:T(8,128)(2,1)S(1)} %all_to_all.15.mine), channel_id=1, source_target_pairs={{0,1},{1,0},{2,3},{3,2},{4,5},{5,4},{6,7},{7,6},{8,9},{9,8},{10,11... | collective-permute-start | bytes 4718600 | tf_op jit(solution)/shard_map/ppermute | solution.py:351
  53.9 43.6 %copy-start.3 = (f32[64]{0:T(128)S(1)}, f32[64]{0:T(128)}, u32[]{:S(2)}) copy-start(f32[64]{0:T(128)} %param.11) | copy-start | bytes 772

commit v5 on v4

--- a/solution.py
+++ b/solution.py
@@ -27,12 +27,15 @@
 FULL = 63
 
 
-def call(kernel, out_shape, in_specs, scratch=(), flops=0, nbytes=0, limit=16, alias=None):
+def call(
+    kernel, out_shape, in_specs, scratch=(), flops=0, nbytes=0, limit=16, alias=None, out_specs=None
+):
     return pl.pallas_call(
         kernel,
         out_shape=out_shape,
         in_specs=in_specs,
-        out_specs=jax.tree.map(lambda _: pl.BlockSpec(memory_space=pltpu.VMEM), out_shape),
+        out_specs=out_specs
+        or jax.tree.map(lambda _: pl.BlockSpec(memory_space=pltpu.VMEM), out_shape),
         scratch_shapes=list(scratch),
         compiler_params=pltpu.CompilerParams(vmem_limit_bytes=limit * MIB),
         input_output_aliases=alias or {},
@@ -179,7 +182,9 @@
         copy.wait()
 
 
-def outer_kernel(edge, first, band, border, means_in, out_in, out, base_mean, rows, means):
+def outer_kernel(
+    edge, first, band, border, means_in, out_in, out, base_mean, rows, means, chunks, sems
+):
     state, column, _, _ = spot()
     whole = state > 0
     means[...] = means_in[...]
@@ -195,12 +200,20 @@
     rows[4 * PITCH : 6 * PITCH] = after * seen
     total = banded(rows, band, 0, 2)
     for k in range(2):
-        put_chunk(total, k, k, out, means)
+        put_chunk(total, k, k, chunks, means)
     rows[4 * PITCH : 6 * PITCH] = after
     rows[2 * PITCH : 4 * PITCH] = before * seen
     total = banded(rows, band, 2, 2)
     for k in range(2):
-        put_chunk(total, k, k + 2, out, means)
+        put_chunk(total, k, k + 2, chunks, means)
+    copies = [
+        pltpu.make_async_copy(chunks.at[k], out.at[k, :, pl.ds(0, COLS)], sems.at[k])
+        for k in range(2)
+    ]
+    for copy in copies:
+        copy.start()
+    for copy in copies:
+        copy.wait()
     base_mean[...] = means[:, pl.ds(pl.multiple_of(column * COLS, COLS), COLS)]
 
 
@@ -337,14 +350,21 @@
         flops=2 * INNER * PITCH * TILES * CH * CH,
         nbytes=4 * MIB,
     )(offsets, anomalies, base, transform)
+    anywhere = pl.BlockSpec(memory_space=pl.ANY)
     outgoing, base_mean = call(
         outer_kernel,
         (shape(GROUP, ROWS, COLS + M), shape32(1, COLS)),
-        [vmem()] * 6,
-        scratch=[pltpu.VMEM((2 * OUTER * PITCH, CH), BF), pltpu.VMEM((1, S), F32)],
+        [vmem()] * 5 + [anywhere],
+        scratch=[
+            pltpu.VMEM((2 * OUTER * PITCH, CH), BF),
+            pltpu.VMEM((1, S), F32),
+            pltpu.VMEM((2, ROWS, COLS), BF),
+            pltpu.SemaphoreType.DMA((2,)),
+        ],
         flops=2 * OUTER * PITCH * TILES * CH * CH,
         nbytes=MIB,
         alias={5: 0},
+        out_specs=(anywhere, vmem()),
     )(edge, first, band, border, means, outgoing)
 
     mine = lax.all_to_all(outgoing, ("y_lo", "x"), 0, 0)

time: 98.6 us -> 98.7 us (level)
  no operation moved by 1% of the time
where the time goes in v5:
time: 98.7 us; the launch traced here: 98.3 us
  blocking collectives  67.7 us (69%)
  waiting for transfers between devices  11.5 us (12%)
  Pallas kernels  9.4 us (10%)
  starting transfers between devices  8.88 us (9%)
    all_to_all x1, blocking collectives, on_device(): mine = lax.all_to_all(outgoing, ('y_lo', 'x'), 0, 0)  24.4 us
    all_to_all x1, blocking collectives, on_device(): sums = lax.all_to_all(sums, 'z', 0, 0)  22.5 us
    all_to_all x1, blocking collectives, on_device(): parts = lax.all_to_all(parts, ('y_hi', 'y_lo', 'x'), 0, 0)  20.8 us
    ppermute x1, waiting for transfers between devices, on_device(): edge = lax.ppermute(edge, ('z', 'y_hi', 'y_lo'), onward)  6.25 us
    ppermute x1, starting transfers between devices, on_device(): edge = lax.ppermute(edge, ('z', 'y_hi', 'y_lo'), onward)  4.92 us
    pallas_call x1, Pallas kernels, on_device(): call(gram_kernel, shape(2 * GROUP, 272, 128), [vmem()] * 5, scratch=[pltp...  2.87 us
    ppermute x1, waiting for transfers between devices, on_device(): other = lax.ppermute(mine, 'core', [(0, 1), (1, 0)])  2.85 us
    pallas_call x1, Pallas kernels, on_device(): call(inner_kernel, (shape(GROUP, ROWS, COLS + M), shape(TILES * CH, CH),...  2.56 us
  transfers between devices with their start and end apart: 3, of which 3 were waited for; matrix products, arithmetic and copies ran while one was open for 0% of the time, Pallas kernels for 3%

profile of v5, /device:TPU:2, one launch (start us, length us, event | category | flops | bytes accessed | tf_op | source)
XLA Modules:
  0.0 98.3 jit_solution(13732768609485210704)
XLA Ops:
  0.6 0.0 copy-start.4
  0.6 0.0 copy-start.5
  0.7 0.0 copy-start.6
  0.7 0.0 copy-start.7
  0.7 2.1 %shard_map.95 = (bf16[80,1024]{1,0:T(8,128)(2,1)}, bf16[64,1024]{1,0:T(8,128)(2,1)}) custom-call(bf16[64,4096]{1,0:T(8,128)(2,1)} %anomalies.3, f32[1,4096]{1,0:T(1,128)} %bitcast.14, f32[1,4096]{1,0:T(1,128)} %bitcast.7, f32[1,4096]{1,0:T(1,128)} %bitcast.9, s32[1,4096]{1,0:T(1,128)} %bitcast.11), custom_call_target="tpu_custom_call" | custom-call | flops 4000000000 | bytes 1048576 | tf_op jit(solution)/shard_map/pallas_call | solution.py:318
  2.7 4.9 %collective-permute-start = (bf16[80,1024]{1,0:T(8,128)(2,1)}, bf16[80,1024]{1,0:T(8,128)(2,1)S(1)}, u32[]{:S(2)}, u32[]{:S(2)}) collective-permute-start(bf16[80,1024]{1,0:T(8,128)(2,1)} %get-tuple-element.14), channel_id=1, source_target_pairs={{0,24},{8,16},{16,40},{24,32},{32,56},{40,48},{48,72},{56,64},{64,... | collective-permute-start | bytes 491528 | tf_op jit(solution)/shard_map/ppermute | solution.py:334
  7.7 2.0 %collective-permute-start.1 = (bf16[64,1024]{1,0:T(8,128)(2,1)}, bf16[64,1024]{1,0:T(8,128)(2,1)S(1)}, u32[]{:S(2)}, u32[]{:S(2)}) collective-permute-start(bf16[64,1024]{1,0:T(8,128)(2,1)} %get-tuple-element.15), channel_id=1, source_target_pairs={{0,8},{8,0},{1,9},{9,1},{2,10},{10,2},{3,11},{11,3},{4,12},{12,4},... | collective-permute-start | bytes 393224 | tf_op jit(solution)/shard_map/ppermute | solution.py:335
  9.7 0.0 copy-done.4
  9.7 0.0 copy-done.5
  9.7 0.0 copy-done.6
  9.8 0.0 copy-done.7
  9.8 2.6 %shard_map.96 = (bf16[8,64,1536]{2,1,0:T(8,128)(2,1)S(1)}, bf16[1280,256]{1,0:T(8,128)(2,1)S(1)}, bf16[64,256]{1,0:T(8,128)(2,1)S(1)}, f32[1,4096]{1,0:T(1,128)S(1)}) custom-call(s32[8]{0:T(128)S(1)} %copy-done.7, bf16[64,4096]{1,0:T(8,128)(2,1)S(1)} %copy-done.4, f32[1,4096]{1,0:T(1,128)S(1)} %bitcast.15, bf16[64,1024]{1,0:T(8,128)(2,1)S(1)} %copy-done.5), custom_call_target="tpu_custom_call" | custom-call | flops 629145600 | bytes 4194304 | tf_op jit(solution)/shard_map/pallas_call | solution.py:337
  12.3 2.4 %collective-permute-done.1.first = bf16[64,1024]{1,0:T(8,128)(2,1)S(1)} collective-permute-done((bf16[64,1024]{1,0:T(8,128)(2,1)}, bf16[64,1024]{1,0:T(8,128)(2,1)S(1)}, u32[]{:S(2)}, u32[]{:S(2)}) %collective-permute-start.1) | collective-permute-done | bytes 131104 | tf_op jit(solution)/shard_map/ppermute | solution.py:335
  14.7 6.3 %collective-permute-done.edge = bf16[80,1024]{1,0:T(8,128)(2,1)S(1)} collective-permute-done((bf16[80,1024]{1,0:T(8,128)(2,1)}, bf16[80,1024]{1,0:T(8,128)(2,1)S(1)}, u32[]{:S(2)}, u32[]{:S(2)}) %collective-permute-start) | collective-permute-done | bytes 163872 | tf_op jit(solution)/shard_map/ppermute | solution.py:334
  21.0 0.4 shard_map.97
  21.4 0.0 copy-start
  21.4 0.0 copy-start.1
  21.5 0.0 copy-start.2
  21.5 24.4 %all_to_all.15.mine = bf16[8,64,1536]{2,1,0:T(8,128)(2,1)S(1)} all-to-all(bf16[8,64,1536]{2,1,0:T(8,128)(2,1)S(1)} %get-tuple-element.20), channel_id=1, replica_groups=mesh['z'=16,'y_hi'=2,'y_lo'=2,'x'=4,'core'=2] {'y_lo','x'}, dimensions={0} | all-to-all | bytes 3145728 | tf_op jit(solution)/shard_map/all_to_all | solution.py:370
  45.8 1.9 %collective-permute-start.2 = (bf16[8,64,1536]{2,1,0:T(8,128)(2,1)S(1)}, bf16[8,64,1536]{2,1,0:T(8,128)(2,1)S(1)}, u32[]{:S(2)}, u32[]{:S(2)}) collective-permute-start(bf16[8,64,1536]{2,1,0:T(8,128)(2,1)S(1)} %all_to_all.15.mine), channel_id=1, source_target_pairs={{0,1},{1,0},{2,3},{3,2},{4,5},{5,4},{6,7},{7,6},{8,9},{9,8},{10,11... | collective-permute-start | bytes 4718600 | tf_op jit(solution)/shard_map/ppermute | solution.py:371
  47.7 0.0 copy-done
  47.8 0.0 copy-done.1
  47.8 0.0 copy-done.2
  47.8 0.5 shard_map.98
  48.3 2.9 %collective-permute-done.2.other = bf16[8,64,1536]{2,1,0:T(8,128)(2,1)S(1)} collective-permute-done((bf16[8,64,1536]{2,1,0:T(8,128)(2,1)S(1)}, bf16[8,64,1536]{2,1,0:T(8,128)(2,1)S(1)}, u32[]{:S(2)}, u32[]{:S(2)}) %collective-permute-start.2) | collective-permute-done | bytes 1572896 | tf_op jit(solution)/shard_map/ppermute | solution.py:371
  51.1 2.9 %shard_map.99 = bf16[16,272,128]{2,1,0:T(8,128)(2,1)S(1)} custom-call(bf16[8,64,1536]{2,1,0:T(8,128)(2,1)S(1)} %all_to_all.15.mine, bf16[8,64,1536]{2,1,0:T(8,128)(2,1)S(1)} %collective-permute-done.2.other, f32[1,512]{1,0:T(1,128)S(1)} %get-tuple-element.21.base_mean, f32[1,512]{1,0:T(1,128)S(1)} %get-tuple-element.22.weight_row, ...), custom_call_target="tpu_custom_call" | custom-call | flops 1610612736 | bytes 4194304 | tf_op jit(solution)/shard_map/pallas_call | solution.py:381
  54.0 0.0 copy-start.3
  54.0 20.8 %all_to_all.16.parts = bf16[16,272,128]{2,1,0:T(8,128)(2,1)S(1)} all-to-all(bf16[16,272,128]{2,1,0:T(8,128)(2,1)S(1)} %shard_map.99), channel_id=1, replica_groups=mesh['z'=16,'y_hi'=2,'y_lo'=2,'x'=4,'core'=2] {'y_hi','y_lo','x'}, dimensions={0} | all-to-all | bytes 2228224 | tf_op jit(solution)/shard_map/all_to_all | solution.py:396
  74.8 0.2 shard_map.100
  75.0 22.5 %all_to_all.17.parts = bf16[16,32,128]{2,1,0:T(8,128)(2,1)S(1)} all-to-all(bf16[16,32,128]{2,1,0:T(8,128)(2,1)S(1)} %shard_map.100), channel_id=1, replica_groups=mesh['z'=16,'y_hi'=2,'y_lo'=2,'x'=4,'core'=2] {'z'}, dimensions={0} | all-to-all | bytes 262144 | tf_op jit(solution)/shard_map/all_to_all | solution.py:398
  97.5 0.0 copy-done.3
  97.6 0.8 shard_map.101
Async XLA Ops:
  0.6 9.1 %copy-start.4 = (bf16[64,4096]{1,0:T(8,128)(2,1)S(1)}, bf16[64,4096]{1,0:T(8,128)(2,1)}, u32[]{:S(2)}) copy-start(bf16[64,4096]{1,0:T(8,128)(2,1)} %anomalies.3) | copy-start | bytes 1572868
  0.6 9.1 %copy-start.5 = (bf16[64,1024]{1,0:T(8,128)(2,1)S(1)}, bf16[64,1024]{1,0:T(8,128)(2,1)}, u32[]{:S(2)}) copy-start(bf16[64,1024]{1,0:T(8,128)(2,1)} %transform.1) | copy-start | bytes 393220
  0.7 9.1 %copy-start.6 = (f32[4096]{0:T(1024)S(1)}, f32[4096]{0:T(1024)}, u32[]{:S(2)}) copy-start(f32[4096]{0:T(1024)} %param.8) | copy-start | bytes 49156
  0.7 9.1 %copy-start.7 = (s32[8]{0:T(128)S(1)}, s32[8]{0:T(128)}, u32[]{:S(2)}) copy-start(s32[8]{0:T(128)} %offsets.1) | copy-start | bytes 100
  2.7 18.3 %collective-permute-start = (bf16[80,1024]{1,0:T(8,128)(2,1)}, bf16[80,1024]{1,0:T(8,128)(2,1)S(1)}, u32[]{:S(2)}, u32[]{:S(2)}) collective-permute-start(bf16[80,1024]{1,0:T(8,128)(2,1)} %get-tuple-element.14), channel_id=1, source_target_pairs={{0,24},{8,16},{16,40},{24,32},{32,56},{40,48},{48,72},{56,64},{64,... | collective-permute-start | bytes 491528 | tf_op jit(solution)/shard_map/ppermute | solution.py:334
  7.7 7.1 %collective-permute-start.1 = (bf16[64,1024]{1,0:T(8,128)(2,1)}, bf16[64,1024]{1,0:T(8,128)(2,1)S(1)}, u32[]{:S(2)}, u32[]{:S(2)}) collective-permute-start(bf16[64,1024]{1,0:T(8,128)(2,1)} %get-tuple-element.15), channel_id=1, source_target_pairs={{0,8},{8,0},{1,9},{9,1},{2,10},{10,2},{3,11},{11,3},{4,12},{12,4},... | collective-permute-start | bytes 393224 | tf_op jit(solution)/shard_map/ppermute | solution.py:335
  21.4 26.3 %copy-start = (f32[4096]{0:T(1024)S(1)}, f32[4096]{0:T(1024)}, u32[]{:S(2)}) copy-start(f32[4096]{0:T(1024)} %param.12) | copy-start | bytes 49156
  21.4 26.3 %copy-start.1 = (f32[4096]{0:T(1024)S(1)}, f32[4096]{0:T(1024)}, u32[]{:S(2)}) copy-start(f32[4096]{0:T(1024)} %param.13) | copy-start | bytes 49156
  21.5 26.3 %copy-start.2 = (s32[4096]{0:T(1024)S(1)}, s32[4096]{0:T(1024)}, u32[]{:S(2)}) copy-start(s32[4096]{0:T(1024)} %param.14) | copy-start | bytes 49156
  45.8 5.3 %collective-permute-start.2 = (bf16[8,64,1536]{2,1,0:T(8,128)(2,1)S(1)}, bf16[8,64,1536]{2,1,0:T(8,128)(2,1)S(1)}, u32[]{:S(2)}, u32[]{:S(2)}) collective-permute-start(bf16[8,64,1536]{2,1,0:T(8,128)(2,1)S(1)} %all_to_all.15.mine), channel_id=1, source_target_pairs={{0,1},{1,0},{2,3},{3,2},{4,5},{5,4},{6,7},{7,6},{8,9},{9,8},{10,11... | collective-permute-start | bytes 4718600 | tf_op jit(solution)/shard_map/ppermute | solution.py:371
  54.0 43.6 %copy-start.3 = (f32[64]{0:T(128)S(1)}, f32[64]{0:T(128)}, u32[]{:S(2)}) copy-start(f32[64]{0:T(128)} %param.11) | copy-start | bytes 772

commit v6 on v5

--- a/solution.py
+++ b/solution.py
@@ -237,6 +237,44 @@
     return jnp.concatenate([row, jnp.zeros((count - 1, 128), F32)], axis=0).astype(BF)
 
 
+def seated_lanes(y_hi):
+    lane = lax.broadcasted_iota(jnp.int32, (16, 128), 1)
+    return (lane >= 16 + 32 * y_hi) & (lane < 24 + 32 * y_hi)
+
+
+def seated(slopes):
+    lane = lax.broadcasted_iota(jnp.int32, (16, 128), 1)
+    mine = ((lane & (ROWS - 1)) >> 2) == lax.broadcasted_iota(jnp.int32, (16, 128), 0)
+    high = slopes.astype(BF).astype(F32)
+    low = slopes - high
+    spread = []
+    for j in range(GROUP):
+        c = slice(j * ROWS, j * ROWS + ROWS)
+        row = jnp.concatenate([high[:, c], low[:, c]], axis=1)
+        spread.append(jnp.where(mine, row, 0.0))
+    source = lax.broadcasted_iota(jnp.int32, (128, 128), 0)
+    target = 16 + (source & 3) + jnp.where(source >= ROWS, 4, 0)
+    pick = lax.broadcasted_iota(jnp.int32, (128, 128), 1) == target
+    pick = jnp.where(pick, 1.0, 0.0).astype(BF)
+    return jnp.dot(
+        jnp.concatenate(spread, axis=0).astype(BF), pick, preferred_element_type=F32
+    )
+
+
+def unseat(tile, y_hi):
+    tile = jnp.where(y_hi == 0, tile, pltpu.roll(tile, 96, 1))
+    lane = lax.broadcasted_iota(jnp.int32, (16, ROWS), 1)
+    row = lax.broadcasted_iota(jnp.int32, (16, ROWS), 0)
+    sums = jnp.zeros((16, ROWS), F32)
+    for q in range(4):
+        part = tile[:, 16 + q : 17 + q] + tile[:, 20 + q : 21 + q]
+        sums = sums + jnp.where((lane >> 2 == row) & (lane & 3 == q), part, 0.0)
+    tall = jnp.concatenate([tile, jnp.zeros((112, 128), F32)], axis=0).T
+    tile = jnp.where(seated_lanes(0), pltpu.roll(tall[64:80], 16, 1), tile)
+    tile = jnp.where(y_hi == 0, tile, pltpu.roll(tile, 32, 1))
+    return jnp.sum(sums, axis=0, keepdims=True), tile
+
+
 def gram_kernel(
     mine, other, base_mean, weight_row, value_row,
     out, transform, gathered, centred, scaled, part,
@@ -272,10 +310,11 @@
     rows = jnp.concatenate([scaled[own[j]] for j in range(GROUP)], axis=0)
     slopes = jnp.sum(part[...].T, axis=0, keepdims=True)
     left_half = lax.broadcasted_iota(jnp.int32, (16, 128), 1) < ROWS
+    seats = seated(slopes)
     gram = lax.dot_general(scaled[...], rows, NT, preferred_element_type=F32)
     for j in range(GROUP):
         lanes = slice(j // 2 * 128, j // 2 * 128 + 128)
-        tail = two_part_rows(slopes[:, j * ROWS : j * ROWS + ROWS], 16)
+        seat = seats[j * 16 : j * 16 + 16]
         for y_hi in range(2):
             target = out.at[y_hi * GROUP + j]
             for z in range(16):
@@ -286,13 +325,19 @@
                     packed = jnp.where(left_half, top, pltpu.roll(bottom, ROWS, 1))
                 else:
                     packed = jnp.where(left_half, pltpu.roll(top, ROWS, 1), bottom)
+                if z // 2 == j:
+                    taken = seated_lanes(y_hi) & (core == z % 2)
+                    packed = jnp.where(taken, pltpu.roll(seat, 32, 1) if y_hi else seat, packed)
                 target[z * 16 : z * 16 + 16] = packed.astype(BF)
-            target[256:272] = tail
-
-
-def middle_kernel(parts, out):
-    total = jnp.sum(parts[...].astype(F32), axis=0)
-    tail = two_part_rows(total[256:257, 0:ROWS] + total[256:257, ROWS:], 16)
+
+
+def middle_kernel(parts, out, total):
+    total[...] = jnp.sum(parts[...].astype(F32), axis=0)
+    block = spot()[2] // ROWS
+    at = pl.ds(pl.multiple_of(block * 16, 16), 16)
+    slopes, tile = unseat(total[at], lax.axis_index("y_hi"))
+    total[at] = tile
+    tail = two_part_rows(slopes, 16)
     for z in range(16):
         out[z, 0:16] = total[z * 16 : z * 16 + 16].astype(BF)
         out[z, 16:32] = tail
@@ -380,7 +425,7 @@
 
     parts = call(
         gram_kernel,
-        shape(2 * GROUP, 272, 128),
+        shape(2 * GROUP, 256, 128),
         [vmem()] * 5,
         scratch=[
             pltpu.VMEM((M, M), BF),
@@ -394,7 +439,13 @@
         limit=32,
     )(mine, other, base_mean, weight_row, value_row)
     parts = lax.all_to_all(parts, ("y_hi", "y_lo", "x"), 0, 0)
-    sums = call(middle_kernel, shape(16, 32, 128), [vmem()], nbytes=2**20)(parts)
+    sums = call(
+        middle_kernel,
+        shape(16, 32, 128),
+        [vmem()],
+        scratch=[pltpu.VMEM((256, 128), F32)],
+        nbytes=MIB,
+    )(parts)
     sums = lax.all_to_all(sums, "z", 0, 0)
     hessian, gradient = call(
         last_kernel, (shape32(32, ROWS), shape32(1, ROWS)), [vmem()] * 2, nbytes=MIB // 4

time: 98.7 us -> 98.5 us (level)
  no operation moved by 1% of the time
where the time goes in v6:
time: 98.5 us; the launch traced here: 98.1 us
  blocking collectives  66.9 us (68%)
  waiting for transfers between devices  11.5 us (12%)
  Pallas kernels  9.97 us (10%)
  starting transfers between devices  8.88 us (9%)
    all_to_all x1, blocking collectives, on_device(): mine = lax.all_to_all(outgoing, ('y_lo', 'x'), 0, 0)  24.4 us
    all_to_all x1, blocking collectives, on_device(): sums = lax.all_to_all(sums, 'z', 0, 0)  22.4 us
    all_to_all x1, blocking collectives, on_device(): parts = lax.all_to_all(parts, ('y_hi', 'y_lo', 'x'), 0, 0)  20.1 us
    ppermute x1, waiting for transfers between devices, on_device(): edge = lax.ppermute(edge, ('z', 'y_hi', 'y_lo'), onward)  6.25 us
    ppermute x1, starting transfers between devices, on_device(): edge = lax.ppermute(edge, ('z', 'y_hi', 'y_lo'), onward)  4.92 us
    pallas_call x1, Pallas kernels, on_device(): call(gram_kernel, shape(2 * GROUP, 256, 128), [vmem()] * 5, scratch=[pltp...  3.16 us
    ppermute x1, waiting for transfers between devices, on_device(): other = lax.ppermute(mine, 'core', [(0, 1), (1, 0)])  2.85 us
    pallas_call x1, Pallas kernels, on_device(): call(inner_kernel, (shape(GROUP, ROWS, COLS + M), shape(TILES * CH, CH),...  2.56 us
  transfers between devices with their start and end apart: 3, of which 3 were waited for; matrix products, arithmetic and copies ran while one was open for 0% of the time, Pallas kernels for 3%

profile of v6, /device:TPU:2, one launch (start us, length us, event | category | flops | bytes accessed | tf_op | source)
XLA Modules:
  0.0 98.1 jit_solution(10067318526240210878)
XLA Ops:
  0.6 0.0 copy-start.4
  0.6 0.0 copy-start.5
  0.7 0.0 copy-start.6
  0.7 0.0 copy-start.7
  0.7 2.1 %shard_map.95 = (bf16[80,1024]{1,0:T(8,128)(2,1)}, bf16[64,1024]{1,0:T(8,128)(2,1)}) custom-call(bf16[64,4096]{1,0:T(8,128)(2,1)} %anomalies.3, f32[1,4096]{1,0:T(1,128)} %bitcast.14, f32[1,4096]{1,0:T(1,128)} %bitcast.7, f32[1,4096]{1,0:T(1,128)} %bitcast.9, s32[1,4096]{1,0:T(1,128)} %bitcast.11), custom_call_target="tpu_custom_call" | custom-call | flops 4000000000 | bytes 1048576 | tf_op jit(solution)/shard_map/pallas_call | solution.py:363
  2.7 4.9 %collective-permute-start = (bf16[80,1024]{1,0:T(8,128)(2,1)}, bf16[80,1024]{1,0:T(8,128)(2,1)S(1)}, u32[]{:S(2)}, u32[]{:S(2)}) collective-permute-start(bf16[80,1024]{1,0:T(8,128)(2,1)} %get-tuple-element.14), channel_id=1, source_target_pairs={{0,24},{8,16},{16,40},{24,32},{32,56},{40,48},{48,72},{56,64},{64,... | collective-permute-start | bytes 491528 | tf_op jit(solution)/shard_map/ppermute | solution.py:379
  7.7 2.0 %collective-permute-start.1 = (bf16[64,1024]{1,0:T(8,128)(2,1)}, bf16[64,1024]{1,0:T(8,128)(2,1)S(1)}, u32[]{:S(2)}, u32[]{:S(2)}) collective-permute-start(bf16[64,1024]{1,0:T(8,128)(2,1)} %get-tuple-element.15), channel_id=1, source_target_pairs={{0,8},{8,0},{1,9},{9,1},{2,10},{10,2},{3,11},{11,3},{4,12},{12,4},... | collective-permute-start | bytes 393224 | tf_op jit(solution)/shard_map/ppermute | solution.py:380
  9.7 0.0 copy-done.4
  9.7 0.0 copy-done.5
  9.7 0.0 copy-done.6
  9.8 0.0 copy-done.7
  9.8 2.6 %shard_map.96 = (bf16[8,64,1536]{2,1,0:T(8,128)(2,1)S(1)}, bf16[1280,256]{1,0:T(8,128)(2,1)S(1)}, bf16[64,256]{1,0:T(8,128)(2,1)S(1)}, f32[1,4096]{1,0:T(1,128)S(1)}) custom-call(s32[8]{0:T(128)S(1)} %copy-done.7, bf16[64,4096]{1,0:T(8,128)(2,1)S(1)} %copy-done.4, f32[1,4096]{1,0:T(1,128)S(1)} %bitcast.15, bf16[64,1024]{1,0:T(8,128)(2,1)S(1)} %copy-done.5), custom_call_target="tpu_custom_call" | custom-call | flops 629145600 | bytes 4194304 | tf_op jit(solution)/shard_map/pallas_call | solution.py:382
  12.3 2.4 %collective-permute-done.1.first = bf16[64,1024]{1,0:T(8,128)(2,1)S(1)} collective-permute-done((bf16[64,1024]{1,0:T(8,128)(2,1)}, bf16[64,1024]{1,0:T(8,128)(2,1)S(1)}, u32[]{:S(2)}, u32[]{:S(2)}) %collective-permute-start.1) | collective-permute-done | bytes 131104 | tf_op jit(solution)/shard_map/ppermute | solution.py:380
  14.7 6.3 %collective-permute-done.edge = bf16[80,1024]{1,0:T(8,128)(2,1)S(1)} collective-permute-done((bf16[80,1024]{1,0:T(8,128)(2,1)}, bf16[80,1024]{1,0:T(8,128)(2,1)S(1)}, u32[]{:S(2)}, u32[]{:S(2)}) %collective-permute-start) | collective-permute-done | bytes 163872 | tf_op jit(solution)/shard_map/ppermute | solution.py:379
  21.0 0.4 shard_map.97
  21.4 0.0 copy-start
  21.4 0.0 copy-start.1
  21.5 0.0 copy-start.2
  21.5 24.4 %all_to_all.15.mine = bf16[8,64,1536]{2,1,0:T(8,128)(2,1)S(1)} all-to-all(bf16[8,64,1536]{2,1,0:T(8,128)(2,1)S(1)} %get-tuple-element.20), channel_id=1, replica_groups=mesh['z'=16,'y_hi'=2,'y_lo'=2,'x'=4,'core'=2] {'y_lo','x'}, dimensions={0} | all-to-all | bytes 3145728 | tf_op jit(solution)/shard_map/all_to_all | solution.py:415
  45.8 1.9 %collective-permute-start.2 = (bf16[8,64,1536]{2,1,0:T(8,128)(2,1)S(1)}, bf16[8,64,1536]{2,1,0:T(8,128)(2,1)S(1)}, u32[]{:S(2)}, u32[]{:S(2)}) collective-permute-start(bf16[8,64,1536]{2,1,0:T(8,128)(2,1)S(1)} %all_to_all.15.mine), channel_id=1, source_target_pairs={{0,1},{1,0},{2,3},{3,2},{4,5},{5,4},{6,7},{7,6},{8,9},{9,8},{10,11... | collective-permute-start | bytes 4718600 | tf_op jit(solution)/shard_map/ppermute | solution.py:416
  47.7 0.0 copy-done
  47.8 0.0 copy-done.1
  47.8 0.0 copy-done.2
  47.8 0.5 shard_map.98
  48.3 2.9 %collective-permute-done.2.other = bf16[8,64,1536]{2,1,0:T(8,128)(2,1)S(1)} collective-permute-done((bf16[8,64,1536]{2,1,0:T(8,128)(2,1)S(1)}, bf16[8,64,1536]{2,1,0:T(8,128)(2,1)S(1)}, u32[]{:S(2)}, u32[]{:S(2)}) %collective-permute-start.2) | collective-permute-done | bytes 1572896 | tf_op jit(solution)/shard_map/ppermute | solution.py:416
  51.1 3.2 %shard_map.99 = bf16[16,256,128]{2,1,0:T(8,128)(2,1)S(1)} custom-call(bf16[8,64,1536]{2,1,0:T(8,128)(2,1)S(1)} %all_to_all.15.mine, bf16[8,64,1536]{2,1,0:T(8,128)(2,1)S(1)} %collective-permute-done.2.other, f32[1,512]{1,0:T(1,128)S(1)} %get-tuple-element.21.base_mean, f32[1,512]{1,0:T(1,128)S(1)} %get-tuple-element.22.weight_row, ...), custom_call_target="tpu_custom_call" | custom-call | flops 1610612736 | bytes 4194304 | tf_op jit(solution)/shard_map/pallas_call | solution.py:426
  54.3 0.0 copy-start.3
  54.3 20.1 %all_to_all.16.parts = bf16[16,256,128]{2,1,0:T(8,128)(2,1)S(1)} all-to-all(bf16[16,256,128]{2,1,0:T(8,128)(2,1)S(1)} %shard_map.99), channel_id=1, replica_groups=mesh['z'=16,'y_hi'=2,'y_lo'=2,'x'=4,'core'=2] {'y_hi','y_lo','x'}, dimensions={0} | all-to-all | bytes 2097152 | tf_op jit(solution)/shard_map/all_to_all | solution.py:441
  74.4 0.5 shard_map.100
  74.9 22.4 %all_to_all.17.parts = bf16[16,32,128]{2,1,0:T(8,128)(2,1)S(1)} all-to-all(bf16[16,32,128]{2,1,0:T(8,128)(2,1)S(1)} %shard_map.100), channel_id=1, replica_groups=mesh['z'=16,'y_hi'=2,'y_lo'=2,'x'=4,'core'=2] {'z'}, dimensions={0} | all-to-all | bytes 262144 | tf_op jit(solution)/shard_map/all_to_all | solution.py:449
  97.4 0.0 copy-done.3
  97.4 0.8 shard_map.101
Async XLA Ops:
  0.6 9.1 %copy-start.4 = (bf16[64,4096]{1,0:T(8,128)(2,1)S(1)}, bf16[64,4096]{1,0:T(8,128)(2,1)}, u32[]{:S(2)}) copy-start(bf16[64,4096]{1,0:T(8,128)(2,1)} %anomalies.3) | copy-start | bytes 1572868
  0.6 9.1 %copy-start.5 = (bf16[64,1024]{1,0:T(8,128)(2,1)S(1)}, bf16[64,1024]{1,0:T(8,128)(2,1)}, u32[]{:S(2)}) copy-start(bf16[64,1024]{1,0:T(8,128)(2,1)} %transform.1) | copy-start | bytes 393220
  0.7 9.1 %copy-start.6 = (f32[4096]{0:T(1024)S(1)}, f32[4096]{0:T(1024)}, u32[]{:S(2)}) copy-start(f32[4096]{0:T(1024)} %param.8) | copy-start | bytes 49156
  0.7 9.1 %copy-start.7 = (s32[8]{0:T(128)S(1)}, s32[8]{0:T(128)}, u32[]{:S(2)}) copy-start(s32[8]{0:T(128)} %offsets.1) | copy-start | bytes 100
  2.7 18.3 %collective-permute-start = (bf16[80,1024]{1,0:T(8,128)(2,1)}, bf16[80,1024]{1,0:T(8,128)(2,1)S(1)}, u32[]{:S(2)}, u32[]{:S(2)}) collective-permute-start(bf16[80,1024]{1,0:T(8,128)(2,1)} %get-tuple-element.14), channel_id=1, source_target_pairs={{0,24},{8,16},{16,40},{24,32},{32,56},{40,48},{48,72},{56,64},{64,... | collective-permute-start | bytes 491528 | tf_op jit(solution)/shard_map/ppermute | solution.py:379
  7.7 7.1 %collective-permute-start.1 = (bf16[64,1024]{1,0:T(8,128)(2,1)}, bf16[64,1024]{1,0:T(8,128)(2,1)S(1)}, u32[]{:S(2)}, u32[]{:S(2)}) collective-permute-start(bf16[64,1024]{1,0:T(8,128)(2,1)} %get-tuple-element.15), channel_id=1, source_target_pairs={{0,8},{8,0},{1,9},{9,1},{2,10},{10,2},{3,11},{11,3},{4,12},{12,4},... | collective-permute-start | bytes 393224 | tf_op jit(solution)/shard_map/ppermute | solution.py:380
  21.4 26.3 %copy-start = (f32[4096]{0:T(1024)S(1)}, f32[4096]{0:T(1024)}, u32[]{:S(2)}) copy-start(f32[4096]{0:T(1024)} %param.12) | copy-start | bytes 49156
  21.4 26.3 %copy-start.1 = (f32[4096]{0:T(1024)S(1)}, f32[4096]{0:T(1024)}, u32[]{:S(2)}) copy-start(f32[4096]{0:T(1024)} %param.13) | copy-start | bytes 49156
  21.5 26.3 %copy-start.2 = (s32[4096]{0:T(1024)S(1)}, s32[4096]{0:T(1024)}, u32[]{:S(2)}) copy-start(s32[4096]{0:T(1024)} %param.14) | copy-start | bytes 49156
  45.8 5.3 %collective-permute-start.2 = (bf16[8,64,1536]{2,1,0:T(8,128)(2,1)S(1)}, bf16[8,64,1536]{2,1,0:T(8,128)(2,1)S(1)}, u32[]{:S(2)}, u32[]{:S(2)}) collective-permute-start(bf16[8,64,1536]{2,1,0:T(8,128)(2,1)S(1)} %all_to_all.15.mine), channel_id=1, source_target_pairs={{0,1},{1,0},{2,3},{3,2},{4,5},{5,4},{6,7},{7,6},{8,9},{9,8},{10,11... | collective-permute-start | bytes 4718600 | tf_op jit(solution)/shard_map/ppermute | solution.py:416
  54.3 43.1 %copy-start.3 = (f32[64]{0:T(128)S(1)}, f32[64]{0:T(128)}, u32[]{:S(2)}) copy-start(f32[64]{0:T(128)} %param.11) | copy-start | bytes 772

commit v7 on v6

--- a/solution.py
+++ b/solution.py
@@ -277,50 +277,55 @@
 
 def gram_kernel(
     mine, other, base_mean, weight_row, value_row,
-    out, transform, gathered, centred, scaled, part,
+    out, gathered, scaled, part,
 ):
     core = lax.axis_index("core")
     crossed = jnp.where(spot()[1] * COLS < EDGE, GROUP // 2, 0)
     for k in range(GROUP):
         for block, side in ((mine, core), (other, 1 - core)):
-            at = pl.ds(pl.multiple_of(k * 128 + side * ROWS, ROWS), ROWS)
-            transform[at] = block[k, :, COLS:]
             home = lax.rem(k + crossed, GROUP) * 128 + side * ROWS
             gathered[pl.ds(pl.multiple_of(home, ROWS), ROWS)] = block[k, :, 0:COLS]
 
-    own = [pl.ds(pl.multiple_of(k * 128 + core * ROWS, ROWS), ROWS) for k in range(GROUP)]
+    half = GROUP * ROWS
     for k in range(COLS // CH):
         c = slice(k * CH, k * CH + CH)
-        mean = jnp.dot(transform[...], gathered[:, c], preferred_element_type=F32)
-        mean = mean + base_mean[:, c]
-        predicted = mean + 0.25 * mean * mean
-        average = jnp.sum(predicted, axis=0, keepdims=True) * (1.0 / M)
-        difference = predicted - average
-        centred[k] = difference
+        predicted = []
+        for block in (mine, other):
+            mean = jnp.dot(
+                block[:, :, COLS:].reshape(half, M), gathered[:, c], preferred_element_type=F32
+            )
+            mean = mean + base_mean[:, c]
+            predicted.append(mean + 0.25 * mean * mean)
+        average = jnp.sum(predicted[0] + predicted[1], axis=0, keepdims=True) * (1.0 / M)
         weight = weight_row[:, c]
-        scaled[:, c] = (difference * jnp.sqrt(weight * (1.0 / (M - 1)))).astype(BF)
+        root = jnp.sqrt(weight * (1.0 / (M - 1)))
         slope = (value_row[:, c] - weight * average) * (1.0 / math.sqrt(M - 1))
-        for j in range(GROUP):
-            product = centred[k, own[j]] * slope
-            product = product[:, :128] + product[:, 128:]
-            if k == 0:
-                part[j * ROWS : j * ROWS + ROWS] = product
-            else:
-                part[j * ROWS : j * ROWS + ROWS] += product
-    rows = jnp.concatenate([scaled[own[j]] for j in range(GROUP)], axis=0)
+        for n in range(2):
+            difference = predicted[n] - average
+            scaled[n * half : n * half + half, c] = (difference * root).astype(BF)
+            if n == 0:
+                product = difference * slope
+                product = product[:, :128] + product[:, 128:]
+                if k == 0:
+                    part[...] = product
+                else:
+                    part[...] += product
     slopes = jnp.sum(part[...].T, axis=0, keepdims=True)
     left_half = lax.broadcasted_iota(jnp.int32, (16, 128), 1) < ROWS
     seats = seated(slopes)
-    gram = lax.dot_general(scaled[...], rows, NT, preferred_element_type=F32)
+    gram = lax.dot_general(scaled[...], scaled[0:half], NT, preferred_element_type=F32)
+    here = [core == n for n in range(2)]
     for j in range(GROUP):
         lanes = slice(j // 2 * 128, j // 2 * 128 + 128)
         seat = seats[j * 16 : j * 16 + 16]
         for y_hi in range(2):
             target = out.at[y_hi * GROUP + j]
             for z in range(16):
-                at = z * 64 + y_hi * 32
-                top = gram[at : at + 16, lanes]
-                bottom = gram[at + 16 : at + 32, lanes]
+                at = z // 2 * ROWS + y_hi * 32
+                both = jnp.where(
+                    here[z % 2], gram[at : at + 32, lanes], gram[half + at : half + at + 32, lanes]
+                )
+                top, bottom = both[0:16], both[16:32]
                 if j % 2 == 0:
                     packed = jnp.where(left_half, top, pltpu.roll(bottom, ROWS, 1))
                 else:
@@ -428,9 +433,7 @@
         shape(2 * GROUP, 256, 128),
         [vmem()] * 5,
         scratch=[
-            pltpu.VMEM((M, M), BF),
             pltpu.VMEM((M, COLS), BF),
-            pltpu.VMEM((COLS // CH, M, CH), F32),
             pltpu.VMEM((M, COLS), BF),
             pltpu.VMEM((GROUP * ROWS, 128), F32),
         ],

time: 98.5 us -> 98 us (level)
  no operation moved by 1% of the time
where the time goes in v7:
time: 98 us; the launch traced here: 97.6 us
  blocking collectives  66.9 us (68%)
  waiting for transfers between devices  11.5 us (12%)
  Pallas kernels  9.43 us (10%)
  starting transfers between devices  8.88 us (9%)
    all_to_all x1, blocking collectives, on_device(): mine = lax.all_to_all(outgoing, ('y_lo', 'x'), 0, 0)  24.4 us
    all_to_all x1, blocking collectives, on_device(): sums = lax.all_to_all(sums, 'z', 0, 0)  22.5 us
    all_to_all x1, blocking collectives, on_device(): parts = lax.all_to_all(parts, ('y_hi', 'y_lo', 'x'), 0, 0)  20.1 us
    ppermute x1, waiting for transfers between devices, on_device(): edge = lax.ppermute(edge, ('z', 'y_hi', 'y_lo'), onward)  6.25 us
    ppermute x1, starting transfers between devices, on_device(): edge = lax.ppermute(edge, ('z', 'y_hi', 'y_lo'), onward)  4.92 us
    ppermute x1, waiting for transfers between devices, on_device(): other = lax.ppermute(mine, 'core', [(0, 1), (1, 0)])  2.85 us
    pallas_call x1, Pallas kernels, on_device(): call(gram_kernel, shape(2 * GROUP, 256, 128), [vmem()] * 5, scratch=[pltp...  2.63 us
    pallas_call x1, Pallas kernels, on_device(): call(inner_kernel, (shape(GROUP, ROWS, COLS + M), shape(TILES * CH, CH),...  2.56 us
  transfers between devices with their start and end apart: 3, of which 3 were waited for; matrix products, arithmetic and copies ran while one was open for 0% of the time, Pallas kernels for 3%

profile of v7, /device:TPU:2, one launch (start us, length us, event | category | flops | bytes accessed | tf_op | source)
XLA Modules:
  0.0 97.6 jit_solution(5914300717539724925)
XLA Ops:
  0.6 0.0 copy-start.4
  0.6 0.0 copy-start.5
  0.7 0.0 copy-start.6
  0.7 0.0 copy-start.7
  0.7 2.1 %shard_map.95 = (bf16[80,1024]{1,0:T(8,128)(2,1)}, bf16[64,1024]{1,0:T(8,128)(2,1)}) custom-call(bf16[64,4096]{1,0:T(8,128)(2,1)} %anomalies.3, f32[1,4096]{1,0:T(1,128)} %bitcast.14, f32[1,4096]{1,0:T(1,128)} %bitcast.7, f32[1,4096]{1,0:T(1,128)} %bitcast.9, s32[1,4096]{1,0:T(1,128)} %bitcast.11), custom_call_target="tpu_custom_call" | custom-call | flops 4000000000 | bytes 1048576 | tf_op jit(solution)/shard_map/pallas_call | solution.py:368
  2.7 4.9 %collective-permute-start = (bf16[80,1024]{1,0:T(8,128)(2,1)}, bf16[80,1024]{1,0:T(8,128)(2,1)S(1)}, u32[]{:S(2)}, u32[]{:S(2)}) collective-permute-start(bf16[80,1024]{1,0:T(8,128)(2,1)} %get-tuple-element.14), channel_id=1, source_target_pairs={{0,24},{8,16},{16,40},{24,32},{32,56},{40,48},{48,72},{56,64},{64,... | collective-permute-start | bytes 491528 | tf_op jit(solution)/shard_map/ppermute | solution.py:384
  7.7 2.0 %collective-permute-start.1 = (bf16[64,1024]{1,0:T(8,128)(2,1)}, bf16[64,1024]{1,0:T(8,128)(2,1)S(1)}, u32[]{:S(2)}, u32[]{:S(2)}) collective-permute-start(bf16[64,1024]{1,0:T(8,128)(2,1)} %get-tuple-element.15), channel_id=1, source_target_pairs={{0,8},{8,0},{1,9},{9,1},{2,10},{10,2},{3,11},{11,3},{4,12},{12,4},... | collective-permute-start | bytes 393224 | tf_op jit(solution)/shard_map/ppermute | solution.py:385
  9.7 0.0 copy-done.4
  9.7 0.0 copy-done.5
  9.7 0.0 copy-done.6
  9.8 0.0 copy-done.7
  9.8 2.6 %shard_map.96 = (bf16[8,64,1536]{2,1,0:T(8,128)(2,1)S(1)}, bf16[1280,256]{1,0:T(8,128)(2,1)S(1)}, bf16[64,256]{1,0:T(8,128)(2,1)S(1)}, f32[1,4096]{1,0:T(1,128)S(1)}) custom-call(s32[8]{0:T(128)S(1)} %copy-done.7, bf16[64,4096]{1,0:T(8,128)(2,1)S(1)} %copy-done.4, f32[1,4096]{1,0:T(1,128)S(1)} %bitcast.15, bf16[64,1024]{1,0:T(8,128)(2,1)S(1)} %copy-done.5), custom_call_target="tpu_custom_call" | custom-call | flops 629145600 | bytes 4194304 | tf_op jit(solution)/shard_map/pallas_call | solution.py:387
  12.3 2.4 %collective-permute-done.1.first = bf16[64,1024]{1,0:T(8,128)(2,1)S(1)} collective-permute-done((bf16[64,1024]{1,0:T(8,128)(2,1)}, bf16[64,1024]{1,0:T(8,128)(2,1)S(1)}, u32[]{:S(2)}, u32[]{:S(2)}) %collective-permute-start.1) | collective-permute-done | bytes 131104 | tf_op jit(solution)/shard_map/ppermute | solution.py:385
  14.7 6.3 %collective-permute-done.edge = bf16[80,1024]{1,0:T(8,128)(2,1)S(1)} collective-permute-done((bf16[80,1024]{1,0:T(8,128)(2,1)}, bf16[80,1024]{1,0:T(8,128)(2,1)S(1)}, u32[]{:S(2)}, u32[]{:S(2)}) %collective-permute-start) | collective-permute-done | bytes 163872 | tf_op jit(solution)/shard_map/ppermute | solution.py:384
  21.0 0.4 shard_map.97
  21.4 0.0 copy-start
  21.4 0.0 copy-start.1
  21.5 0.0 copy-start.2
  21.5 24.4 %all_to_all.15.mine = bf16[8,64,1536]{2,1,0:T(8,128)(2,1)S(1)} all-to-all(bf16[8,64,1536]{2,1,0:T(8,128)(2,1)S(1)} %get-tuple-element.20), channel_id=1, replica_groups=mesh['z'=16,'y_hi'=2,'y_lo'=2,'x'=4,'core'=2] {'y_lo','x'}, dimensions={0} | all-to-all | bytes 3145728 | tf_op jit(solution)/shard_map/all_to_all | solution.py:420
  45.8 1.9 %collective-permute-start.2 = (bf16[8,64,1536]{2,1,0:T(8,128)(2,1)S(1)}, bf16[8,64,1536]{2,1,0:T(8,128)(2,1)S(1)}, u32[]{:S(2)}, u32[]{:S(2)}) collective-permute-start(bf16[8,64,1536]{2,1,0:T(8,128)(2,1)S(1)} %all_to_all.15.mine), channel_id=1, source_target_pairs={{0,1},{1,0},{2,3},{3,2},{4,5},{5,4},{6,7},{7,6},{8,9},{9,8},{10,11... | collective-permute-start | bytes 4718600 | tf_op jit(solution)/shard_map/ppermute | solution.py:421
  47.7 0.0 copy-done
  47.8 0.0 copy-done.1
  47.8 0.0 copy-done.2
  47.8 0.5 shard_map.98
  48.3 2.9 %collective-permute-done.2.other = bf16[8,64,1536]{2,1,0:T(8,128)(2,1)S(1)} collective-permute-done((bf16[8,64,1536]{2,1,0:T(8,128)(2,1)S(1)}, bf16[8,64,1536]{2,1,0:T(8,128)(2,1)S(1)}, u32[]{:S(2)}, u32[]{:S(2)}) %collective-permute-start.2) | collective-permute-done | bytes 1572896 | tf_op jit(solution)/shard_map/ppermute | solution.py:421
  51.1 2.6 %shard_map.99 = bf16[16,256,128]{2,1,0:T(8,128)(2,1)S(1)} custom-call(bf16[8,64,1536]{2,1,0:T(8,128)(2,1)S(1)} %all_to_all.15.mine, bf16[8,64,1536]{2,1,0:T(8,128)(2,1)S(1)} %collective-permute-done.2.other, f32[1,512]{1,0:T(1,128)S(1)} %get-tuple-element.21.base_mean, f32[1,512]{1,0:T(1,128)S(1)} %get-tuple-element.22.weight_row, ...), custom_call_target="tpu_custom_call" | custom-call | flops 1610612736 | bytes 4194304 | tf_op jit(solution)/shard_map/pallas_call | solution.py:431
  53.8 0.0 copy-start.3
  53.8 20.1 %all_to_all.16.parts = bf16[16,256,128]{2,1,0:T(8,128)(2,1)S(1)} all-to-all(bf16[16,256,128]{2,1,0:T(8,128)(2,1)S(1)} %shard_map.99), channel_id=1, replica_groups=mesh['z'=16,'y_hi'=2,'y_lo'=2,'x'=4,'core'=2] {'y_hi','y_lo','x'}, dimensions={0} | all-to-all | bytes 2097152 | tf_op jit(solution)/shard_map/all_to_all | solution.py:444
  73.9 0.5 shard_map.100
  74.4 22.5 %all_to_all.17.parts = bf16[16,32,128]{2,1,0:T(8,128)(2,1)S(1)} all-to-all(bf16[16,32,128]{2,1,0:T(8,128)(2,1)S(1)} %shard_map.100), channel_id=1, replica_groups=mesh['z'=16,'y_hi'=2,'y_lo'=2,'x'=4,'core'=2] {'z'}, dimensions={0} | all-to-all | bytes 262144 | tf_op jit(solution)/shard_map/all_to_all | solution.py:452
  96.8 0.0 copy-done.3
  96.9 0.8 shard_map.101
Async XLA Ops:
  0.6 9.1 %copy-start.4 = (bf16[64,4096]{1,0:T(8,128)(2,1)S(1)}, bf16[64,4096]{1,0:T(8,128)(2,1)}, u32[]{:S(2)}) copy-start(bf16[64,4096]{1,0:T(8,128)(2,1)} %anomalies.3) | copy-start | bytes 1572868
  0.6 9.1 %copy-start.5 = (bf16[64,1024]{1,0:T(8,128)(2,1)S(1)}, bf16[64,1024]{1,0:T(8,128)(2,1)}, u32[]{:S(2)}) copy-start(bf16[64,1024]{1,0:T(8,128)(2,1)} %transform.1) | copy-start | bytes 393220
  0.7 9.1 %copy-start.6 = (f32[4096]{0:T(1024)S(1)}, f32[4096]{0:T(1024)}, u32[]{:S(2)}) copy-start(f32[4096]{0:T(1024)} %param.8) | copy-start | bytes 49156
  0.7 9.1 %copy-start.7 = (s32[8]{0:T(128)S(1)}, s32[8]{0:T(128)}, u32[]{:S(2)}) copy-start(s32[8]{0:T(128)} %offsets.1) | copy-start | bytes 100
  2.7 18.3 %collective-permute-start = (bf16[80,1024]{1,0:T(8,128)(2,1)}, bf16[80,1024]{1,0:T(8,128)(2,1)S(1)}, u32[]{:S(2)}, u32[]{:S(2)}) collective-permute-start(bf16[80,1024]{1,0:T(8,128)(2,1)} %get-tuple-element.14), channel_id=1, source_target_pairs={{0,24},{8,16},{16,40},{24,32},{32,56},{40,48},{48,72},{56,64},{64,... | collective-permute-start | bytes 491528 | tf_op jit(solution)/shard_map/ppermute | solution.py:384
  7.7 7.1 %collective-permute-start.1 = (bf16[64,1024]{1,0:T(8,128)(2,1)}, bf16[64,1024]{1,0:T(8,128)(2,1)S(1)}, u32[]{:S(2)}, u32[]{:S(2)}) collective-permute-start(bf16[64,1024]{1,0:T(8,128)(2,1)} %get-tuple-element.15), channel_id=1, source_target_pairs={{0,8},{8,0},{1,9},{9,1},{2,10},{10,2},{3,11},{11,3},{4,12},{12,4},... | collective-permute-start | bytes 393224 | tf_op jit(solution)/shard_map/ppermute | solution.py:385
  21.4 26.3 %copy-start = (f32[4096]{0:T(1024)S(1)}, f32[4096]{0:T(1024)}, u32[]{:S(2)}) copy-start(f32[4096]{0:T(1024)} %param.12) | copy-start | bytes 49156
  21.4 26.3 %copy-start.1 = (f32[4096]{0:T(1024)S(1)}, f32[4096]{0:T(1024)}, u32[]{:S(2)}) copy-start(f32[4096]{0:T(1024)} %param.13) | copy-start | bytes 49156
  21.5 26.3 %copy-start.2 = (s32[4096]{0:T(1024)S(1)}, s32[4096]{0:T(1024)}, u32[]{:S(2)}) copy-start(s32[4096]{0:T(1024)} %param.14) | copy-start | bytes 49156
  45.8 5.3 %collective-permute-start.2 = (bf16[8,64,1536]{2,1,0:T(8,128)(2,1)S(1)}, bf16[8,64,1536]{2,1,0:T(8,128)(2,1)S(1)}, u32[]{:S(2)}, u32[]{:S(2)}) collective-permute-start(bf16[8,64,1536]{2,1,0:T(8,128)(2,1)S(1)} %all_to_all.15.mine), channel_id=1, source_target_pairs={{0,1},{1,0},{2,3},{3,2},{4,5},{5,4},{6,7},{7,6},{8,9},{9,8},{10,11... | collective-permute-start | bytes 4718600 | tf_op jit(solution)/shard_map/ppermute | solution.py:421
  53.8 43.1 %copy-start.3 = (f32[64]{0:T(128)S(1)}, f32[64]{0:T(128)}, u32[]{:S(2)}) copy-start(f32[64]{0:T(128)} %param.11) | copy-start | bytes 772

commit v8 on v7

--- a/solution.py
+++ b/solution.py
@@ -261,18 +261,26 @@
     )
 
 
-def unseat(tile, y_hi):
-    tile = jnp.where(y_hi == 0, tile, pltpu.roll(tile, 96, 1))
+def first_half(tile, y_hi):
+    return jnp.where(y_hi == 0, tile, pltpu.roll(tile, 96, 1))
+
+
+def read_seats(tile, y_hi):
+    tile = first_half(tile, y_hi)
     lane = lax.broadcasted_iota(jnp.int32, (16, ROWS), 1)
     row = lax.broadcasted_iota(jnp.int32, (16, ROWS), 0)
     sums = jnp.zeros((16, ROWS), F32)
     for q in range(4):
         part = tile[:, 16 + q : 17 + q] + tile[:, 20 + q : 21 + q]
         sums = sums + jnp.where((lane >> 2 == row) & (lane & 3 == q), part, 0.0)
+    return jnp.sum(sums, axis=0, keepdims=True)
+
+
+def refill_seats(tile, y_hi):
+    tile = first_half(tile, y_hi)
     tall = jnp.concatenate([tile, jnp.zeros((112, 128), F32)], axis=0).T
     tile = jnp.where(seated_lanes(0), pltpu.roll(tall[64:80], 16, 1), tile)
-    tile = jnp.where(y_hi == 0, tile, pltpu.roll(tile, 32, 1))
-    return jnp.sum(sums, axis=0, keepdims=True), tile
+    return jnp.where(y_hi == 0, tile, pltpu.roll(tile, 32, 1))
 
 
 def gram_kernel(
@@ -337,24 +345,37 @@
 
 
 def middle_kernel(parts, out, total):
-    total[...] = jnp.sum(parts[...].astype(F32), axis=0)
+    for first in range(0, 256, 64):
+        rows = slice(first, first + 64)
+        sums = parts[0, rows].astype(F32)
+        for k in range(1, 2 * GROUP):
+            sums = sums + parts[k, rows].astype(F32)
+        total[rows] = sums
+        for z in range(first // 16, first // 16 + 4):
+            at = z * 16 - first
+            out[z, 0:16] = sums[at : at + 16].astype(BF)
     block = spot()[2] // ROWS
     at = pl.ds(pl.multiple_of(block * 16, 16), 16)
-    slopes, tile = unseat(total[at], lax.axis_index("y_hi"))
-    total[at] = tile
-    tail = two_part_rows(slopes, 16)
+    tail = two_part_rows(read_seats(total[at], lax.axis_index("y_hi")), 16)
     for z in range(16):
-        out[z, 0:16] = total[z * 16 : z * 16 + 16].astype(BF)
         out[z, 16:32] = tail
 
 
-def last_kernel(parts, weights, hessian, gradient):
+def last_kernel(parts, weights, hessian, gradient, packed):
     _, _, row0, column0 = spot()
-    total = jnp.sum(parts[...].astype(F32), axis=0)
+    total = parts[0].astype(F32)
+    for z in range(1, 16):
+        total = total + parts[z].astype(F32)
+    packed[...] = total[0:16]
+
+    @pl.when(lax.axis_index("z") == row0 // ROWS)
+    def _():
+        packed[...] = refill_seats(packed[...], lax.axis_index("y_hi"))
+
     row = lax.broadcasted_iota(jnp.int32, (16, ROWS), 1) + row0
     column = lax.broadcasted_iota(jnp.int32, (16, ROWS), 0) + column0
     for half in range(2):
-        block = total[0:16, half * ROWS : half * ROWS + ROWS]
+        block = packed[:, half * ROWS : half * ROWS + ROWS]
         same = row == column + half * 16
         hessian[half * 16 : half * 16 + 16] = block + jnp.where(same, 1.0, 0.0)
     gradient[...] = weights[...] - (total[16:17, 0:ROWS] + total[16:17, ROWS:])
@@ -451,7 +472,8 @@
     )(parts)
     sums = lax.all_to_all(sums, "z", 0, 0)
     hessian, gradient = call(
-        last_kernel, (shape32(32, ROWS), shape32(1, ROWS)), [vmem()] * 2, nbytes=MIB // 4
+        last_kernel, (shape32(32, ROWS), shape32(1, ROWS)), [vmem()] * 2, nbytes=MIB // 4,
+        scratch=[pltpu.VMEM((16, 128), F32)],
     )(sums, weights.reshape(1, ROWS))
     return hessian.T, gradient.reshape(ROWS)
 

time: 98 us -> 97.9 us (level)
  no operation moved by 1% of the time
where the time goes in v8:
time: 97.9 us; the launch traced here: 97.6 us
  blocking collectives  66.9 us (68%)
  waiting for transfers between devices  11.5 us (12%)
  Pallas kernels  9.38 us (10%)
  starting transfers between devices  8.88 us (9%)
    all_to_all x1, blocking collectives, on_device(): mine = lax.all_to_all(outgoing, ('y_lo', 'x'), 0, 0)  24.4 us
    all_to_all x1, blocking collectives, on_device(): sums = lax.all_to_all(sums, 'z', 0, 0)  22.5 us
    all_to_all x1, blocking collectives, on_device(): parts = lax.all_to_all(parts, ('y_hi', 'y_lo', 'x'), 0, 0)  20.1 us
    ppermute x1, waiting for transfers between devices, on_device(): edge = lax.ppermute(edge, ('z', 'y_hi', 'y_lo'), onward)  6.25 us
    ppermute x1, starting transfers between devices, on_device(): edge = lax.ppermute(edge, ('z', 'y_hi', 'y_lo'), onward)  4.92 us
    ppermute x1, waiting for transfers between devices, on_device(): other = lax.ppermute(mine, 'core', [(0, 1), (1, 0)])  2.85 us
    pallas_call x1, Pallas kernels, on_device(): call(gram_kernel, shape(2 * GROUP, 256, 128), [vmem()] * 5, scratch=[pltp...  2.63 us
    pallas_call x1, Pallas kernels, on_device(): call(inner_kernel, (shape(GROUP, ROWS, COLS + M), shape(TILES * CH, CH),...  2.56 us
  transfers between devices with their start and end apart: 3, of which 3 were waited for; matrix products, arithmetic and copies ran while one was open for 0% of the time, Pallas kernels for 3%

profile of v8, /device:TPU:2, one launch (start us, length us, event | category | flops | bytes accessed | tf_op | source)
XLA Modules:
  0.0 97.6 jit_solution(2140018567955423081)
XLA Ops:
  0.6 0.0 copy-start.4
  0.6 0.0 copy-start.5
  0.7 0.0 copy-start.6
  0.7 0.0 copy-start.7
  0.7 2.1 %shard_map.95 = (bf16[80,1024]{1,0:T(8,128)(2,1)}, bf16[64,1024]{1,0:T(8,128)(2,1)}) custom-call(bf16[64,4096]{1,0:T(8,128)(2,1)} %anomalies.3, f32[1,4096]{1,0:T(1,128)} %bitcast.14, f32[1,4096]{1,0:T(1,128)} %bitcast.7, f32[1,4096]{1,0:T(1,128)} %bitcast.9, s32[1,4096]{1,0:T(1,128)} %bitcast.11), custom_call_target="tpu_custom_call" | custom-call | flops 4000000000 | bytes 1048576 | tf_op jit(solution)/shard_map/pallas_call | solution.py:389
  2.7 4.9 %collective-permute-start = (bf16[80,1024]{1,0:T(8,128)(2,1)}, bf16[80,1024]{1,0:T(8,128)(2,1)S(1)}, u32[]{:S(2)}, u32[]{:S(2)}) collective-permute-start(bf16[80,1024]{1,0:T(8,128)(2,1)} %get-tuple-element.14), channel_id=1, source_target_pairs={{0,24},{8,16},{16,40},{24,32},{32,56},{40,48},{48,72},{56,64},{64,... | collective-permute-start | bytes 491528 | tf_op jit(solution)/shard_map/ppermute | solution.py:405
  7.7 2.0 %collective-permute-start.1 = (bf16[64,1024]{1,0:T(8,128)(2,1)}, bf16[64,1024]{1,0:T(8,128)(2,1)S(1)}, u32[]{:S(2)}, u32[]{:S(2)}) collective-permute-start(bf16[64,1024]{1,0:T(8,128)(2,1)} %get-tuple-element.15), channel_id=1, source_target_pairs={{0,8},{8,0},{1,9},{9,1},{2,10},{10,2},{3,11},{11,3},{4,12},{12,4},... | collective-permute-start | bytes 393224 | tf_op jit(solution)/shard_map/ppermute | solution.py:406
  9.7 0.0 copy-done.4
  9.7 0.0 copy-done.5
  9.7 0.0 copy-done.6
  9.8 0.0 copy-done.7
  9.8 2.6 %shard_map.96 = (bf16[8,64,1536]{2,1,0:T(8,128)(2,1)S(1)}, bf16[1280,256]{1,0:T(8,128)(2,1)S(1)}, bf16[64,256]{1,0:T(8,128)(2,1)S(1)}, f32[1,4096]{1,0:T(1,128)S(1)}) custom-call(s32[8]{0:T(128)S(1)} %copy-done.7, bf16[64,4096]{1,0:T(8,128)(2,1)S(1)} %copy-done.4, f32[1,4096]{1,0:T(1,128)S(1)} %bitcast.15, bf16[64,1024]{1,0:T(8,128)(2,1)S(1)} %copy-done.5), custom_call_target="tpu_custom_call" | custom-call | flops 629145600 | bytes 4194304 | tf_op jit(solution)/shard_map/pallas_call | solution.py:408
  12.3 2.4 %collective-permute-done.1.first = bf16[64,1024]{1,0:T(8,128)(2,1)S(1)} collective-permute-done((bf16[64,1024]{1,0:T(8,128)(2,1)}, bf16[64,1024]{1,0:T(8,128)(2,1)S(1)}, u32[]{:S(2)}, u32[]{:S(2)}) %collective-permute-start.1) | collective-permute-done | bytes 131104 | tf_op jit(solution)/shard_map/ppermute | solution.py:406
  14.7 6.3 %collective-permute-done.edge = bf16[80,1024]{1,0:T(8,128)(2,1)S(1)} collective-permute-done((bf16[80,1024]{1,0:T(8,128)(2,1)}, bf16[80,1024]{1,0:T(8,128)(2,1)S(1)}, u32[]{:S(2)}, u32[]{:S(2)}) %collective-permute-start) | collective-permute-done | bytes 163872 | tf_op jit(solution)/shard_map/ppermute | solution.py:405
  21.0 0.4 shard_map.97
  21.4 0.0 copy-start
  21.4 0.0 copy-start.1
  21.5 0.0 copy-start.2
  21.5 24.4 %all_to_all.15.mine = bf16[8,64,1536]{2,1,0:T(8,128)(2,1)S(1)} all-to-all(bf16[8,64,1536]{2,1,0:T(8,128)(2,1)S(1)} %get-tuple-element.20), channel_id=1, replica_groups=mesh['z'=16,'y_hi'=2,'y_lo'=2,'x'=4,'core'=2] {'y_lo','x'}, dimensions={0} | all-to-all | bytes 3145728 | tf_op jit(solution)/shard_map/all_to_all | solution.py:441
  45.8 1.9 %collective-permute-start.2 = (bf16[8,64,1536]{2,1,0:T(8,128)(2,1)S(1)}, bf16[8,64,1536]{2,1,0:T(8,128)(2,1)S(1)}, u32[]{:S(2)}, u32[]{:S(2)}) collective-permute-start(bf16[8,64,1536]{2,1,0:T(8,128)(2,1)S(1)} %all_to_all.15.mine), channel_id=1, source_target_pairs={{0,1},{1,0},{2,3},{3,2},{4,5},{5,4},{6,7},{7,6},{8,9},{9,8},{10,11... | collective-permute-start | bytes 4718600 | tf_op jit(solution)/shard_map/ppermute | solution.py:442
  47.7 0.0 copy-done
  47.8 0.0 copy-done.1
  47.8 0.0 copy-done.2
  47.8 0.5 shard_map.98
  48.3 2.9 %collective-permute-done.2.other = bf16[8,64,1536]{2,1,0:T(8,128)(2,1)S(1)} collective-permute-done((bf16[8,64,1536]{2,1,0:T(8,128)(2,1)S(1)}, bf16[8,64,1536]{2,1,0:T(8,128)(2,1)S(1)}, u32[]{:S(2)}, u32[]{:S(2)}) %collective-permute-start.2) | collective-permute-done | bytes 1572896 | tf_op jit(solution)/shard_map/ppermute | solution.py:442
  51.1 2.6 %shard_map.99 = bf16[16,256,128]{2,1,0:T(8,128)(2,1)S(1)} custom-call(bf16[8,64,1536]{2,1,0:T(8,128)(2,1)S(1)} %all_to_all.15.mine, bf16[8,64,1536]{2,1,0:T(8,128)(2,1)S(1)} %collective-permute-done.2.other, f32[1,512]{1,0:T(1,128)S(1)} %get-tuple-element.21.base_mean, f32[1,512]{1,0:T(1,128)S(1)} %get-tuple-element.22.weight_row, ...), custom_call_target="tpu_custom_call" | custom-call | flops 1610612736 | bytes 4194304 | tf_op jit(solution)/shard_map/pallas_call | solution.py:452
  53.8 0.0 copy-start.3
  53.8 20.1 %all_to_all.16.parts = bf16[16,256,128]{2,1,0:T(8,128)(2,1)S(1)} all-to-all(bf16[16,256,128]{2,1,0:T(8,128)(2,1)S(1)} %shard_map.99), channel_id=1, replica_groups=mesh['z'=16,'y_hi'=2,'y_lo'=2,'x'=4,'core'=2] {'y_hi','y_lo','x'}, dimensions={0} | all-to-all | bytes 2097152 | tf_op jit(solution)/shard_map/all_to_all | solution.py:465
  73.9 0.4 shard_map.100
  74.3 22.5 %all_to_all.17.parts = bf16[16,32,128]{2,1,0:T(8,128)(2,1)S(1)} all-to-all(bf16[16,32,128]{2,1,0:T(8,128)(2,1)S(1)} %shard_map.100), channel_id=1, replica_groups=mesh['z'=16,'y_hi'=2,'y_lo'=2,'x'=4,'core'=2] {'z'}, dimensions={0} | all-to-all | bytes 262144 | tf_op jit(solution)/shard_map/all_to_all | solution.py:473
  96.8 0.0 copy-done.3
  96.8 0.8 shard_map.101
Async XLA Ops:
  0.6 9.1 %copy-start.4 = (bf16[64,4096]{1,0:T(8,128)(2,1)S(1)}, bf16[64,4096]{1,0:T(8,128)(2,1)}, u32[]{:S(2)}) copy-start(bf16[64,4096]{1,0:T(8,128)(2,1)} %anomalies.3) | copy-start | bytes 1572868
  0.6 9.1 %copy-start.5 = (bf16[64,1024]{1,0:T(8,128)(2,1)S(1)}, bf16[64,1024]{1,0:T(8,128)(2,1)}, u32[]{:S(2)}) copy-start(bf16[64,1024]{1,0:T(8,128)(2,1)} %transform.1) | copy-start | bytes 393220
  0.7 9.1 %copy-start.6 = (f32[4096]{0:T(1024)S(1)}, f32[4096]{0:T(1024)}, u32[]{:S(2)}) copy-start(f32[4096]{0:T(1024)} %param.8) | copy-start | bytes 49156
  0.7 9.1 %copy-start.7 = (s32[8]{0:T(128)S(1)}, s32[8]{0:T(128)}, u32[]{:S(2)}) copy-start(s32[8]{0:T(128)} %offsets.1) | copy-start | bytes 100
  2.7 18.3 %collective-permute-start = (bf16[80,1024]{1,0:T(8,128)(2,1)}, bf16[80,1024]{1,0:T(8,128)(2,1)S(1)}, u32[]{:S(2)}, u32[]{:S(2)}) collective-permute-start(bf16[80,1024]{1,0:T(8,128)(2,1)} %get-tuple-element.14), channel_id=1, source_target_pairs={{0,24},{8,16},{16,40},{24,32},{32,56},{40,48},{48,72},{56,64},{64,... | collective-permute-start | bytes 491528 | tf_op jit(solution)/shard_map/ppermute | solution.py:405
  7.7 7.1 %collective-permute-start.1 = (bf16[64,1024]{1,0:T(8,128)(2,1)}, bf16[64,1024]{1,0:T(8,128)(2,1)S(1)}, u32[]{:S(2)}, u32[]{:S(2)}) collective-permute-start(bf16[64,1024]{1,0:T(8,128)(2,1)} %get-tuple-element.15), channel_id=1, source_target_pairs={{0,8},{8,0},{1,9},{9,1},{2,10},{10,2},{3,11},{11,3},{4,12},{12,4},... | collective-permute-start | bytes 393224 | tf_op jit(solution)/shard_map/ppermute | solution.py:406
  21.4 26.3 %copy-start = (f32[4096]{0:T(1024)S(1)}, f32[4096]{0:T(1024)}, u32[]{:S(2)}) copy-start(f32[4096]{0:T(1024)} %param.12) | copy-start | bytes 49156
  21.4 26.3 %copy-start.1 = (f32[4096]{0:T(1024)S(1)}, f32[4096]{0:T(1024)}, u32[]{:S(2)}) copy-start(f32[4096]{0:T(1024)} %param.13) | copy-start | bytes 49156
  21.5 26.3 %copy-start.2 = (s32[4096]{0:T(1024)S(1)}, s32[4096]{0:T(1024)}, u32[]{:S(2)}) copy-start(s32[4096]{0:T(1024)} %param.14) | copy-start | bytes 49156
  45.8 5.3 %collective-permute-start.2 = (bf16[8,64,1536]{2,1,0:T(8,128)(2,1)S(1)}, bf16[8,64,1536]{2,1,0:T(8,128)(2,1)S(1)}, u32[]{:S(2)}, u32[]{:S(2)}) collective-permute-start(bf16[8,64,1536]{2,1,0:T(8,128)(2,1)S(1)} %all_to_all.15.mine), channel_id=1, source_target_pairs={{0,1},{1,0},{2,3},{3,2},{4,5},{5,4},{6,7},{7,6},{8,9},{9,8},{10,11... | collective-permute-start | bytes 4718600 | tf_op jit(solution)/shard_map/ppermute | solution.py:442
  53.8 43.0 %copy-start.3 = (f32[64]{0:T(128)S(1)}, f32[64]{0:T(128)}, u32[]{:S(2)}) copy-start(f32[64]{0:T(128)} %param.11) | copy-start | bytes 772

commit v9 on v8

--- a/solution.py
+++ b/solution.py
@@ -100,7 +100,7 @@
 
 
 def edge_kernel(
-    anomalies, base, observed, obs_scale, obs_rows, edge, first,
+    anomalies, base, observed, obs_scale, obs_rows, edge,
     base_edge, observed_all, scale_all, rows_all, sems,
 ):
     border = pl.ds(S - EDGE, EDGE)
@@ -110,7 +110,6 @@
         pltpu.make_async_copy(observed, observed_all, sems.at[2]),
         pltpu.make_async_copy(base.at[:, border], base_edge, sems.at[3]),
         pltpu.make_async_copy(anomalies.at[:, border], edge.at[pl.ds(0, ROWS)], sems.at[4]),
-        pltpu.make_async_copy(anomalies.at[:, pl.ds(0, EDGE)], first, sems.at[5]),
     ]
     for copy in copies:
         copy.start()
@@ -126,7 +125,6 @@
     extra.append(jnp.zeros((7, EDGE), BF))
     edge[ROWS:] = jnp.concatenate(extra, axis=0)
     copies[4].wait()
-    copies[5].wait()
 
 
 def banded(rows, band, first, count):
@@ -386,16 +384,16 @@
     base = row(base_state)
     obs = (row(observed), row(obs_scale), row(obs_rows))
 
-    edge, first = call(
+    edge = call(
         edge_kernel,
-        (shape(PITCH, EDGE), shape(ROWS, EDGE)),
+        shape(PITCH, EDGE),
         [hbm()] * 5,
         scratch=[
             pltpu.VMEM((1, EDGE), F32),
             pltpu.VMEM((1, S), F32),
             pltpu.VMEM((1, S), F32),
             pltpu.VMEM((1, S), jnp.int32),
-            pltpu.SemaphoreType.DMA((6,)),
+            pltpu.SemaphoreType.DMA((5,)),
         ],
         flops=4 * 10**9,
         nbytes=MIB,
@@ -403,7 +401,7 @@
     )(anomalies, base, *obs)
     onward = [(d, (d + 2) % 64 ^ 1) for d in range(64)]
     edge = lax.ppermute(edge, ("z", "y_hi", "y_lo"), onward)
-    first = lax.ppermute(first, "y_lo", [(0, 1), (1, 0)])
+    first = lax.ppermute(anomalies[:, :EDGE], "y_lo", [(0, 1), (1, 0)])
 
     outgoing, band, border, means = call(
         inner_kernel,

time: 97.9 us -> 97.7 us (level)
  no operation moved by 1% of the time
where the time goes in v9:
time: 97.7 us; the launch traced here: 97.3 us
  blocking collectives  66.8 us (68%)
  waiting for transfers between devices  11.5 us (12%)
  Pallas kernels  9.33 us (10%)
  starting transfers between devices  8.88 us (9%)
    all_to_all x1, blocking collectives, on_device(): mine = lax.all_to_all(outgoing, ('y_lo', 'x'), 0, 0)  24.4 us
    all_to_all x1, blocking collectives, on_device(): sums = lax.all_to_all(sums, 'z', 0, 0)  22.3 us
    all_to_all x1, blocking collectives, on_device(): parts = lax.all_to_all(parts, ('y_hi', 'y_lo', 'x'), 0, 0)  20.1 us
    ppermute x1, waiting for transfers between devices, on_device(): edge = lax.ppermute(edge, ('z', 'y_hi', 'y_lo'), onward)  6.43 us
    ppermute x1, starting transfers between devices, on_device(): edge = lax.ppermute(edge, ('z', 'y_hi', 'y_lo'), onward)  4.92 us
    ppermute x1, waiting for transfers between devices, on_device(): other = lax.ppermute(mine, 'core', [(0, 1), (1, 0)])  2.85 us
    pallas_call x1, Pallas kernels, on_device(): call(gram_kernel, shape(2 * GROUP, 256, 128), [vmem()] * 5, scratch=[pltp...  2.62 us
    pallas_call x1, Pallas kernels, on_device(): call(inner_kernel, (shape(GROUP, ROWS, COLS + M), shape(TILES * CH, CH),...  2.56 us
  transfers between devices with their start and end apart: 3, of which 3 were waited for; matrix products, arithmetic and copies ran while one was open for 0% of the time, Pallas kernels for 3%

profile of v9, /device:TPU:2, one launch (start us, length us, event | category | flops | bytes accessed | tf_op | source)
XLA Modules:
  0.0 97.3 jit_solution(3266748788409856673)
XLA Ops:
  0.6 0.0 copy-start
  0.6 0.0 copy-start.5
  0.7 0.0 copy-start.6
  0.7 0.0 copy-start.7
  0.7 2.0 %shard_map.95 = bf16[80,1024]{1,0:T(8,128)(2,1)} custom-call(bf16[64,4096]{1,0:T(8,128)(2,1)} %anomalies.3, f32[1,4096]{1,0:T(1,128)} %bitcast.14, f32[1,4096]{1,0:T(1,128)} %bitcast.7, f32[1,4096]{1,0:T(1,128)} %bitcast.9, s32[1,4096]{1,0:T(1,128)} %bitcast.11), custom_call_target="tpu_custom_call" | custom-call | flops 4000000000 | bytes 1048576 | tf_op jit(solution)/shard_map/pallas_call | solution.py:387
  2.7 4.9 %collective-permute-start = (bf16[80,1024]{1,0:T(8,128)(2,1)}, bf16[80,1024]{1,0:T(8,128)(2,1)S(1)}, u32[]{:S(2)}, u32[]{:S(2)}) collective-permute-start(bf16[80,1024]{1,0:T(8,128)(2,1)} %shard_map.95), channel_id=1, source_target_pairs={{0,24},{8,16},{16,40},{24,32},{32,56},{40,48},{48,72},{56,64},{64,... | collective-permute-start | bytes 491528 | tf_op jit(solution)/shard_map/ppermute | solution.py:403
  7.6 0.0 copy-done
  7.7 2.0 %collective-permute-start.1 = (bf16[64,1024]{1,0:T(8,128)(2,1)S(1)}, bf16[64,1024]{1,0:T(8,128)(2,1)S(1)}, u32[]{:S(2)}, u32[]{:S(2)}) collective-permute-start(bf16[64,1024]{1,0:T(8,128)(2,1)S(1)} %slice.3), channel_id=1, source_target_pairs={{0,8},{8,0},{1,9},{9,1},{2,10},{10,2},{3,11},{11,3},{4,12},{12,4},... | collective-permute-start | bytes 393224 | tf_op jit(solution)/shard_map/ppermute | solution.py:404
  9.7 0.0 copy-done.5
  9.7 0.0 copy-done.6
  9.7 0.0 copy-done.7
  9.7 2.6 %shard_map.96 = (bf16[8,64,1536]{2,1,0:T(8,128)(2,1)S(1)}, bf16[1280,256]{1,0:T(8,128)(2,1)S(1)}, bf16[64,256]{1,0:T(8,128)(2,1)S(1)}, f32[1,4096]{1,0:T(1,128)S(1)}) custom-call(s32[8]{0:T(128)S(1)} %copy-done.7, bf16[64,4096]{1,0:T(8,128)(2,1)S(1)} %copy-done, f32[1,4096]{1,0:T(1,128)S(1)} %bitcast.15, bf16[64,1024]{1,0:T(8,128)(2,1)S(1)} %copy-done.5), custom_call_target="tpu_custom_call" | custom-call | flops 629145600 | bytes 4194304 | tf_op jit(solution)/shard_map/pallas_call | solution.py:406
  12.3 2.2 %collective-permute-done.1.first = bf16[64,1024]{1,0:T(8,128)(2,1)S(1)} collective-permute-done((bf16[64,1024]{1,0:T(8,128)(2,1)S(1)}, bf16[64,1024]{1,0:T(8,128)(2,1)S(1)}, u32[]{:S(2)}, u32[]{:S(2)}) %collective-permute-start.1) | collective-permute-done | bytes 131104 | tf_op jit(solution)/shard_map/ppermute | solution.py:404
  14.5 6.4 %collective-permute-done.edge = bf16[80,1024]{1,0:T(8,128)(2,1)S(1)} collective-permute-done((bf16[80,1024]{1,0:T(8,128)(2,1)}, bf16[80,1024]{1,0:T(8,128)(2,1)S(1)}, u32[]{:S(2)}, u32[]{:S(2)}) %collective-permute-start) | collective-permute-done | bytes 163872 | tf_op jit(solution)/shard_map/ppermute | solution.py:403
  20.9 0.4 shard_map.97
  21.4 0.0 copy-start.1
  21.4 0.0 copy-start.2
  21.4 0.0 copy-start.3
  21.4 24.4 %all_to_all.15.mine = bf16[8,64,1536]{2,1,0:T(8,128)(2,1)S(1)} all-to-all(bf16[8,64,1536]{2,1,0:T(8,128)(2,1)S(1)} %get-tuple-element.16), channel_id=1, replica_groups=mesh['z'=16,'y_hi'=2,'y_lo'=2,'x'=4,'core'=2] {'y_lo','x'}, dimensions={0} | all-to-all | bytes 3145728 | tf_op jit(solution)/shard_map/all_to_all | solution.py:439
  45.8 1.9 %collective-permute-start.2 = (bf16[8,64,1536]{2,1,0:T(8,128)(2,1)S(1)}, bf16[8,64,1536]{2,1,0:T(8,128)(2,1)S(1)}, u32[]{:S(2)}, u32[]{:S(2)}) collective-permute-start(bf16[8,64,1536]{2,1,0:T(8,128)(2,1)S(1)} %all_to_all.15.mine), channel_id=1, source_target_pairs={{0,1},{1,0},{2,3},{3,2},{4,5},{5,4},{6,7},{7,6},{8,9},{9,8},{10,11... | collective-permute-start | bytes 4718600 | tf_op jit(solution)/shard_map/ppermute | solution.py:440
  47.7 0.0 copy-done.1
  47.7 0.0 copy-done.2
  47.7 0.0 copy-done.3
  47.7 0.5 shard_map.98
  48.2 2.8 %collective-permute-done.2.other = bf16[8,64,1536]{2,1,0:T(8,128)(2,1)S(1)} collective-permute-done((bf16[8,64,1536]{2,1,0:T(8,128)(2,1)S(1)}, bf16[8,64,1536]{2,1,0:T(8,128)(2,1)S(1)}, u32[]{:S(2)}, u32[]{:S(2)}) %collective-permute-start.2) | collective-permute-done | bytes 1572896 | tf_op jit(solution)/shard_map/ppermute | solution.py:440
  51.1 2.6 %shard_map.99 = bf16[16,256,128]{2,1,0:T(8,128)(2,1)S(1)} custom-call(bf16[8,64,1536]{2,1,0:T(8,128)(2,1)S(1)} %all_to_all.15.mine, bf16[8,64,1536]{2,1,0:T(8,128)(2,1)S(1)} %collective-permute-done.2.other, f32[1,512]{1,0:T(1,128)S(1)} %get-tuple-element.17.base_mean, f32[1,512]{1,0:T(1,128)S(1)} %get-tuple-element.18.weight_row, ...), custom_call_target="tpu_custom_call" | custom-call | flops 1610612736 | bytes 4194304 | tf_op jit(solution)/shard_map/pallas_call | solution.py:450
  53.7 0.0 copy-start.4
  53.7 20.1 %all_to_all.16.parts = bf16[16,256,128]{2,1,0:T(8,128)(2,1)S(1)} all-to-all(bf16[16,256,128]{2,1,0:T(8,128)(2,1)S(1)} %shard_map.99), channel_id=1, replica_groups=mesh['z'=16,'y_hi'=2,'y_lo'=2,'x'=4,'core'=2] {'y_hi','y_lo','x'}, dimensions={0} | all-to-all | bytes 2097152 | tf_op jit(solution)/shard_map/all_to_all | solution.py:463
  73.8 0.4 shard_map.100
  74.3 22.3 %all_to_all.17.parts = bf16[16,32,128]{2,1,0:T(8,128)(2,1)S(1)} all-to-all(bf16[16,32,128]{2,1,0:T(8,128)(2,1)S(1)} %shard_map.100), channel_id=1, replica_groups=mesh['z'=16,'y_hi'=2,'y_lo'=2,'x'=4,'core'=2] {'z'}, dimensions={0} | all-to-all | bytes 262144 | tf_op jit(solution)/shard_map/all_to_all | solution.py:471
  96.6 0.0 copy-done.4
  96.6 0.8 shard_map.101
  (1 shorter events, 0.0 us)
Async XLA Ops:
  0.6 7.0 %copy-start = (bf16[64,4096]{1,0:T(8,128)(2,1)S(1)}, bf16[64,4096]{1,0:T(8,128)(2,1)}, u32[]{:S(2)}) copy-start(bf16[64,4096]{1,0:T(8,128)(2,1)} %anomalies.3) | copy-start | bytes 1572868
  0.6 9.1 %copy-start.5 = (bf16[64,1024]{1,0:T(8,128)(2,1)S(1)}, bf16[64,1024]{1,0:T(8,128)(2,1)}, u32[]{:S(2)}) copy-start(bf16[64,1024]{1,0:T(8,128)(2,1)} %transform.1) | copy-start | bytes 393220
  0.7 9.1 %copy-start.6 = (f32[4096]{0:T(1024)S(1)}, f32[4096]{0:T(1024)}, u32[]{:S(2)}) copy-start(f32[4096]{0:T(1024)} %param.8) | copy-start | bytes 49156
  0.7 9.1 %copy-start.7 = (s32[8]{0:T(128)S(1)}, s32[8]{0:T(128)}, u32[]{:S(2)}) copy-start(s32[8]{0:T(128)} %offsets.1) | copy-start | bytes 100
  2.7 18.3 %collective-permute-start = (bf16[80,1024]{1,0:T(8,128)(2,1)}, bf16[80,1024]{1,0:T(8,128)(2,1)S(1)}, u32[]{:S(2)}, u32[]{:S(2)}) collective-permute-start(bf16[80,1024]{1,0:T(8,128)(2,1)} %shard_map.95), channel_id=1, source_target_pairs={{0,24},{8,16},{16,40},{24,32},{32,56},{40,48},{48,72},{56,64},{64,... | collective-permute-start | bytes 491528 | tf_op jit(solution)/shard_map/ppermute | solution.py:403
  7.7 6.9 %collective-permute-start.1 = (bf16[64,1024]{1,0:T(8,128)(2,1)S(1)}, bf16[64,1024]{1,0:T(8,128)(2,1)S(1)}, u32[]{:S(2)}, u32[]{:S(2)}) collective-permute-start(bf16[64,1024]{1,0:T(8,128)(2,1)S(1)} %slice.3), channel_id=1, source_target_pairs={{0,8},{8,0},{1,9},{9,1},{2,10},{10,2},{3,11},{11,3},{4,12},{12,4},... | collective-permute-start | bytes 393224 | tf_op jit(solution)/shard_map/ppermute | solution.py:404
  21.4 26.3 %copy-start.1 = (f32[4096]{0:T(1024)S(1)}, f32[4096]{0:T(1024)}, u32[]{:S(2)}) copy-start(f32[4096]{0:T(1024)} %param.12) | copy-start | bytes 49156
  21.4 26.3 %copy-start.2 = (f32[4096]{0:T(1024)S(1)}, f32[4096]{0:T(1024)}, u32[]{:S(2)}) copy-start(f32[4096]{0:T(1024)} %param.13) | copy-start | bytes 49156
  21.4 26.3 %copy-start.3 = (s32[4096]{0:T(1024)S(1)}, s32[4096]{0:T(1024)}, u32[]{:S(2)}) copy-start(s32[4096]{0:T(1024)} %param.14) | copy-start | bytes 49156
  45.8 5.3 %collective-permute-start.2 = (bf16[8,64,1536]{2,1,0:T(8,128)(2,1)S(1)}, bf16[8,64,1536]{2,1,0:T(8,128)(2,1)S(1)}, u32[]{:S(2)}, u32[]{:S(2)}) collective-permute-start(bf16[8,64,1536]{2,1,0:T(8,128)(2,1)S(1)} %all_to_all.15.mine), channel_id=1, source_target_pairs={{0,1},{1,0},{2,3},{3,2},{4,5},{5,4},{6,7},{7,6},{8,9},{9,8},{10,11... | collective-permute-start | bytes 4718600 | tf_op jit(solution)/shard_map/ppermute | solution.py:440
  53.7 42.9 %copy-start.4 = (f32[64]{0:T(128)S(1)}, f32[64]{0:T(128)}, u32[]{:S(2)}) copy-start(f32[64]{0:T(128)} %param.11) | copy-start | bytes 772
